TPU v7x, 512 devices: a whole 4x4x16 slice. The times are simulated.
512 devices in a mesh: dp: 16 (over z), head: 8 (over x, core), srv: 4 (over y).
Axes of the slice: x: 4, y: 4, z: 16, core: 2. Of those that a mesh axis runs over, the one named last changes fastest.
Arguments:
- queries: bfloat16 [2048, 8, 1024], P('dp', 'srv', 'head'), may hold values from -5 to 5
- keys: bfloat16 [10240, 1024], P(('dp', 'head')), may hold values from -5 to 5
- values: bfloat16 [10240, 1024], P(('dp', 'head')), may hold values from -6 to 6
- output_gradient: bfloat16 [2048, 8, 1024], P('dp', 'srv', 'head'), may hold values from -6 to 6
- doc_ids: int32 [10240], P('dp'), may hold values from 0 to 7, never falling along the last dimension, each value on 1 to 5120 neighbouring positions
Outputs:
- attention: bfloat16 [2048, 8, 1024], P('dp', 'srv', 'head')
- q_grad: bfloat16 [2048, 8, 1024], P('dp', 'srv', 'head')
- k_grad: bfloat16 [10240, 1024], P(('dp', 'head', 'srv'))
- v_grad: bfloat16 [10240, 1024], P(('dp', 'head', 'srv'))
Inputs may be any that keep to these rules, and one draw needn't show every extreme that they name: `doc_ids`: document numbers never fall along the keys; every document holds at most 5120 keys, and one holds exactly 5120.
All inputs are finite; a program needn't handle non-finite values.
Results may differ from a plain program's by a relative error of at most 0.039.
Values may be sent and summed in bfloat16 or wider, within the bound.
No kernel may reach another device: no remote copies, remote signals or barrier semaphores. Data moves between devices by JAX's collectives and lax.ppermute only.
A program may use at most 64 MiB of HBM per device.

v0:
```python
import math

import jax
import jax.numpy as jnp
from jax import lax
from jax.sharding import PartitionSpec as P

HEAD_SIZE = 128


NEGATIVE = -1e30


def local(queries, keys, values, output_gradient, doc_ids):
    home_rows, pair_heads, group_width = queries.shape
    groups = group_width // HEAD_SIZE
    scale_factor = HEAD_SIZE ** (-0.5)
    key_rows, value_rows = (
        lax.all_to_all(keys, "head", split_axis=1, concat_axis=0, tiled=True),
        lax.all_to_all(values, "head", split_axis=1, concat_axis=0, tiled=True),
    )
    key_count = key_rows.shape[0]
    servers = lax.axis_size("dp")
    server = lax.axis_index("dp")
    key_at = server * key_count + jnp.arange(key_count, dtype=jnp.int32)
    all_docs = lax.all_gather(doc_ids, "dp", axis=0, tiled=True)
    query_total = home_rows * servers
    context = all_docs.shape[0] - query_total
    query_docs = all_docs[context:]
    query_places = context + jnp.arange(query_total, dtype=jnp.int32)
    all_q, all_dout = (
        lax.all_gather(queries, "dp", axis=0, tiled=True),
        lax.all_gather(output_gradient, "dp", axis=0, tiled=True),
    )
    block_rows = math.gcd(512, query_total)
    block_count = query_total // block_rows
    key_heads = key_rows.reshape(key_count, groups, HEAD_SIZE)
    value_heads = value_rows.reshape(key_count, groups, HEAD_SIZE)
    query_blocks = all_q.reshape(block_count, block_rows, pair_heads, groups, HEAD_SIZE)
    grad_blocks = all_dout.reshape(block_count, block_rows, pair_heads, groups, HEAD_SIZE)
    place_blocks = query_places.reshape(block_count, block_rows)
    doc_blocks = query_docs.reshape(block_count, block_rows)

    def admissible(places, query_doc):
        return (key_at[None, :] <= places[:, None]) & (doc_ids[None, :] == query_doc[:, None])

    def scores_of(query_block):
        return (
            jnp.einsum("pjgd,kgd->gjpk", query_block, key_heads, preferred_element_type=jnp.float32)
            * scale_factor
        )

    def block_max(inputs):
        query_block, places, query_doc = inputs
        allowed = admissible(places, query_doc)

        def compute():
            raw_scores = scores_of(query_block)
            masked = jnp.where(allowed[None, None], raw_scores, NEGATIVE)
            return (jnp.max(masked, axis=-1).transpose(2, 1, 0), raw_scores)

        return compute()

    def block_top(inputs):
        return block_max(inputs)[0]

    local_max = lax.map(block_top, (query_blocks, place_blocks, doc_blocks))
    row_max = lax.pmax(local_max.reshape(query_total, pair_heads, groups), "dp")
    max_blocks = row_max.reshape(block_count, block_rows, pair_heads, groups)

    def block_sum(inputs):
        stored, places, query_doc, row_top = inputs
        allowed = admissible(places, query_doc)

        def compute():
            block_scores = scores_of(stored)
            shifted = block_scores - row_top.transpose(2, 1, 0)[..., None]
            weights = jnp.where(allowed[None, None], jnp.exp(shifted), 0.0)
            weighted = jnp.einsum(
                "gjpk,kgd->pjgd",
                weights.astype(jnp.bfloat16),
                value_heads,
                preferred_element_type=jnp.float32,
            )
            return (
                weighted.reshape(block_rows, pair_heads, group_width),
                jnp.sum(weights, axis=-1).transpose(2, 1, 0),
            )

        return compute()

    part_out, part_norm = lax.map(block_sum, (query_blocks, place_blocks, doc_blocks, max_blocks))
    part_out = part_out.reshape(query_total, pair_heads, group_width)
    part_norm = part_norm.reshape(query_total, pair_heads, groups)
    home_out, home_norm = (
        lax.psum_scatter(part_out, "dp", scatter_dimension=0, tiled=True),
        lax.psum_scatter(part_norm, "dp", scatter_dimension=0, tiled=True),
    )
    home_max = lax.dynamic_slice_in_dim(row_max, server * home_rows, home_rows, 0)
    attn_home = (
        home_out.reshape(home_rows, pair_heads, groups, HEAD_SIZE) / home_norm[..., None]
    ).astype(jnp.bfloat16)
    log_home = home_max + jnp.log(home_norm)
    grad_home = output_gradient.reshape(home_rows, pair_heads, groups, HEAD_SIZE).astype(
        jnp.float32
    )
    delta_home = jnp.sum(grad_home * attn_home.astype(jnp.float32), axis=-1)
    log_all, delta_all = (
        lax.all_gather(log_home, "dp", axis=0, tiled=True),
        lax.all_gather(delta_home, "dp", axis=0, tiled=True),
    )
    attention = attn_home.reshape(home_rows, pair_heads, group_width)
    log_blocks = log_all.reshape(block_count, block_rows, pair_heads, groups)
    delta_blocks = delta_all.reshape(block_count, block_rows, pair_heads, groups)

    def block_grad(totals, inputs):
        query_block, grad_block, places, query_doc, log_norm, row_delta = inputs
        allowed = admissible(places, query_doc)

        def compute():
            shifted = scores_of(query_block) - log_norm.transpose(2, 1, 0)[..., None]
            probs = jnp.where(allowed[None, None], jnp.exp(shifted), 0.0)
            value_grad = jnp.einsum(
                "gjpk,pjgd->kgd",
                probs.astype(jnp.bfloat16),
                grad_block,
                preferred_element_type=jnp.float32,
            )
            weight_grad = jnp.einsum(
                "pjgd,kgd->gjpk", grad_block, value_heads, preferred_element_type=jnp.float32
            )
            score_grad = (probs * (weight_grad - row_delta.transpose(2, 1, 0)[..., None])).astype(
                jnp.bfloat16
            )
            query_grad = (
                jnp.einsum(
                    "gjpk,kgd->pjgd", score_grad, key_heads, preferred_element_type=jnp.float32
                )
                * scale_factor
            )
            key_grad = (
                jnp.einsum(
                    "gjpk,pjgd->kgd", score_grad, query_block, preferred_element_type=jnp.float32
                )
                * scale_factor
            )
            return (query_grad.reshape(block_rows, pair_heads, group_width), key_grad, value_grad)

        query_grad, key_grad, value_grad = compute()
        return ((totals[0] + key_grad, totals[1] + value_grad), query_grad)

    zero_start = jnp.zeros((key_count, groups, HEAD_SIZE), jnp.float32)
    grad_inputs = (query_blocks, grad_blocks, place_blocks, doc_blocks, log_blocks, delta_blocks)
    (key_total, value_total), query_parts = lax.scan(
        block_grad, (zero_start, zero_start), grad_inputs
    )
    q_summed = lax.psum_scatter(
        query_parts.reshape(query_total, pair_heads, group_width).astype(jnp.bfloat16),
        "dp",
        scatter_dimension=0,
        tiled=True,
    )
    spread_key, spread_value = (
        lax.all_to_all(
            key_total.reshape(key_count, group_width).astype(jnp.bfloat16),
            "head",
            split_axis=0,
            concat_axis=1,
            tiled=True,
        ).astype(jnp.float32),
        lax.all_to_all(
            value_total.reshape(key_count, group_width).astype(jnp.bfloat16),
            "head",
            split_axis=0,
            concat_axis=1,
            tiled=True,
        ).astype(jnp.float32),
    )
    k_summed, v_summed = (
        lax.psum_scatter(
            spread_key.astype(jnp.bfloat16), "srv", scatter_dimension=0, tiled=True
        ).astype(jnp.float32),
        lax.psum_scatter(
            spread_value.astype(jnp.bfloat16), "srv", scatter_dimension=0, tiled=True
        ).astype(jnp.float32),
    )
    return (attention, q_summed, k_summed.astype(jnp.bfloat16), v_summed.astype(jnp.bfloat16))


def solution(mesh):
    placed = (
        P("dp", "srv", "head"),
        P(("dp", "head"), None),
        P(("dp", "head"), None),
        P("dp", "srv", "head"),
        P("dp"),
    )
    return jax.shard_map(
        local,
        mesh=mesh,
        in_specs=placed,
        out_specs=(
            P("dp", "srv", "head"),
            P("dp", "srv", "head"),
            P(("dp", "head", "srv"), None),
            P(("dp", "head", "srv"), None),
        ),
        check_vma=False,
    )
```

profile of v0, /device:TPU:1, one launch (start us, length us, event | category | flops | bytes accessed | tf_op | source)
XLA Modules:
  0.0 642.2 jit_solution(6897663471784736279)
XLA Ops:
  9.5 10.2 %all-to-all-start = ((bf16[80,8,128]{2,0,1:T(8,128)(2,1)}), bf16[80,8,128]{2,0,1:T(8,128)(2,1)S(1)}, u32[]{:S(2)}, u32[]{:S(2)}) async-start(bf16[80,8,128]{2,0,1:T(8,128)(2,1)} %copy_bitcast_fusion.3), calls=%async_computation | async-start | bytes 327680 | tf_op jit(solution)/shard_map/all_to_all | solution.py:19
  21.9 24.0 %all-gather.1 = s32[16,1,640]{2,1,0:T(1,128)S(1)} all-gather(s32[1,1,640]{2,1,0:T(1,128)S(1)} %reshape.364), channel_id=1, replica_groups=mesh['dp'=16,'head'=8,'srv'=4] {'dp'}, dimensions={0}, use_global_device_ids=true | all-gather | bytes 43520 | tf_op jit(solution)/shard_map/all_gather | solution.py:26
  46.6 31.1 %all-gather.5.cloned.1.call-done = bf16[2048,2,128]{2,0,1:T(8,128)(2,1)} async-done(((bf16[128,2,128]{2,0,1:T(8,128)(2,1)}), bf16[2048,2,128]{2,0,1:T(8,128)(2,1)}) %all-gather.5.cloned.1.call-update) | async-done | bytes 1048592 | tf_op jit(solution)/shard_map/all_gather | solution.py:32
  78.9 14.4 %all-to-all-start.1 = ((bf16[80,8,128]{2,0,1:T(8,128)(2,1)}), bf16[80,8,128]{2,0,1:T(8,128)(2,1)}, u32[]{:S(2)}, u32[]{:S(2)}) async-start(bf16[80,8,128]{2,0,1:T(8,128)(2,1)} %copy_bitcast_fusion.2), calls=%async_computation.1 | async-start | bytes 327680 | tf_op jit(solution)/shard_map/all_to_all | solution.py:20
  93.4 7.6 %while.39 = (s32[]{:T(128)}, f32[4,512,2,1]{1,0,2,3:T(4,128)S(1)}, s32[4,512]{1,0:T(4,128)}, s32[640]{0:T(1024)S(1)}, s32[4,512]{1,0:T(4,128)S(1)}, /*index=5*/b...) while((s32[]{:T(128)}, f32[4,512,2,1]{1,0,2,3:T(4,128)S(1)}, ...), condition=%wide.region_2.3_spmd.clone, body=%wide.region_0.2_spmd.clone.sunk | while | flops 170720896 | bytes 1121917 | solution.py:67
  101.0 41.1 %pmax.7 = f32[2048,2,1]{0,1,2:T(2,128)} all-reduce(f32[2048,2,1]{0,1,2:T(2,128)S(1)} %reshape.354), channel_id=1, replica_groups=mesh['dp'=16,'head'=8,'srv'=4] {'dp'}, use_global_device_ids=true, to_apply=%region_3.4 | all-reduce | flops 4096 | bytes 32768 | tf_op jit(solution)/shard_map/pmax | solution.py:68
  142.1 22.3 %while.40 = (s32[]{:T(128)}, f32[4,512,2,128]{3,2,1,0:T(2,128)S(1)}, f32[4,512,2,1]{1,3,2,0:T(1,128)}, s32[4,512]{1,0:T(4,128)}, s32[640]{0:T(1024)S(1)}, /*inde...) while((s32[]{:T(128)}, ...), condition=%wide.region_6.7_spmd.clone, body=%wide.region_4.6_spmd.clone.sunk | while | flops 341769856 | bytes 8437397 | solution.py:92
  170.0 67.5 %reduce-scatter.8.cloned.1.call-done = f32[128,2]{1,0:T(8,128)} async-done(((f32[2048,2]{1,0:T(8,128)}), f32[128,2]{1,0:T(8,128)}) %reduce-scatter.8.cloned.1.call-update) | async-done | bytes 1040
  239.3 20.3 %all_gather.17 = f32[2048,2,1]{0,1,2:T(2,128)S(1)} all-gather(f32[128,2,1]{0,1,2:T(2,128)S(1)} %log_add_fusion), channel_id=1, replica_groups=mesh['dp'=16,'head'=8,'srv'=4] {'dp'}, dimensions={0}, use_global_device_ids=true | all-gather | bytes 17408 | tf_op jit(solution)/shard_map/all_gather | solution.py:109
  259.5 123.3 %all-reduce.10.cloned.1.call-done = f32[2048,2,128]{2,1,0:T(2,128)} async-done(((f32[2048,2,128]{2,1,0:T(2,128)}), f32[2048,2,128]{2,1,0:T(2,128)}) %all-reduce.10.cloned.1.call-update) | async-done | bytes 2097168
  384.6 29.0 %all-gather = f32[2048,2]{1,0:T(8,128)S(1)} all-gather(f32[128,2]{1,0:T(8,128)S(1)} %get-tuple-element.445), channel_id=2, replica_groups=mesh['dp'=16,'head'=8,'srv'=4] {'dp'}, dimensions={0}, use_global_device_ids=true | all-gather | bytes 17408 | tf_op jit(solution)/shard_map/all_gather | solution.py:110
  414.0 38.2 %all-gather.7.cloned.1.call-done = bf16[2048,2,128]{2,0,1:T(8,128)(2,1)} async-done(((bf16[128,2,128]{2,0,1:T(8,128)(2,1)}), bf16[2048,2,128]{2,0,1:T(8,128)(2,1)}) %all-gather.7.cloned.1.call-update) | async-done | bytes 1048592 | tf_op jit(solution)/shard_map/all_gather | solution.py:33
  452.1 37.4 %while.41 = (s32[]{:T(128)}, f32[640,1,128]{0,2,1:T(8,128)S(1)}, f32[640,1,128]{0,2,1:T(8,128)}, bf16[4,512,2,128]{3,1,2,0:T(8,128)(2,1)}, bf16[4,512,2,1,128]{4...) while((s32[]{:T(128)}, f32[640,1,128]{0,2,1:T(8,128)S(1)}, ...), condition=%wide.region_11.12_spmd.clone, body=%wide.region_10.11_spmd.clone.sunk | while | flops 846938752 | bytes 35077916 | solution.py:154
  456.3 3.6 fusion.122
  465.7 3.6 fusion.122
  475.0 3.6 fusion.122
  484.4 3.6 fusion.122
  490.3 14.5 %all-to-all-start.2 = ((bf16[8,80,128]{2,1,0:T(8,128)(2,1)}), bf16[8,80,128]{2,1,0:T(8,128)(2,1)S(1)}, u32[]{:S(2)}, u32[]{:S(2)}) async-start(bf16[8,80,128]{2,1,0:T(8,128)(2,1)} %bitcast.15), calls=%async_computation.2 | async-start | bytes 327680 | tf_op jit(solution)/shard_map/all_to_all | solution.py:164
  504.9 3.3 copy.77
  510.5 4.2 all-to-all-start.3
  514.7 5.6 all-to-all-done.3
  520.3 10.6 %fusion.72 = (bf16[24,1024]{1,0:T(8,128)(2,1)S(1)}, bf16[24,1024]{1,0:T(8,128)(2,1)S(1)}) fusion(bf16[80,1024]{1,0:T(8,128)(2,1)S(1)} %copy_bitcast_fusion.1, bf16[80,1024]{1,0:T(8,128)(2,1)S(1)} %copy_bitcast_fusion), kind=kCustom, calls=%all-reduce-scatter.2 | all-reduce-scatter fusion | flops 196609 | bytes 428032
  532.7 3.0 collective-permute-start.1
  539.4 94.8 %all-reduce.12.cloned.1.call-done = bf16[2048,2,128]{2,1,0:T(2,128)(2,1)} async-done(((bf16[2048,2,128]{2,1,0:T(2,128)(2,1)}), bf16[2048,2,128]{2,1,0:T(2,128)(2,1)}) %all-reduce.12.cloned.1.call-update) | async-done | bytes 1048592
  (173 shorter events, 76.9 us)
Async XLA Ops:
  7.2 1.6 copy-start
  7.2 86.2 %copy-start.3 = (s32[640]{0:T(1024)S(1)}, s32[640]{0:T(1024)}, u32[]{:S(2)}) copy-start(s32[640]{0:T(1024)} %param.15) | copy-start | bytes 7684
  7.2 70.4 %all-gather.5.cloned.1.call-start = ((), (), s32[]{:S(2)}) async-start(), calls=%async_computation.5 | async-start | bytes 1114112 | tf_op jit(solution)/shard_map/all_gather | solution.py:32
  9.5 69.5 %all-to-all-start = ((bf16[80,8,128]{2,0,1:T(8,128)(2,1)}), bf16[80,8,128]{2,0,1:T(8,128)(2,1)S(1)}, u32[]{:S(2)}, u32[]{:S(2)}) async-start(bf16[80,8,128]{2,0,1:T(8,128)(2,1)} %copy_bitcast_fusion.3), calls=%async_computation | async-start | bytes 327680 | tf_op jit(solution)/shard_map/all_to_all | solution.py:19
  78.9 63.2 %all-to-all-start.1 = ((bf16[80,8,128]{2,0,1:T(8,128)(2,1)}), bf16[80,8,128]{2,0,1:T(8,128)(2,1)}, u32[]{:S(2)}, u32[]{:S(2)}) async-start(bf16[80,8,128]{2,0,1:T(8,128)(2,1)} %copy_bitcast_fusion.2), calls=%async_computation.1 | async-start | bytes 327680 | tf_op jit(solution)/shard_map/all_to_all | solution.py:20
  93.4 144.2 %reduce-scatter.8.cloned.1.call-start = ((), (), s32[]{:S(2)}) async-start(), calls=%async_computation.7 | async-start | bytes 1114112
  164.4 2.2 copy-start.2
  164.4 2.9 copy-start.7
  166.6 216.3 %all-reduce.10.cloned.1.call-start = ((), (), s32[]{:S(2)}) async-start(), calls=%async_computation.8 | async-start | bytes 4194304
  167.3 284.8 %all-gather.7.cloned.1.call-start = ((), (), s32[]{:S(2)}) async-start(), calls=%async_computation.6 | async-start | bytes 1114112 | tf_op jit(solution)/shard_map/all_gather | solution.py:33
  452.6 3.2 copy-start.1
  456.3 3.6 copy-start.4
  462.0 3.2 copy-start.1
  465.7 3.6 copy-start.4
  471.3 3.2 copy-start.1
  475.0 3.6 copy-start.4
  480.7 3.2 copy-start.1
  484.4 3.6 copy-start.4
  489.5 18.7 %copy-start.6 = (f32[640,1,128]{0,2,1:T(8,128)S(1)}, f32[640,1,128]{0,2,1:T(8,128)}, u32[]{:S(2)}) copy-start(f32[640,1,128]{0,2,1:T(8,128)} %get-tuple-element.183) | copy-start | bytes 983044
  490.3 20.1 %all-to-all-start.2 = ((bf16[8,80,128]{2,1,0:T(8,128)(2,1)}), bf16[8,80,128]{2,1,0:T(8,128)(2,1)S(1)}, u32[]{:S(2)}, u32[]{:S(2)}) async-start(bf16[8,80,128]{2,1,0:T(8,128)(2,1)} %bitcast.15), calls=%async_computation.2 | async-start | bytes 327680 | tf_op jit(solution)/shard_map/all_to_all | solution.py:164
  504.9 129.3 %all-reduce.12.cloned.1.call-start = ((), (), s32[]{:S(2)}) async-start(), calls=%async_computation.9 | async-start | bytes 2097152
  510.5 9.8 %all-to-all-start.3 = ((bf16[8,80,128]{2,1,0:T(8,128)(2,1)}), bf16[8,80,128]{2,1,0:T(8,128)(2,1)S(1)}, u32[]{:S(2)}, u32[]{:S(2)}) async-start(bf16[8,80,128]{2,1,0:T(8,128)(2,1)} %bitcast.17), calls=%async_computation.3 | async-start | bytes 327680 | tf_op jit(solution)/shard_map/all_to_all | solution.py:171
  530.9 6.8 %collective-permute-start = (bf16[12,1024]{1,0:T(8,128)(2,1)S(1)}, bf16[12,1024]{1,0:T(8,128)(2,1)S(1)}, u32[]{:S(2)}, u32[]{:S(2)}) collective-permute-start(bf16[12,1024]{1,0:T(8,128)(2,1)S(1)} %slice.16), channel_id=1, source_target_pairs={{0,1},{1,2},{2,3},{4,5},{5,6},{6,7},{8,9},{9,10},{10,11},{12,13},{... | collective-permute-start | bytes 73736
  532.7 5.2 collective-permute-start.1
  (4 other events, 4.0 us)
Sparse Core Ops, SparseCore 0:
  10.7 66.8 all-gather.4
  166.7 70.7 reduce-scatter.7
  240.0 142.8 all-reduce.9
  385.6 66.4 all-gather.6
  508.3 125.8 all-reduce.11
where the time goes:
time: 653 us; the launch traced here: 642 us
  waiting for transfers between devices  363 us (56%)
  blocking collectives  125 us (19%)
  starting transfers between devices  48.3 us (7%)
  matrix products  42.8 us (7%)
  local copies, waits for them, and re-layouts  40.5 us (6%)
  between operations  15.3 us (2%)
  other arithmetic  7 us (1%)
    unnamed x10, waiting for transfers between devices  286 us
    pmax x1, blocking collectives, local(): row_max = lax.pmax(local_max.reshape(query_total, pair_heads, groups), 'dp')  41.1 us
    all_gather x1, waiting for transfers between devices, local(): lax.all_gather(output_gradient, 'dp', axis=0, tiled=True)  38.2 us
    all_gather x1, waiting for transfers between devices, local(): lax.all_gather(queries, 'dp', axis=0, tiled=True)  31.1 us
    all_gather x1, blocking collectives, local(): lax.all_gather(delta_home, 'dp', axis=0, tiled=True)  29 us
    all_gather x1, blocking collectives, local(): all_docs = lax.all_gather(doc_ids, 'dp', axis=0, tiled=True)  24 us
    all_gather x1, blocking collectives, local(): lax.all_gather(log_home, 'dp', axis=0, tiled=True)  20.3 us
    all_to_all x1, starting transfers between devices, local(): lax.all_to_all(key_total.reshape(key_count, group_width).astype(jnp.bfloa...  14.5 us
  transfers between devices with their start and end apart: 11, of which 7 were waited for; matrix products, arithmetic and copies ran while one was open for 6% of the time, Pallas kernels for 0%

commit v1 on v0

v1 whole, which is shorter than its diff:
```python
import functools

import jax
import jax.numpy as jnp
from jax import lax
from jax.experimental import pallas as pl
from jax.experimental.pallas import tpu as pltpu
from jax.sharding import PartitionSpec as P

HEAD = 128
DP = 16
QUAD = 4
WINDOW = 10
PAIRS = WINDOW // 2
DOCS = 8
SCALE = HEAD**-0.5
EXP2_SCALE = SCALE * 1.4426950408889634
NEGATIVE = -1e30
QUADS = tuple(tuple(range(QUAD * q, QUAD * q + QUAD)) for q in range(DP // QUAD))

F32 = jnp.float32
BF16 = jnp.bfloat16
NT = (((1,), (1,)), ((), ()))
NN = (((1,), (0,)), ((), ()))
TN = (((0,), (0,)), ((), ()))


def dot(lhs, rhs, dims):
    return lax.dot_general(lhs, rhs, dims, preferred_element_type=F32)


def place_pattern(rows):
    at = lax.broadcasted_iota(jnp.int32, (rows, 128), 0)
    srv, rest = at // 80, at % 80
    shard, rest = rest // 40, rest % 40
    return 640 * shard + 80 * (rest // 20) + 20 * srv + rest % 20


def fold8(block, op):
    rows, cols = block.shape
    return op(block.reshape(rows // 8, 8, cols), axis=0)


def forward_kernel(info, starts, qg, kv, e_ref, o_ref, stats_ref, s_ref, m_ref, l_ref):
    first, last, place, query_at = info[0], info[1], info[2], info[3]
    tiles, cols, _ = qg.shape
    keys = kv.shape[0] * kv.shape[2]
    pattern = place + place_pattern(keys)
    pattern = jnp.concatenate([pattern] * (cols // 128), axis=1)
    lane = lax.broadcasted_iota(jnp.int32, (1, cols), 1)
    m_ref[...] = jnp.full(m_ref.shape, NEGATIVE, F32)
    l_ref[...] = jnp.zeros(l_ref.shape, F32)
    o_ref[...] = jnp.zeros(o_ref.shape, F32)
    query_places, doc_starts = [], []
    for tile in range(tiles):
        query_place = query_at + (cols // 2) * tile + lane // 2
        doc_start = jnp.zeros_like(query_place)
        for doc in range(DOCS):
            doc_start = jnp.where(
                starts[doc] <= query_place, jnp.maximum(doc_start, starts[doc]), doc_start
            )
        query_places.append(query_place)
        doc_starts.append(doc_start)

    def scores(t, carry):
        k = kv[:, t, :, :HEAD].reshape(keys, HEAD)
        key_place = pattern + 1280 * t
        for tile in range(tiles):
            span = pl.ds(tile * cols, cols)
            s = dot(k, qg[tile, :, :HEAD], NT)
            allowed = (key_place >= doc_starts[tile]) & (key_place <= query_places[tile])
            s = jnp.where(allowed, s, NEGATIVE)
            s_ref[t, :, span] = s
            m_ref[tile] = jnp.maximum(m_ref[tile], fold8(s, jnp.max))
        return carry

    lax.fori_loop(first, last, scores, 0)
    tops = [jnp.max(m_ref[tile], axis=0, keepdims=True) for tile in range(tiles)]

    def weigh(t, carry):
        v = kv[:, t, :, HEAD:].reshape(keys, HEAD)
        for tile in range(tiles):
            span = pl.ds(tile * cols, cols)
            e = jnp.exp2((s_ref[t, :, span] - tops[tile]) * EXP2_SCALE)
            l_ref[tile] += fold8(e, jnp.sum)
            e = e.astype(BF16)
            e_ref[t, :, span] = e
            o_ref[tile] += dot(v, e, TN)
        return carry

    lax.fori_loop(first, last, weigh, 0)
    stats_ref[...] = jnp.zeros(stats_ref.shape, F32)
    for tile in range(tiles):
        gradient = qg[tile, :, HEAD:].astype(F32).T
        stats_ref[tile : tile + 1, :] = tops[tile]
        stats_ref[tiles + tile : tiles + tile + 1, :] = jnp.sum(
            l_ref[tile], axis=0, keepdims=True
        )
        stats_ref[2 * tiles + tile : 2 * tiles + tile + 1, :] = jnp.sum(
            gradient * o_ref[tile], axis=0, keepdims=True
        )


def backward_kernel(info, qg, kv, e_ref, o_ref, own, stats, oq_ref, dkv_ref, dq_ref):
    first, last = info[0], info[1]
    tiles, cols, _ = qg.shape
    keys = kv.shape[0] * kv.shape[2]
    dkv_ref[...] = jnp.zeros(dkv_ref.shape, BF16)
    dq_ref[...] = jnp.zeros(dq_ref.shape, F32)
    shares, deltas = [], []
    for tile in range(tiles):
        row = lambda ref, kind: ref[kind * tiles + tile : kind * tiles + tile + 1, :]
        parts = [stats.at[part] for part in range(stats.shape[0])]
        top = functools.reduce(jnp.maximum, [row(p, 0) for p in parts])
        weights = [jnp.exp2((row(p, 0) - top) * EXP2_SCALE) for p in parts]
        norm = sum(w * row(p, 1) for w, p in zip(weights, parts))
        deltas.append(sum(w * row(p, 2) for w, p in zip(weights, parts)) / norm)
        shares.append(jnp.exp2((row(own, 0) - top) * EXP2_SCALE) / norm)

    def grads(t, carry):
        k = kv[:, t, :, :HEAD].reshape(keys, HEAD)
        v = kv[:, t, :, HEAD:].reshape(keys, HEAD)
        dk = jnp.zeros((keys, HEAD), F32)
        dv = jnp.zeros((keys, HEAD), F32)
        for tile in range(tiles):
            q, gradient = qg[tile, :, :HEAD], qg[tile, :, HEAD:]
            p = e_ref[t, :, pl.ds(tile * cols, cols)].astype(F32) * shares[tile]
            ds = (p * (dot(v, gradient, NT) - deltas[tile])).astype(BF16)
            dv += dot(p.astype(BF16), gradient, NN)
            dk += dot(ds, q, NN)
            dq_ref[tile] += dot(k, ds, TN)
        dk = (dk * SCALE).astype(BF16).reshape(kv.shape[0], kv.shape[2], HEAD)
        dv = dv.astype(BF16).reshape(kv.shape[0], kv.shape[2], HEAD)
        dkv_ref[:, t, :, :HEAD] = dk
        dkv_ref[:, t, :, HEAD:] = dv
        return carry

    lax.fori_loop(first, last, grads, 0)
    for tile in range(tiles):
        oq_ref[tile, :, :HEAD] = (o_ref[tile] * shares[tile]).T.astype(BF16)
        oq_ref[tile, :, HEAD:] = (dq_ref[tile] * SCALE).T.astype(BF16)


def exchange(block, axis, groups=None):
    return lax.all_to_all(block, axis, 0, 0, tiled=True, axis_index_groups=groups)


def spread(block, count):
    return jnp.broadcast_to(block[None], (count, *block.shape))


def local(queries, keys, values, output_gradient, doc_ids):
    rows = queries.shape[0] * queries.shape[1]
    dp, srv = lax.axis_index("dp"), lax.axis_index("srv")
    quad, member = dp // QUAD, dp % QUAD
    heads, srvs = 8, 4
    shard_rows = keys.shape[0] // srvs
    vmem = pl.BlockSpec(memory_space=pltpu.VMEM)
    smem = pl.BlockSpec(memory_space=pltpu.SMEM)

    mine = lambda x: lax.dynamic_slice_in_dim(x, srv * shard_rows, shard_rows, 0).reshape(
        shard_rows, heads, HEAD
    )
    kv = jnp.concatenate([mine(keys), mine(values)], axis=2).transpose(1, 0, 2)
    kv = exchange(kv, "head")
    kv = kv.reshape(QUAD, heads // QUAD * shard_rows, 2 * HEAD)
    count = jnp.sum(
        (doc_ids[:, None] == jnp.arange(DOCS, dtype=jnp.int32)[None, :]).astype(jnp.int32), axis=0
    )
    count = jnp.concatenate([count // 128, count % 128]).astype(BF16)
    extra = jnp.zeros((QUAD, 8, 2 * HEAD), BF16).at[:, 0, : 2 * DOCS].set(count[None])
    piece = kv.shape[1]
    kv = spread(jnp.concatenate([kv, extra], axis=1), DP // QUAD)
    kv = exchange(kv.reshape(DP, piece + 8, 2 * HEAD), "dp")
    count = jnp.sum(kv[:, piece, : 2 * DOCS].astype(F32), axis=0).astype(jnp.int32)
    count = count[:DOCS] * 128 + count[DOCS:]
    doc = jnp.arange(DOCS, dtype=jnp.int32)
    starts = jnp.sum(jnp.where(doc[None, :] < doc[:, None], count[None, :], 0), axis=1)
    window = jnp.minimum(4 + quad, DP - WINDOW)
    kv = lax.dynamic_slice(kv, (window, 0, 0), (WINDOW, piece, 2 * HEAD))
    kv = exchange(spread(kv, srvs), "srv", None)
    kv = kv.reshape(srvs, PAIRS, 2 * piece, 2 * HEAD)

    qg = jnp.concatenate(
        [queries.reshape(rows, HEAD), output_gradient.reshape(rows, HEAD)], axis=1
    )
    qg = exchange(spread(qg, QUAD), "dp", QUADS)
    qg = qg.reshape(QUAD, rows, 2 * HEAD)

    query_at = 8192 + 512 * quad
    doc_start = jnp.max(jnp.where(starts <= query_at, starts, 0))
    first = jnp.maximum(doc_start // 640 - window, 0) // 2
    last = jnp.minimum(((query_at + 511) // 640 - window) // 2 + 1, PAIRS)
    info = jnp.stack([first, last, 640 * window + 160 * member, query_at]).astype(jnp.int32)

    key_block = srvs * 2 * piece
    params = pltpu.CompilerParams(vmem_limit_bytes=40 * 1024 * 1024)
    e, o, stats = pl.pallas_call(
        forward_kernel,
        out_shape=(
            jax.ShapeDtypeStruct((PAIRS, key_block, QUAD * rows), BF16),
            jax.ShapeDtypeStruct((QUAD, HEAD, rows), F32),
            jax.ShapeDtypeStruct((16, rows), F32),
        ),
        in_specs=[smem, smem, vmem, vmem],
        out_specs=(vmem, vmem, vmem),
        scratch_shapes=[
            pltpu.VMEM((PAIRS, key_block, QUAD * rows), F32),
            pltpu.VMEM((QUAD, 8, rows), F32),
            pltpu.VMEM((QUAD, 8, rows), F32),
        ],
        compiler_params=params,
        name="forward",
    )(info, starts, qg, kv)
    all_stats = exchange(spread(stats, QUAD).reshape(QUAD * 16, rows), "dp", QUADS)
    all_stats = all_stats.reshape(QUAD, 16, rows)
    oq, dkv = pl.pallas_call(
        backward_kernel,
        out_shape=(
            jax.ShapeDtypeStruct((QUAD, rows, 2 * HEAD), BF16),
            jax.ShapeDtypeStruct(kv.shape, BF16),
        ),
        in_specs=[smem, vmem, vmem, vmem, vmem, vmem, vmem],
        out_specs=(vmem, vmem),
        scratch_shapes=[pltpu.VMEM((QUAD, HEAD, rows), F32)],
        compiler_params=params,
        name="backward",
    )(info, qg, kv, e, o, stats, all_stats)

    total = lambda x: jnp.sum(x.astype(F32), axis=0).astype(BF16)
    dkv = exchange(dkv.reshape(srvs, WINDOW, piece, 2 * HEAD), "srv")
    dkv = lax.dynamic_update_slice(
        jnp.zeros((DP, piece, 2 * HEAD), BF16), total(dkv), (window, 0, 0)
    )
    dkv = exchange(dkv, "dp")
    dkv = total(dkv.reshape(DP // QUAD, QUAD, piece, 2 * HEAD))
    dkv = exchange(dkv.reshape(heads, shard_rows, 2 * HEAD), "head")
    dkv = dkv.transpose(1, 0, 2)
    k_grad = dkv[:, :, :HEAD].reshape(shard_rows, heads * HEAD)
    v_grad = dkv[:, :, HEAD:].reshape(shard_rows, heads * HEAD)

    oq = total(exchange(oq, "dp", QUADS))
    attention = oq[:, :HEAD].reshape(queries.shape)
    q_grad = oq[:, HEAD:].reshape(queries.shape)
    return attention, q_grad, k_grad, v_grad


def solution(mesh):
    placed = (
        P("dp", "srv", "head"),
        P(("dp", "head"), None),
        P(("dp", "head"), None),
        P("dp", "srv", "head"),
        P("dp"),
    )
    return jax.shard_map(
        local,
        mesh=mesh,
        in_specs=placed,
        out_specs=(
            P("dp", "srv", "head"),
            P("dp", "srv", "head"),
            P(("dp", "head", "srv"), None),
            P(("dp", "head", "srv"), None),
        ),
        check_vma=False,
    )
```

time: 653 us -> 170 us (0.26); the launches traced: 642 us -> 169 us
  waiting for transfers between devices: 363 us -> 66.8 us
  blocking collectives: 125 us -> 17.8 us
  matrix products: 42.8 us -> 0 us
  local copies, waits for them, and re-layouts: 40.5 us -> 8.19 us
  starting transfers between devices: 48.3 us -> 61.1 us
  between operations: 15.3 us -> 2.77 us
  Pallas kernels: 0 us -> 8.92 us
    unnamed x10 -> x0, waiting for transfers between devices: 286 us -> none
    all_gather x3 -> x0, blocking collectives: 73.3 us -> none  [the longest x1 29 us: local(): lax.all_gather(delta_home, 'dp', axis=0, tiled=True)]
    all_gather x2 -> x0, waiting for transfers between devices: 69.2 us -> none  [the longest x1 38.2 us: local(): lax.all_gather(output_gradient, 'dp', axis=0, tiled=True)]
    all_to_all x4 -> x7, waiting for transfers between devices: 7.06 us -> 66.8 us  [exchange(): lax.all_to_all(block, axis, 0, 0, tiled=True, axis_index_groups=groups)]
    dot_general x32 -> x0, matrix products: 42.8 us -> none  [the longest x4 14.3 us: compute(): jnp.einsum('gjpk,pjgd->kgd', probs.astype(jnp.bfloat16), grad_block, pref...]
    pmax x1 -> x0, blocking collectives: 41.1 us -> none  [local(): row_max = lax.pmax(local_max.reshape(query_total, pair_heads, groups), 'dp')]
    all_to_all x0 -> x2, blocking collectives: none -> 17.8 us  [exchange(): lax.all_to_all(block, axis, 0, 0, tiled=True, axis_index_groups=groups)]
    all_to_all x4 -> x7, starting transfers between devices: 43.3 us -> 61.1 us  [exchange(): lax.all_to_all(block, axis, 0, 0, tiled=True, axis_index_groups=groups)]
  transfers between devices with their start and end apart: 11 -> 7, of which waited for: 7 -> 7; matrix products, arithmetic and copies ran while one was open for 6% -> 3% of each run, Pallas kernels for 0% -> 0%
where the time goes in v1:
time: 170 us; the launch traced here: 169 us
  waiting for transfers between devices  66.8 us (39%)
  starting transfers between devices  61.1 us (36%)
  blocking collectives  17.8 us (10%)
  Pallas kernels  8.92 us (5%)
  local copies, waits for them, and re-layouts  8.19 us (5%)
  other arithmetic  3.03 us (2%)
  between operations  2.77 us (2%)
    all_to_all x7, waiting for transfers between devices, exchange(): lax.all_to_all(block, axis, 0, 0, tiled=True, axis_index_groups=groups)  66.8 us
    all_to_all x7, starting transfers between devices, exchange(): lax.all_to_all(block, axis, 0, 0, tiled=True, axis_index_groups=groups)  61.1 us
    all_to_all x2, blocking collectives, exchange(): lax.all_to_all(block, axis, 0, 0, tiled=True, axis_index_groups=groups)  17.8 us
    pallas_call x1, Pallas kernels, local(): pl.pallas_call(backward_kernel, out_shape=(jax.ShapeDtypeStruct((QUAD, ro...  5.26 us
    pallas_call x1, Pallas kernels, local(): pl.pallas_call(forward_kernel, out_shape=(jax.ShapeDtypeStruct((PAIRS, ke...  3.66 us
  transfers between devices with their start and end apart: 7, of which 7 were waited for; matrix products, arithmetic and copies ran while one was open for 3% of the time, Pallas kernels for 0%

profile of v1, /device:TPU:1, one launch (start us, length us, event | category | flops | bytes accessed | tf_op | source)
XLA Modules:
  0.0 168.7 jit_solution(3340785424308987012)
XLA Ops:
  0.6 0.9 constant_dynamic-slice_fusion.1
  2.3 10.1 %all-to-all-start = ((bf16[8,20,256]{2,1,0:T(8,128)(2,1)}), bf16[8,20,256]{2,1,0:T(8,128)(2,1)S(1)}, u32[]{:S(2)}, u32[]{:S(2)}) async-start(bf16[8,20,256]{2,1,0:T(8,128)(2,1)} %copy.15), calls=%async_computation | async-start | bytes 196608 | tf_op jit(solution)/shard_map/all_to_all | solution.py:145
  12.4 0.8 convert_reduce_fusion
  13.3 4.1 %all-to-all-done = bf16[8,20,256]{2,1,0:T(8,128)(2,1)S(1)} async-done(((bf16[8,20,256]{2,1,0:T(8,128)(2,1)}), bf16[8,20,256]{2,1,0:T(8,128)(2,1)S(1)}, u32[]{:S(2)}, u32[]{:S(2)}) %all-to-all-start) | async-done | bytes 81952 | tf_op jit(solution)/shard_map/all_to_all | solution.py:145
  17.5 0.8 broadcast_in_dim.23
  18.2 10.6 %all-to-all-start.1 = ((bf16[16,48,256]{2,1,0:T(8,128)(2,1)}), bf16[16,48,256]{2,1,0:T(8,128)(2,1)S(1)}, u32[]{:S(2)}, u32[]{:S(2)}) async-start(bf16[16,48,256]{2,1,0:T(8,128)(2,1)} %bitcast.3), calls=%async_computation.1 | async-start | bytes 786432 | tf_op jit(solution)/shard_map/all_to_all | solution.py:145
  28.8 0.9 pad_maximum_fusion
  29.7 17.1 %all-to-all-done.1 = bf16[16,48,256]{2,1,0:T(8,128)(2,1)S(1)} async-done(((bf16[16,48,256]{2,1,0:T(8,128)(2,1)}), bf16[16,48,256]{2,1,0:T(8,128)(2,1)S(1)}, u32[]{:S(2)}, u32[]{:S(2)}) %all-to-all-start.1) | async-done | bytes 393248 | tf_op jit(solution)/shard_map/all_to_all | solution.py:145
  46.8 0.8 broadcast_in_dim.26
  47.6 8.1 %all-to-all-start.2 = ((bf16[4,256,256]{2,1,0:T(8,128)(2,1)}), bf16[4,256,256]{2,1,0:T(8,128)(2,1)S(1)}, u32[]{:S(2)}, u32[]{:S(2)}) async-start(bf16[4,256,256]{2,1,0:T(8,128)(2,1)} %broadcast_in_dim.26), calls=%async_computation.2 | async-start | bytes 1048576 | tf_op jit(solution)/shard_map/all_to_all | solution.py:145
  55.8 13.3 %all-to-all-done.2.qg = bf16[4,256,256]{2,1,0:T(8,128)(2,1)S(1)} async-done(((bf16[4,256,256]{2,1,0:T(8,128)(2,1)}), bf16[4,256,256]{2,1,0:T(8,128)(2,1)S(1)}, u32[]{:S(2)}, u32[]{:S(2)}) %all-to-all-start.2) | async-done | bytes 524320 | tf_op jit(solution)/shard_map/all_to_all | solution.py:145
  69.0 0.9 broadcast_in_dim.27
  70.0 4.2 %all-to-all-start.3 = ((bf16[4,10,40,256]{3,2,1,0:T(8,128)(2,1)}), bf16[4,10,40,256]{3,2,1,0:T(8,128)(2,1)S(1)}, u32[]{:S(2)}, u32[]{:S(2)}) async-start(bf16[4,10,40,256]{3,2,1,0:T(8,128)(2,1)} %broadcast_in_dim.27), calls=%async_computation.3 | async-start | bytes 1638400 | tf_op jit(solution)/shard_map/all_to_all | solution.py:145
  77.1 7.0 %all-to-all-done.3 = bf16[4,10,40,256]{3,2,1,0:T(8,128)(2,1)S(1)} async-done(((bf16[4,10,40,256]{3,2,1,0:T(8,128)(2,1)}), bf16[4,10,40,256]{3,2,1,0:T(8,128)(2,1)S(1)}, u32[]{:S(2)}, u32[]{:S(2)}) %all-to-all-start.3) | async-done | bytes 819232 | tf_op jit(solution)/shard_map/all_to_all | solution.py:145
  84.1 3.7 %forward.1 = (bf16[5,320,1024]{2,1,0:T(8,128)(2,1)S(1)}, f32[4,128,256]{2,1,0:T(8,128)S(1)}, f32[16,256]{1,0:T(8,128)S(1)}) custom-call(s32[4]{0:T(128)S(1)} %pad_add_fusion.info, s32[8]{0:T(128)S(1)} %select_reduce_fusion.starts, bf16[4,256,256]{2,1,0:T(8,128)(2,1)S(1)} %all-to-all-done.2.qg, bf16[4,5,80,256]{3,2,1,0:T(8,128)(2,1)S(1)} %bitcast.31), custom_call_target="tpu_custom_call" | custom-call | tf_op jit(solution)/shard_map/forward/pallas_call | solution.py:198
  87.8 7.0 %all_to_all.46.stats = f32[4,16,256]{2,1,0:T(8,128)S(1)} all-to-all(f32[4,16,256]{2,1,0:T(8,128)S(1)} %broadcast_in_dim.28), channel_id=1, replica_groups={{0,32,64,96},{128,160,192,224},{256,288,320,352},{384,416,448,480},{1,3..., dimensions={0} | all-to-all | bytes 131072 | tf_op jit(solution)/shard_map/all_to_all | solution.py:145
  94.7 5.3 %backward.1 = (bf16[4,256,256]{2,1,0:T(8,128)(2,1)}, bf16[4,5,80,256]{3,2,1,0:T(8,128)(2,1)S(1)}) custom-call(s32[4]{0:T(128)S(1)} %pad_add_fusion.info, bf16[4,256,256]{2,1,0:T(8,128)(2,1)S(1)} %all-to-all-done.2.qg, bf16[4,5,80,256]{3,2,1,0:T(8,128)(2,1)S(1)} %bitcast.32, bf16[5,320,1024]{2,1,0:T(8,128)(2,1)S(1)} %get-tuple-element.21.e_ref, ...), custom_call_target="tpu_custom_call" | custom-call | tf_op jit(solution)/shard_map/backward/pallas_call | solution.py:217
  100.0 10.9 %all_to_all.47 = bf16[4,10,40,256]{3,2,1,0:T(8,128)(2,1)S(1)} all-to-all(bf16[4,10,40,256]{3,2,1,0:T(8,128)(2,1)S(1)} %bitcast.33), channel_id=1, replica_groups=mesh['dp'=16,'head'=8,'srv'=4] {'srv'}, dimensions={0} | all-to-all | bytes 1638400 | tf_op jit(solution)/shard_map/all_to_all | solution.py:145
  110.9 3.5 %all-to-all-start.5 = ((bf16[4,256,256]{2,1,0:T(8,128)(2,1)}), bf16[4,256,256]{2,1,0:T(8,128)(2,1)S(1)}, u32[]{:S(2)}, u32[]{:S(2)}) async-start(bf16[4,256,256]{2,1,0:T(8,128)(2,1)} %get-tuple-element.24), calls=%async_computation.5 | async-start | bytes 1048576 | tf_op jit(solution)/shard_map/all_to_all | solution.py:145
  115.9 7.5 %all-to-all-done.5 = bf16[4,256,256]{2,1,0:T(8,128)(2,1)S(1)} async-done(((bf16[4,256,256]{2,1,0:T(8,128)(2,1)}), bf16[4,256,256]{2,1,0:T(8,128)(2,1)S(1)}, u32[]{:S(2)}, u32[]{:S(2)}) %all-to-all-start.5) | async-done | bytes 524320 | tf_op jit(solution)/shard_map/all_to_all | solution.py:145
  123.5 10.4 %all-to-all-start.7 = ((bf16[16,40,256]{2,1,0:T(8,128)(2,1)}), bf16[16,40,256]{2,1,0:T(8,128)(2,1)S(1)}, u32[]{:S(2)}, u32[]{:S(2)}) async-start(bf16[16,40,256]{2,1,0:T(8,128)(2,1)} %constant_dynamic-update-slice_fusion), calls=%async_computation.7 | async-start | bytes 655360 | tf_op jit(solution)/shard_map/all_to_all | solution.py:145
  133.9 13.5 %all-to-all-done.7 = bf16[16,40,256]{2,1,0:T(8,128)(2,1)S(1)} async-done(((bf16[16,40,256]{2,1,0:T(8,128)(2,1)}), bf16[16,40,256]{2,1,0:T(8,128)(2,1)S(1)}, u32[]{:S(2)}, u32[]{:S(2)}) %all-to-all-start.7) | async-done | bytes 327712 | tf_op jit(solution)/shard_map/all_to_all | solution.py:145
  148.1 14.3 %all-to-all-start.8 = ((bf16[8,20,256]{2,1,0:T(8,128)(2,1)}), bf16[8,20,256]{2,1,0:T(8,128)(2,1)S(1)}, u32[]{:S(2)}, u32[]{:S(2)}) async-start(bf16[8,20,256]{2,1,0:T(8,128)(2,1)} %reshape.141), calls=%async_computation.8 | async-start | bytes 196608 | tf_op jit(solution)/shard_map/all_to_all | solution.py:145
  163.0 4.3 %all-to-all-done.8 = bf16[8,20,256]{2,1,0:T(8,128)(2,1)S(1)} async-done(((bf16[8,20,256]{2,1,0:T(8,128)(2,1)}), bf16[8,20,256]{2,1,0:T(8,128)(2,1)S(1)}, u32[]{:S(2)}, u32[]{:S(2)}) %all-to-all-start.8) | async-done | bytes 81952 | tf_op jit(solution)/shard_map/all_to_all | solution.py:145
  (33 shorter events, 6.1 us)
Async XLA Ops:
  2.3 15.1 %all-to-all-start = ((bf16[8,20,256]{2,1,0:T(8,128)(2,1)}), bf16[8,20,256]{2,1,0:T(8,128)(2,1)S(1)}, u32[]{:S(2)}, u32[]{:S(2)}) async-start(bf16[8,20,256]{2,1,0:T(8,128)(2,1)} %copy.15), calls=%async_computation | async-start | bytes 196608 | tf_op jit(solution)/shard_map/all_to_all | solution.py:145
  18.2 28.6 %all-to-all-start.1 = ((bf16[16,48,256]{2,1,0:T(8,128)(2,1)}), bf16[16,48,256]{2,1,0:T(8,128)(2,1)S(1)}, u32[]{:S(2)}, u32[]{:S(2)}) async-start(bf16[16,48,256]{2,1,0:T(8,128)(2,1)} %bitcast.3), calls=%async_computation.1 | async-start | bytes 786432 | tf_op jit(solution)/shard_map/all_to_all | solution.py:145
  47.6 21.4 %all-to-all-start.2 = ((bf16[4,256,256]{2,1,0:T(8,128)(2,1)}), bf16[4,256,256]{2,1,0:T(8,128)(2,1)S(1)}, u32[]{:S(2)}, u32[]{:S(2)}) async-start(bf16[4,256,256]{2,1,0:T(8,128)(2,1)} %broadcast_in_dim.26), calls=%async_computation.2 | async-start | bytes 1048576 | tf_op jit(solution)/shard_map/all_to_all | solution.py:145
  70.0 14.1 %all-to-all-start.3 = ((bf16[4,10,40,256]{3,2,1,0:T(8,128)(2,1)}), bf16[4,10,40,256]{3,2,1,0:T(8,128)(2,1)S(1)}, u32[]{:S(2)}, u32[]{:S(2)}) async-start(bf16[4,10,40,256]{3,2,1,0:T(8,128)(2,1)} %broadcast_in_dim.27), calls=%async_computation.3 | async-start | bytes 1638400 | tf_op jit(solution)/shard_map/all_to_all | solution.py:145
  110.9 12.6 %all-to-all-start.5 = ((bf16[4,256,256]{2,1,0:T(8,128)(2,1)}), bf16[4,256,256]{2,1,0:T(8,128)(2,1)S(1)}, u32[]{:S(2)}, u32[]{:S(2)}) async-start(bf16[4,256,256]{2,1,0:T(8,128)(2,1)} %get-tuple-element.24), calls=%async_computation.5 | async-start | bytes 1048576 | tf_op jit(solution)/shard_map/all_to_all | solution.py:145
  123.5 23.9 %all-to-all-start.7 = ((bf16[16,40,256]{2,1,0:T(8,128)(2,1)}), bf16[16,40,256]{2,1,0:T(8,128)(2,1)S(1)}, u32[]{:S(2)}, u32[]{:S(2)}) async-start(bf16[16,40,256]{2,1,0:T(8,128)(2,1)} %constant_dynamic-update-slice_fusion), calls=%async_computation.7 | async-start | bytes 655360 | tf_op jit(solution)/shard_map/all_to_all | solution.py:145
  148.1 19.3 %all-to-all-start.8 = ((bf16[8,20,256]{2,1,0:T(8,128)(2,1)}), bf16[8,20,256]{2,1,0:T(8,128)(2,1)S(1)}, u32[]{:S(2)}, u32[]{:S(2)}) async-start(bf16[8,20,256]{2,1,0:T(8,128)(2,1)} %reshape.141), calls=%async_computation.8 | async-start | bytes 196608 | tf_op jit(solution)/shard_map/all_to_all | solution.py:145

commit v2 on v1

v2 whole, which is shorter than its diff:
```python
import functools

import jax
import jax.numpy as jnp
from jax import lax
from jax.experimental import pallas as pl
from jax.experimental.pallas import tpu as pltpu
from jax.sharding import PartitionSpec as P

HEAD = 128
DP = 16
QUAD = 4
BLOCKS = 3
SHARD = 640
CONTEXT = 8192
DOCS = 8
SCALE = HEAD**-0.5
EXP2_SCALE = SCALE * 1.4426950408889634
NEGATIVE = -1e30
NEAR = tuple(tuple(range(QUAD * q, QUAD * q + QUAD)) for q in range(DP // QUAD))
FAR = tuple(tuple(range(m, DP, QUAD)) for m in range(QUAD))

F32 = jnp.float32
BF16 = jnp.bfloat16
NT = (((1,), (1,)), ((), ()))
NN = (((1,), (0,)), ((), ()))
TN = (((0,), (0,)), ((), ()))


def dot(lhs, rhs, dims):
    return lax.dot_general(lhs, rhs, dims, preferred_element_type=F32)


def fold8(block, op):
    rows, cols = block.shape
    return op(block.reshape(rows // 8, 8, cols), axis=0)


def member_of(member, turn):
    return lax.rem(member - turn + QUAD, QUAD)


def forward_kernel(
    info, q0, q1, q2, q3, kv, e_ref, o_ref, stats_ref, active, s_ref, m_ref, l_ref
):
    quad, member = info[0], info[1]
    qs = (q0, q1, q2, q3)
    cols = o_ref.shape[2]
    srvs, _, part, _ = kv.shape
    keys = srvs * part
    query_at = CONTEXT + 2 * cols * quad

    count = sum(jnp.sum(q[cols:, :].astype(F32), axis=0, keepdims=True) for q in qs)
    lanes = lax.broadcasted_iota(jnp.int32, count.shape, 1)
    starts = []
    for doc in range(DOCS):
        high = jnp.sum(jnp.where(lanes < doc, count, 0.0)) * 64.0
        low = jnp.sum(jnp.where((lanes >= DOCS) & (lanes < DOCS + doc), count, 0.0))
        starts.append((high + low).astype(jnp.int32))
    reach = jnp.int32(0)
    for start in starts:
        reach = jnp.where(start <= query_at, jnp.maximum(reach, start), reach)
    first, last = jnp.int32(0), jnp.int32(0)
    for block in range(BLOCKS):
        shard = SHARD * (QUAD * (block + 1) + member)
        first += (shard + SHARD <= reach).astype(jnp.int32)
        last += (shard < query_at + 2 * cols).astype(jnp.int32)
    active[0] = first
    active[1] = last

    at = lax.broadcasted_iota(jnp.int32, (keys, 128), 0)
    rest = at % part
    pattern = 80 * (rest // 20) + 20 * (at // part) + rest % 20 + SHARD * (QUAD + member)
    pattern = jnp.concatenate([pattern] * (cols // 128), axis=1)
    lane = lax.broadcasted_iota(jnp.int32, (1, cols), 1)
    m_ref[...] = jnp.full(m_ref.shape, NEGATIVE, F32)
    l_ref[...] = jnp.zeros(l_ref.shape, F32)
    o_ref[...] = jnp.zeros(o_ref.shape, F32)
    query_places, doc_starts = [], []
    for turn in range(QUAD):
        query_place = query_at + (cols // 2) * member_of(member, turn) + lane // 2
        doc_start = jnp.zeros_like(query_place)
        for start in starts:
            doc_start = jnp.where(start <= query_place, jnp.maximum(doc_start, start), doc_start)
        query_places.append(query_place)
        doc_starts.append(doc_start)

    def scores(t, carry):
        k = kv[:, t, :, :HEAD].reshape(keys, HEAD)
        key_place = pattern + QUAD * SHARD * t
        for turn in range(QUAD):
            span = pl.ds(turn * cols, cols)
            s = dot(k, qs[turn][:cols, :HEAD], NT)
            allowed = (key_place >= doc_starts[turn]) & (key_place <= query_places[turn])
            s = jnp.where(allowed, s, NEGATIVE)
            s_ref[t, :, span] = s
            m_ref[turn] = jnp.maximum(m_ref[turn], fold8(s, jnp.max))
        return carry

    lax.fori_loop(first, last, scores, 0)
    tops = [jnp.max(m_ref[turn], axis=0, keepdims=True) for turn in range(QUAD)]

    def weigh(t, carry):
        v = kv[:, t, :, HEAD:].reshape(keys, HEAD)
        for turn in range(QUAD):
            span = pl.ds(turn * cols, cols)
            e = jnp.exp2((s_ref[t, :, span] - tops[turn]) * EXP2_SCALE)
            l_ref[turn] += fold8(e, jnp.sum)
            e = e.astype(BF16)
            e_ref[t, :, span] = e
            o_ref[turn] += dot(v, e, TN)
        return carry

    lax.fori_loop(first, last, weigh, 0)
    for turn in range(QUAD):
        tile = member_of(member, turn)
        gradient = qs[turn][:cols, HEAD:].astype(F32).T
        norm = jnp.sum(l_ref[turn], axis=0, keepdims=True)
        delta = jnp.sum(gradient * o_ref[turn], axis=0, keepdims=True)
        for copy in range(QUAD):
            stats_ref[copy, pl.ds(tile, 1), :] = tops[turn]
            stats_ref[copy, pl.ds(QUAD + tile, 1), :] = norm
            stats_ref[copy, pl.ds(2 * QUAD + tile, 1), :] = delta
            stats_ref[copy, pl.ds(3 * QUAD + tile, 1), :] = jnp.zeros_like(norm)


def backward_kernel(
    info, active, q0, q1, q2, q3, kv, e_ref, o_ref, stats, oq0, oq1, oq2, oq3, dkv_ref, dq_ref
):
    member = info[1]
    first, last = active[0], active[1]
    qs, oqs = (q0, q1, q2, q3), (oq0, oq1, oq2, oq3)
    cols = o_ref.shape[2]
    srvs, _, part, _ = kv.shape
    keys = srvs * part
    dq_ref[...] = jnp.zeros(dq_ref.shape, F32)
    shares, deltas = [], []
    for turn in range(QUAD):
        tile = member_of(member, turn)
        row = lambda who, kind: stats[who, pl.ds(kind * QUAD + tile, 1), :]
        top = functools.reduce(jnp.maximum, [row(who, 0) for who in range(QUAD)])
        weights = [jnp.exp2((row(who, 0) - top) * EXP2_SCALE) for who in range(QUAD)]
        norm = sum(weights[who] * row(who, 1) for who in range(QUAD))
        deltas.append(sum(weights[who] * row(who, 2) for who in range(QUAD)) / norm)
        shares.append(jnp.exp2((row(member, 0) - top) * EXP2_SCALE) / norm)

    def clear(t, carry):
        dkv_ref[:, t] = jnp.zeros((srvs, part, 2 * HEAD), BF16)
        return carry

    lax.fori_loop(0, first, clear, 0)
    lax.fori_loop(last, BLOCKS, clear, 0)

    def grads(t, carry):
        k = kv[:, t, :, :HEAD].reshape(keys, HEAD)
        v = kv[:, t, :, HEAD:].reshape(keys, HEAD)
        dk = jnp.zeros((keys, HEAD), F32)
        dv = jnp.zeros((keys, HEAD), F32)
        for turn in range(QUAD):
            q, gradient = qs[turn][:cols, :HEAD], qs[turn][:cols, HEAD:]
            p = e_ref[t, :, pl.ds(turn * cols, cols)].astype(F32) * shares[turn]
            ds = (p * (dot(v, gradient, NT) - deltas[turn])).astype(BF16)
            dv += dot(p.astype(BF16), gradient, NN)
            dk += dot(ds, q, NN)
            dq_ref[turn] += dot(k, ds, TN)
        dkv_ref[:, t, :, :HEAD] = (dk * SCALE).astype(BF16).reshape(srvs, part, HEAD)
        dkv_ref[:, t, :, HEAD:] = dv.astype(BF16).reshape(srvs, part, HEAD)
        return carry

    lax.fori_loop(first, last, grads, 0)
    for turn in range(QUAD):
        oqs[turn][:, :HEAD] = (o_ref[turn] * shares[turn]).T.astype(BF16)
        oqs[turn][:, HEAD:] = (dq_ref[turn] * SCALE).T.astype(BF16)


def exchange(block, axis, groups=None):
    return lax.all_to_all(block, axis, 0, 0, tiled=True, axis_index_groups=groups)


def rotate(block, turn):
    pairs = [(q[i], q[(i + turn) % QUAD]) for q in NEAR for i in range(QUAD)]
    return lax.ppermute(block, "dp", pairs)


def local(queries, keys, values, output_gradient, doc_ids):
    rows = queries.shape[0] * queries.shape[1]
    heads, srvs = 8, 4
    dp, srv = lax.axis_index("dp"), lax.axis_index("srv")
    info = jnp.stack([dp // QUAD, dp % QUAD]).astype(jnp.int32)
    shard_rows = keys.shape[0] // srvs
    part = heads * shard_rows
    vmem = pl.BlockSpec(memory_space=pltpu.VMEM)
    smem = pl.BlockSpec(memory_space=pltpu.SMEM)

    mine = lambda x: lax.dynamic_slice_in_dim(x, srv * shard_rows, shard_rows, 0).reshape(
        shard_rows, heads, HEAD
    )
    kv = jnp.concatenate([mine(keys), mine(values)], axis=2).transpose(1, 0, 2)
    kv = exchange(kv, "head").reshape(part, 2 * HEAD)
    count = jnp.sum(
        (doc_ids[:, None] == jnp.arange(DOCS, dtype=jnp.int32)[None, :]).astype(jnp.int32), axis=0
    )
    count = jnp.concatenate([count // 64, count % 64]).astype(BF16)
    count = jnp.pad(count[None], ((0, 7), (0, 2 * HEAD - 2 * DOCS)))
    kv = jnp.concatenate([kv, count], axis=0)
    kv = lax.all_gather(kv, "dp", axis=0, axis_index_groups=FAR)
    count = jnp.sum(kv[:, part:].astype(F32), axis=0).astype(BF16)
    kv = jnp.broadcast_to(kv[None, 1:, :part], (srvs, BLOCKS, part, 2 * HEAD))
    kv = exchange(kv, "srv").reshape(srvs, BLOCKS, part, 2 * HEAD)

    qg = jnp.concatenate(
        [queries.reshape(rows, HEAD), output_gradient.reshape(rows, HEAD)], axis=1
    )
    qg = jnp.concatenate([qg, count], axis=0)
    qs = [qg] + [rotate(qg, turn) for turn in range(1, QUAD)]

    key_block = srvs * part
    params = pltpu.CompilerParams(vmem_limit_bytes=40 * 1024 * 1024)
    e, o, stats, active = pl.pallas_call(
        forward_kernel,
        out_shape=(
            jax.ShapeDtypeStruct((BLOCKS, key_block, QUAD * rows), BF16),
            jax.ShapeDtypeStruct((QUAD, HEAD, rows), F32),
            jax.ShapeDtypeStruct((QUAD, 4 * QUAD, rows), F32),
            jax.ShapeDtypeStruct((2,), jnp.int32),
        ),
        in_specs=[smem] + [vmem] * 5,
        out_specs=(vmem, vmem, vmem, smem),
        scratch_shapes=[
            pltpu.VMEM((BLOCKS, key_block, QUAD * rows), F32),
            pltpu.VMEM((QUAD, 8, rows), F32),
            pltpu.VMEM((QUAD, 8, rows), F32),
        ],
        compiler_params=params,
        name="forward",
    )(info, *qs, kv)
    stats = exchange(stats.reshape(QUAD * 4 * QUAD, rows), "dp", NEAR)
    stats = stats.reshape(QUAD, 4 * QUAD, rows)
    *oqs, dkv = pl.pallas_call(
        backward_kernel,
        out_shape=(
            *[jax.ShapeDtypeStruct((rows, 2 * HEAD), BF16)] * QUAD,
            jax.ShapeDtypeStruct(kv.shape, BF16),
        ),
        in_specs=[smem, smem] + [vmem] * 8,
        out_specs=(vmem,) * 5,
        scratch_shapes=[pltpu.VMEM((QUAD, HEAD, rows), F32)],
        compiler_params=params,
        name="backward",
    )(info, active, *qs, kv, e, o, stats)

    oqs = [oqs[0]] + [rotate(oqs[turn], -turn) for turn in range(1, QUAD)]
    total = lambda x: jnp.sum(x.astype(F32), axis=0).astype(BF16)
    dkv = exchange(dkv, "srv")
    dkv, oqs = lax.optimization_barrier((dkv, oqs))
    dkv = total(dkv)
    dkv = jnp.concatenate([jnp.zeros_like(dkv[:1]), dkv], axis=0)
    dkv = total(exchange(dkv, "dp", FAR))
    dkv = exchange(dkv.reshape(heads, shard_rows, 2 * HEAD), "head")
    dkv = dkv.transpose(1, 0, 2)
    k_grad = dkv[:, :, :HEAD].reshape(shard_rows, heads * HEAD)
    v_grad = dkv[:, :, HEAD:].reshape(shard_rows, heads * HEAD)

    oq = sum(x.astype(F32) for x in oqs).astype(BF16)
    attention = oq[:, :HEAD].reshape(queries.shape)
    q_grad = oq[:, HEAD:].reshape(queries.shape)
    return attention, q_grad, k_grad, v_grad


def solution(mesh):
    placed = (
        P("dp", "srv", "head"),
        P(("dp", "head"), None),
        P(("dp", "head"), None),
        P("dp", "srv", "head"),
        P("dp"),
    )
    return jax.shard_map(
        local,
        mesh=mesh,
        in_specs=placed,
        out_specs=(
            P("dp", "srv", "head"),
            P("dp", "srv", "head"),
            P(("dp", "head", "srv"), None),
            P(("dp", "head", "srv"), None),
        ),
        check_vma=False,
    )
```

time: 170 us -> 132 us (0.78)
  waiting for transfers between devices: 66.8 us -> 33.3 us
  blocking collectives: 17.8 us -> 28.5 us
  starting transfers between devices: 61.1 us -> 54.3 us
  Pallas kernels: 8.92 us -> 6.42 us
  local copies, waits for them, and re-layouts: 8.19 us -> 6.06 us
  between operations: 2.77 us -> 0.87 us
    all_to_all x7 -> x5, waiting for transfers between devices: 66.8 us -> 21.7 us  [exchange(): lax.all_to_all(block, axis, 0, 0, tiled=True, axis_index_groups=groups)]
    all_to_all x7 -> x5, starting transfers between devices: 61.1 us -> 38.4 us  [exchange(): lax.all_to_all(block, axis, 0, 0, tiled=True, axis_index_groups=groups)]
    all_gather x0 -> x1, blocking collectives: none -> 21.2 us  [local(): kv = lax.all_gather(kv, 'dp', axis=0, axis_index_groups=FAR)]
    ppermute x0 -> x6, starting transfers between devices: none -> 15.9 us  [rotate(): return lax.ppermute(block, 'dp', pairs)]
    ppermute x0 -> x6, waiting for transfers between devices: none -> 11.6 us  [rotate(): return lax.ppermute(block, 'dp', pairs)]
    all_to_all x2 -> x1, blocking collectives: 17.8 us -> 7.27 us  [exchange(): lax.all_to_all(block, axis, 0, 0, tiled=True, axis_index_groups=groups)]
    pallas_call x2, Pallas kernels: 8.92 us -> 6.42 us  [the longest x1 3.26 us: local(): pl.pallas_call(backward_kernel, out_shape=(*[jax.ShapeDtypeStruct((rows,...]
    broadcast_in_dim x5 -> x1, local copies, waits for them, and re-layouts: 3.28 us -> 1.04 us  [local(): kv = jnp.broadcast_to(kv[None, 1:, :part], (srvs, BLOCKS, part, 2 * HEAD))]
  transfers between devices with their start and end apart: 7 -> 11, of which waited for: 7 -> 6; matrix products, arithmetic and copies ran while one was open for 3% -> 1% of each run, Pallas kernels for 0% -> 0%
where the time goes in v2:
time: 132 us; the launch traced here: 131 us
  starting transfers between devices  54.3 us (41%)
  waiting for transfers between devices  33.3 us (25%)
  blocking collectives  28.5 us (22%)
  Pallas kernels  6.42 us (5%)
  local copies, waits for them, and re-layouts  6.06 us (5%)
  other arithmetic  1.36 us (1%)
    all_to_all x5, starting transfers between devices, exchange(): lax.all_to_all(block, axis, 0, 0, tiled=True, axis_index_groups=groups)  38.4 us
    all_to_all x5, waiting for transfers between devices, exchange(): lax.all_to_all(block, axis, 0, 0, tiled=True, axis_index_groups=groups)  21.7 us
    all_gather x1, blocking collectives, local(): kv = lax.all_gather(kv, 'dp', axis=0, axis_index_groups=FAR)  21.2 us
    ppermute x6, starting transfers between devices, rotate(): return lax.ppermute(block, 'dp', pairs)  15.9 us
    ppermute x6, waiting for transfers between devices, rotate(): return lax.ppermute(block, 'dp', pairs)  11.6 us
    all_to_all x1, blocking collectives, exchange(): lax.all_to_all(block, axis, 0, 0, tiled=True, axis_index_groups=groups)  7.27 us
    pallas_call x1, Pallas kernels, local(): pl.pallas_call(backward_kernel, out_shape=(*[jax.ShapeDtypeStruct((rows,...  3.26 us
    pallas_call x1, Pallas kernels, local(): pl.pallas_call(forward_kernel, out_shape=(jax.ShapeDtypeStruct((BLOCKS, k...  3.16 us
  transfers between devices with their start and end apart: 11, of which 6 were waited for; matrix products, arithmetic and copies ran while one was open for 1% of the time, Pallas kernels for 0%

profile of v2, /device:TPU:1, one launch (start us, length us, event | category | flops | bytes accessed | tf_op | source)
XLA Modules:
  0.0 130.8 jit_solution(2740054538292490357)
XLA Ops:
  0.7 0.9 constant_dynamic-slice_fusion
  2.3 10.1 %all-to-all-start = ((bf16[8,20,256]{2,1,0:T(8,128)(2,1)}), bf16[8,20,256]{2,1,0:T(8,128)(2,1)S(1)}, u32[]{:S(2)}, u32[]{:S(2)}) async-start(bf16[8,20,256]{2,1,0:T(8,128)(2,1)} %copy.16), calls=%async_computation | async-start | bytes 196608 | tf_op jit(solution)/shard_map/all_to_all | solution.py:177
  12.5 0.8 convert_reduce_fusion
  13.4 4.1 %all-to-all-done = bf16[8,20,256]{2,1,0:T(8,128)(2,1)S(1)} async-done(((bf16[8,20,256]{2,1,0:T(8,128)(2,1)}), bf16[8,20,256]{2,1,0:T(8,128)(2,1)S(1)}, u32[]{:S(2)}, u32[]{:S(2)}) %all-to-all-start) | async-done | bytes 81952 | tf_op jit(solution)/shard_map/all_to_all | solution.py:177
  17.5 21.2 %all-gather = bf16[672,256]{1,0:T(8,128)(2,1)S(1)} all-gather(bf16[168,256]{1,0:T(8,128)(2,1)S(1)} %pad_maximum_fusion.1), channel_id=2, replica_groups={{0,128,256,384},{32,160,288,416},{64,192,320,448},{96,224,352,480},{1,1..., dimensions={0}, use_global_device_ids=true | all-gather | bytes 430080 | tf_op jit(solution)/shard_map/all_gather | solution.py:206
  38.7 1.0 broadcast_in_dim.2
  39.8 4.2 %all-to-all-start.1 = ((bf16[4,3,160,256]{3,2,1,0:T(8,128)(2,1)}), bf16[4,3,160,256]{3,2,1,0:T(8,128)(2,1)S(1)}, u32[]{:S(2)}, u32[]{:S(2)}) async-start(bf16[4,3,160,256]{3,2,1,0:T(8,128)(2,1)} %broadcast_in_dim.2), calls=%async_computation.1 | async-start | bytes 1966080 | tf_op jit(solution)/shard_map/all_to_all | solution.py:177
  44.0 3.7 %collective-permute-start.2 = (bf16[264,256]{1,0:T(8,128)(2,1)S(1)}, bf16[264,256]{1,0:T(8,128)(2,1)S(1)}, u32[]{:S(2)}, u32[]{:S(2)}) collective-permute-start(bf16[264,256]{1,0:T(8,128)(2,1)S(1)} %pad_maximum_fusion.q0), channel_id=1, source_target_pairs={{0,96},{32,0},{64,32},{96,64},{128,224},{160,128},{192,160},{224,1... | collective-permute-start | bytes 405512 | tf_op jit(solution)/shard_map/ppermute | solution.py:182
  47.8 1.9 %collective-permute-start.1 = (bf16[264,256]{1,0:T(8,128)(2,1)S(1)}, bf16[264,256]{1,0:T(8,128)(2,1)S(1)}, u32[]{:S(2)}, u32[]{:S(2)}) collective-permute-start(bf16[264,256]{1,0:T(8,128)(2,1)S(1)} %pad_maximum_fusion.q0), channel_id=1, source_target_pairs={{0,64},{32,96},{64,0},{96,32},{128,192},{160,224},{192,128},{224,1... | collective-permute-start | bytes 405512 | tf_op jit(solution)/shard_map/ppermute | solution.py:182
  49.7 2.7 %collective-permute-start = (bf16[264,256]{1,0:T(8,128)(2,1)S(1)}, bf16[264,256]{1,0:T(8,128)(2,1)S(1)}, u32[]{:S(2)}, u32[]{:S(2)}) collective-permute-start(bf16[264,256]{1,0:T(8,128)(2,1)S(1)} %pad_maximum_fusion.q0), channel_id=1, source_target_pairs={{0,32},{32,64},{64,96},{96,0},{128,160},{160,192},{192,224},{224,1... | collective-permute-start | bytes 405512 | tf_op jit(solution)/shard_map/ppermute | solution.py:182
  52.5 5.8 %collective-permute-done.1.q2 = bf16[264,256]{1,0:T(8,128)(2,1)S(1)} collective-permute-done((bf16[264,256]{1,0:T(8,128)(2,1)S(1)}, bf16[264,256]{1,0:T(8,128)(2,1)S(1)}, u32[]{:S(2)}, u32[]{:S(2)}) %collective-permute-start.1) | collective-permute-done | bytes 135200 | tf_op jit(solution)/shard_map/ppermute | solution.py:182
  58.4 3.2 %forward.1 = (bf16[3,640,1024]{2,1,0:T(8,128)(2,1)S(1)}, f32[4,128,256]{2,1,0:T(8,128)S(1)}, f32[4,16,256]{2,1,0:T(8,128)S(1)}, s32[2]{0:T(128)S(1)}) custom-call(s32[2]{0:T(128)S(1)} %pad_add_fusion.info, bf16[264,256]{1,0:T(8,128)(2,1)S(1)} %pad_maximum_fusion.q0, bf16[264,256]{1,0:T(8,128)(2,1)S(1)} %collective-permute-done.q1, ...), custom_call_target="tpu_custom_call" | custom-call | tf_op jit(solution)/shard_map/forward/pallas_call | solution.py:219
  61.5 7.3 %all_to_all.31.stats = f32[4,16,256]{2,1,0:T(8,128)S(1)} all-to-all(f32[4,16,256]{2,1,0:T(8,128)S(1)} %get-tuple-element.21), channel_id=1, replica_groups={{0,32,64,96},{128,160,192,224},{256,288,320,352},{384,416,448,480},{1,3..., dimensions={0} | all-to-all | bytes 131072 | tf_op jit(solution)/shard_map/all_to_all | solution.py:177
  68.8 3.3 %backward.1 = (bf16[256,256]{1,0:T(8,128)(2,1)S(1)}, bf16[256,256]{1,0:T(8,128)(2,1)S(1)}, bf16[256,256]{1,0:T(8,128)(2,1)S(1)}, bf16[256,256]{1,0:T(8,128)(2,1)S(1)}, bf16[4,3,160,256]{3,2,1,0:T(8,128)(2,1)}) custom-call(s32[2]{0:T(128)S(1)} %pad_add_fusion.info, s32[2]{0:T(128)S(1)} %get-tuple-element.18.active, bf16[264,256]{1,0:T(8,128)(2,1)S(1)} %pad_maximum_fusion.q0, ...), custom_call_target="tpu_custom_call" | custom-call | tf_op jit(solution)/shard_map/backward/pallas_call | solution.py:239
  72.1 4.1 %all-to-all-start.3 = ((bf16[4,3,160,256]{3,2,1,0:T(8,128)(2,1)}), bf16[4,3,160,256]{3,2,1,0:T(8,128)(2,1)S(1)}, u32[]{:S(2)}, u32[]{:S(2)}) async-start(bf16[4,3,160,256]{3,2,1,0:T(8,128)(2,1)} %get-tuple-element.22), calls=%async_computation.3 | async-start | bytes 1966080 | tf_op jit(solution)/shard_map/all_to_all | solution.py:177
  76.2 1.9 %collective-permute-start.3 = (bf16[256,256]{1,0:T(8,128)(2,1)S(1)}, bf16[256,256]{1,0:T(8,128)(2,1)S(1)}, u32[]{:S(2)}, u32[]{:S(2)}) collective-permute-start(bf16[256,256]{1,0:T(8,128)(2,1)S(1)} %get-tuple-element.24), channel_id=1, source_target_pairs={{0,96},{32,0},{64,32},{96,64},{128,224},{160,128},{192,160},{224,1... | collective-permute-start | bytes 393224 | tf_op jit(solution)/shard_map/ppermute | solution.py:182
  78.1 3.7 %collective-permute-start.4 = (bf16[256,256]{1,0:T(8,128)(2,1)S(1)}, bf16[256,256]{1,0:T(8,128)(2,1)S(1)}, u32[]{:S(2)}, u32[]{:S(2)}) collective-permute-start(bf16[256,256]{1,0:T(8,128)(2,1)S(1)} %get-tuple-element.25), channel_id=1, source_target_pairs={{0,64},{32,96},{64,0},{96,32},{128,192},{160,224},{192,128},{224,1... | collective-permute-start | bytes 393224 | tf_op jit(solution)/shard_map/ppermute | solution.py:182
  81.8 1.9 %collective-permute-start.5 = (bf16[256,256]{1,0:T(8,128)(2,1)S(1)}, bf16[256,256]{1,0:T(8,128)(2,1)S(1)}, u32[]{:S(2)}, u32[]{:S(2)}) collective-permute-start(bf16[256,256]{1,0:T(8,128)(2,1)S(1)} %get-tuple-element.26), channel_id=1, source_target_pairs={{0,32},{32,64},{64,96},{96,0},{128,160},{160,192},{192,224},{224,1... | collective-permute-start | bytes 393224 | tf_op jit(solution)/shard_map/ppermute | solution.py:182
  83.7 2.4 %collective-permute-done.4 = bf16[256,256]{1,0:T(8,128)(2,1)S(1)} collective-permute-done((bf16[256,256]{1,0:T(8,128)(2,1)S(1)}, bf16[256,256]{1,0:T(8,128)(2,1)S(1)}, u32[]{:S(2)}, u32[]{:S(2)}) %collective-permute-start.4) | collective-permute-done | bytes 131104 | tf_op jit(solution)/shard_map/ppermute | solution.py:182
  86.1 3.4 %collective-permute-done.5 = bf16[256,256]{1,0:T(8,128)(2,1)S(1)} collective-permute-done((bf16[256,256]{1,0:T(8,128)(2,1)S(1)}, bf16[256,256]{1,0:T(8,128)(2,1)S(1)}, u32[]{:S(2)}, u32[]{:S(2)}) %collective-permute-start.5) | collective-permute-done | bytes 131104 | tf_op jit(solution)/shard_map/ppermute | solution.py:182
  90.4 8.2 %all-to-all-start.4 = ((bf16[4,160,256]{2,1,0:T(8,128)(2,1)}), bf16[4,160,256]{2,1,0:T(8,128)(2,1)S(1)}, u32[]{:S(2)}, u32[]{:S(2)}) async-start(bf16[4,160,256]{2,1,0:T(8,128)(2,1)} %concatenate.37), calls=%async_computation.4 | async-start | bytes 655360 | tf_op jit(solution)/shard_map/all_to_all | solution.py:177
  98.7 13.3 %all-to-all-done.4 = bf16[4,160,256]{2,1,0:T(8,128)(2,1)S(1)} async-done(((bf16[4,160,256]{2,1,0:T(8,128)(2,1)}), bf16[4,160,256]{2,1,0:T(8,128)(2,1)S(1)}, u32[]{:S(2)}, u32[]{:S(2)}) %all-to-all-start.4) | async-done | bytes 327712 | tf_op jit(solution)/shard_map/all_to_all | solution.py:177
  112.7 11.8 %all-to-all-start.5 = ((bf16[8,20,256]{2,1,0:T(8,128)(2,1)}), bf16[8,20,256]{2,1,0:T(8,128)(2,1)S(1)}, u32[]{:S(2)}, u32[]{:S(2)}) async-start(bf16[8,20,256]{2,1,0:T(8,128)(2,1)} %reshape.78), calls=%async_computation.5 | async-start | bytes 196608 | tf_op jit(solution)/shard_map/all_to_all | solution.py:177
  125.1 4.3 %all-to-all-done.5 = bf16[8,20,256]{2,1,0:T(8,128)(2,1)S(1)} async-done(((bf16[8,20,256]{2,1,0:T(8,128)(2,1)}), bf16[8,20,256]{2,1,0:T(8,128)(2,1)S(1)}, u32[]{:S(2)}, u32[]{:S(2)}) %all-to-all-start.5) | async-done | bytes 81952 | tf_op jit(solution)/shard_map/all_to_all | solution.py:177
  (36 shorter events, 4.6 us)
Async XLA Ops:
  0.6 43.3 %copy-start = (bf16[128,2,128]{2,1,0:T(2,128)(2,1)S(1)}, bf16[128,2,128]{2,1,0:T(2,128)(2,1)}, u32[]{:S(2)}) copy-start(bf16[128,2,128]{2,1,0:T(2,128)(2,1)} %param.8) | copy-start | bytes 196612
  0.6 43.3 %copy-start.1 = (bf16[128,2,128]{2,1,0:T(2,128)(2,1)S(1)}, bf16[128,2,128]{2,1,0:T(2,128)(2,1)}, u32[]{:S(2)}) copy-start(bf16[128,2,128]{2,1,0:T(2,128)(2,1)} %param.5) | copy-start | bytes 196612
  2.3 15.1 %all-to-all-start = ((bf16[8,20,256]{2,1,0:T(8,128)(2,1)}), bf16[8,20,256]{2,1,0:T(8,128)(2,1)S(1)}, u32[]{:S(2)}, u32[]{:S(2)}) async-start(bf16[8,20,256]{2,1,0:T(8,128)(2,1)} %copy.16), calls=%async_computation | async-start | bytes 196608 | tf_op jit(solution)/shard_map/all_to_all | solution.py:177
  39.8 18.6 %all-to-all-start.1 = ((bf16[4,3,160,256]{3,2,1,0:T(8,128)(2,1)}), bf16[4,3,160,256]{3,2,1,0:T(8,128)(2,1)S(1)}, u32[]{:S(2)}, u32[]{:S(2)}) async-start(bf16[4,3,160,256]{3,2,1,0:T(8,128)(2,1)} %broadcast_in_dim.2), calls=%async_computation.1 | async-start | bytes 1966080 | tf_op jit(solution)/shard_map/all_to_all | solution.py:177
  44.0 8.5 %collective-permute-start.2 = (bf16[264,256]{1,0:T(8,128)(2,1)S(1)}, bf16[264,256]{1,0:T(8,128)(2,1)S(1)}, u32[]{:S(2)}, u32[]{:S(2)}) collective-permute-start(bf16[264,256]{1,0:T(8,128)(2,1)S(1)} %pad_maximum_fusion.q0), channel_id=1, source_target_pairs={{0,96},{32,0},{64,32},{96,64},{128,224},{160,128},{192,160},{224,1... | collective-permute-start | bytes 405512 | tf_op jit(solution)/shard_map/ppermute | solution.py:182
  47.8 10.6 %collective-permute-start.1 = (bf16[264,256]{1,0:T(8,128)(2,1)S(1)}, bf16[264,256]{1,0:T(8,128)(2,1)S(1)}, u32[]{:S(2)}, u32[]{:S(2)}) collective-permute-start(bf16[264,256]{1,0:T(8,128)(2,1)S(1)} %pad_maximum_fusion.q0), channel_id=1, source_target_pairs={{0,64},{32,96},{64,0},{96,32},{128,192},{160,224},{192,128},{224,1... | collective-permute-start | bytes 405512 | tf_op jit(solution)/shard_map/ppermute | solution.py:182
  49.7 8.7 %collective-permute-start = (bf16[264,256]{1,0:T(8,128)(2,1)S(1)}, bf16[264,256]{1,0:T(8,128)(2,1)S(1)}, u32[]{:S(2)}, u32[]{:S(2)}) collective-permute-start(bf16[264,256]{1,0:T(8,128)(2,1)S(1)} %pad_maximum_fusion.q0), channel_id=1, source_target_pairs={{0,32},{32,64},{64,96},{96,0},{128,160},{160,192},{192,224},{224,1... | collective-permute-start | bytes 405512 | tf_op jit(solution)/shard_map/ppermute | solution.py:182
  72.1 17.4 %all-to-all-start.3 = ((bf16[4,3,160,256]{3,2,1,0:T(8,128)(2,1)}), bf16[4,3,160,256]{3,2,1,0:T(8,128)(2,1)S(1)}, u32[]{:S(2)}, u32[]{:S(2)}) async-start(bf16[4,3,160,256]{3,2,1,0:T(8,128)(2,1)} %get-tuple-element.22), calls=%async_computation.3 | async-start | bytes 1966080 | tf_op jit(solution)/shard_map/all_to_all | solution.py:177
  76.2 7.6 %collective-permute-start.3 = (bf16[256,256]{1,0:T(8,128)(2,1)S(1)}, bf16[256,256]{1,0:T(8,128)(2,1)S(1)}, u32[]{:S(2)}, u32[]{:S(2)}) collective-permute-start(bf16[256,256]{1,0:T(8,128)(2,1)S(1)} %get-tuple-element.24), channel_id=1, source_target_pairs={{0,96},{32,0},{64,32},{96,64},{128,224},{160,128},{192,160},{224,1... | collective-permute-start | bytes 393224 | tf_op jit(solution)/shard_map/ppermute | solution.py:182
  78.1 8.0 %collective-permute-start.4 = (bf16[256,256]{1,0:T(8,128)(2,1)S(1)}, bf16[256,256]{1,0:T(8,128)(2,1)S(1)}, u32[]{:S(2)}, u32[]{:S(2)}) collective-permute-start(bf16[256,256]{1,0:T(8,128)(2,1)S(1)} %get-tuple-element.25), channel_id=1, source_target_pairs={{0,64},{32,96},{64,0},{96,32},{128,192},{160,224},{192,128},{224,1... | collective-permute-start | bytes 393224 | tf_op jit(solution)/shard_map/ppermute | solution.py:182
  81.8 7.7 %collective-permute-start.5 = (bf16[256,256]{1,0:T(8,128)(2,1)S(1)}, bf16[256,256]{1,0:T(8,128)(2,1)S(1)}, u32[]{:S(2)}, u32[]{:S(2)}) collective-permute-start(bf16[256,256]{1,0:T(8,128)(2,1)S(1)} %get-tuple-element.26), channel_id=1, source_target_pairs={{0,32},{32,64},{64,96},{96,0},{128,160},{160,192},{192,224},{224,1... | collective-permute-start | bytes 393224 | tf_op jit(solution)/shard_map/ppermute | solution.py:182
  90.4 21.6 %all-to-all-start.4 = ((bf16[4,160,256]{2,1,0:T(8,128)(2,1)}), bf16[4,160,256]{2,1,0:T(8,128)(2,1)S(1)}, u32[]{:S(2)}, u32[]{:S(2)}) async-start(bf16[4,160,256]{2,1,0:T(8,128)(2,1)} %concatenate.37), calls=%async_computation.4 | async-start | bytes 655360 | tf_op jit(solution)/shard_map/all_to_all | solution.py:177
  112.7 16.8 %all-to-all-start.5 = ((bf16[8,20,256]{2,1,0:T(8,128)(2,1)}), bf16[8,20,256]{2,1,0:T(8,128)(2,1)S(1)}, u32[]{:S(2)}, u32[]{:S(2)}) async-start(bf16[8,20,256]{2,1,0:T(8,128)(2,1)} %reshape.78), calls=%async_computation.5 | async-start | bytes 196608 | tf_op jit(solution)/shard_map/all_to_all | solution.py:177

commit v3 on v2

v3 whole, which is shorter than its diff:
```python
import functools

import jax
import jax.numpy as jnp
from jax import lax
from jax.experimental import pallas as pl
from jax.experimental.pallas import tpu as pltpu
from jax.sharding import PartitionSpec as P

HEAD = 128
DP = 16
QUAD = 4
BLOCKS = 3
SHARD = 640
CONTEXT = 8192
DOCS = 8
GROUPS = 8
SRVS = 4
PIECE = SHARD // GROUPS // SRVS
SCALE = HEAD**-0.5
EXP2_SCALE = SCALE * 1.4426950408889634
NEGATIVE = -1e30
NEAR = tuple(tuple(range(QUAD * q, QUAD * q + QUAD)) for q in range(DP // QUAD))
FAR = tuple(tuple(range(m, DP, QUAD)) for m in range(QUAD))

F32 = jnp.float32
BF16 = jnp.bfloat16
NT = (((1,), (1,)), ((), ()))
NN = (((1,), (0,)), ((), ()))


def dot(lhs, rhs, dims):
    return lax.dot_general(lhs, rhs, dims, preferred_element_type=F32)


def flip(block):
    size = block.shape[1]
    rows = lax.broadcasted_iota(jnp.int32, (size, size), 0)
    columns = lax.broadcasted_iota(jnp.int32, (size, size), 1)
    return dot((rows == columns).astype(BF16), block, NT)


def fold8(block, op):
    rows, cols = block.shape
    return op(block.reshape(rows // 8, 8, cols), axis=0)


def member_of(member, turn):
    return lax.rem(member - turn + QUAD, QUAD)


def fetch(sources, targets, sems):
    copies = [
        pltpu.make_async_copy(source, target, sems.at[i])
        for i, (source, target) in enumerate(zip(sources, targets))
    ]
    for copy in copies:
        copy.start()
    return copies


def pack_kernel(
    docs_in, keys_in, values_in, out_ref, docs, keys, values, k_ref, v_ref, f_ref, sems
):
    srv = lax.axis_index("srv")
    for copy in fetch((docs_in, keys_in, values_in), (docs, keys, values), sems):
        copy.wait()
    k_ref[...] = keys[...].astype(F32)
    v_ref[...] = values[...].astype(F32)

    def mine(ref):
        piece = ref[:PIECE, :]
        for part in range(1, SRVS):
            other = ref[PIECE * part : PIECE * (part + 1), :]
            piece = jnp.where(srv == part, other, piece)
        return piece

    k, v = mine(k_ref), mine(v_ref)
    for group in range(GROUPS):
        span = slice(PIECE * group, PIECE * (group + 1))
        columns = slice(HEAD * group, HEAD * (group + 1))
        f_ref[span, :HEAD] = k[:, columns]
        f_ref[span, HEAD:] = v[:, columns]
    lanes = lax.broadcasted_iota(jnp.int32, (8, 2 * HEAD), 1)
    row = jnp.zeros((8, 2 * HEAD), F32)
    for doc in range(DOCS):
        count = jnp.sum(jnp.where(docs[...] == doc, 1.0, 0.0), axis=1, keepdims=True)
        count = jnp.sum(count, axis=0, keepdims=True).astype(jnp.int32)
        row = jnp.where(lanes == doc, (count >> 6).astype(F32), row)
        row = jnp.where(lanes == DOCS + doc, (count & 63).astype(F32), row)
    first = lax.broadcasted_iota(jnp.int32, (8, 2 * HEAD), 0) == 0
    f_ref[PIECE * GROUPS :, :] = jnp.where(first, row, 0.0)
    out_ref[...] = f_ref[...].astype(BF16)


def fan_kernel(gathered, queries, gradient, out_ref, qg_ref, f_ref, slab_ref, sems):
    rows = queries.shape[0]
    targets = (qg_ref.at[pl.ds(0, rows), pl.ds(0, HEAD)], qg_ref.at[pl.ds(0, rows), pl.ds(HEAD, HEAD)])
    copies = fetch((queries, gradient), targets, sems)
    for quad in range(QUAD):
        f_ref[quad] = gathered[quad].astype(F32)
    for group in range(GROUPS):
        for block in range(BLOCKS):
            slab_ref[group, PIECE * block : PIECE * (block + 1), :] = f_ref[
                block + 1, PIECE * group : PIECE * (group + 1), :
            ]
        slab = slab_ref[group].astype(BF16)
        for srv in range(SRVS):
            out_ref[group, srv] = slab
    count = sum(f_ref[quad, PIECE * GROUPS :, :] for quad in range(QUAD))
    qg_ref[rows:, :] = count.astype(BF16)
    for copy in copies:
        copy.wait()


def fold_kernel(parts, out_ref, slab_ref, f_ref):
    for group in range(GROUPS):
        slab_ref[group] = sum(parts[group, srv].astype(F32) for srv in range(SRVS))
        for block in range(BLOCKS):
            f_ref[block, PIECE * group : PIECE * (group + 1), :] = slab_ref[
                group, PIECE * block : PIECE * (block + 1), :
            ]
    out_ref[0] = jnp.zeros(out_ref.shape[1:], BF16)
    for block in range(BLOCKS):
        out_ref[block + 1] = f_ref[block].astype(BF16)


def finish_kernel(parts, k_ref, v_ref, f_ref):
    f_ref[...] = sum(parts[quad].astype(F32) for quad in range(QUAD))
    for group in range(GROUPS):
        span = slice(PIECE * group, PIECE * (group + 1))
        columns = slice(HEAD * group, HEAD * (group + 1))
        k_ref[:, columns] = f_ref[span, :HEAD].astype(BF16)
        v_ref[:, columns] = f_ref[span, HEAD:].astype(BF16)


def forward_kernel(
    qg, slabs, e_ref, o_ref, stats_ref, active, kv, s_ref, m_ref, l_ref, slab_ref, f_ref
):
    dp = lax.axis_index("dp")
    quad, member = dp // QUAD, dp % QUAD
    qs = [qg.at[member_of(member, turn)] for turn in range(QUAD)]
    cols = o_ref.shape[2]
    keys = kv.shape[1]
    query_at = CONTEXT + 2 * cols * quad

    count = sum(jnp.sum(qg[who, cols:, :].astype(F32), axis=0, keepdims=True) for who in range(QUAD))
    lanes = lax.broadcasted_iota(jnp.int32, count.shape, 1)
    starts = []
    for doc in range(DOCS):
        high = jnp.sum(jnp.where(lanes < doc, count, 0.0)) * 64.0
        low = jnp.sum(jnp.where((lanes >= DOCS) & (lanes < DOCS + doc), count, 0.0))
        starts.append((high + low).astype(jnp.int32))
    reach = jnp.int32(0)
    for start in starts:
        reach = jnp.where(start <= query_at, jnp.maximum(reach, start), reach)
    first, last = jnp.int32(0), jnp.int32(0)
    for block in range(BLOCKS):
        shard = SHARD * (QUAD * (block + 1) + member)
        first += (shard + SHARD <= reach).astype(jnp.int32)
        last += (shard < query_at + 2 * cols).astype(jnp.int32)
    active[0] = first
    active[1] = last

    for group in range(GROUPS):
        for srv in range(SRVS):
            slab_ref[group, srv] = slabs[group, srv].astype(F32)
            at = PIECE * (SRVS * group + srv)
            for block in range(BLOCKS):
                f_ref[block, at : at + PIECE, :] = slab_ref[
                    group, srv, PIECE * block : PIECE * (block + 1), :
                ]
    for block in range(BLOCKS):
        kv[block] = f_ref[block].astype(BF16)

    pattern = lax.broadcasted_iota(jnp.int32, (keys, cols), 0) + SHARD * (QUAD + member)
    lane = lax.broadcasted_iota(jnp.int32, (1, cols), 1)
    m_ref[...] = jnp.full(m_ref.shape, NEGATIVE, F32)
    l_ref[...] = jnp.zeros(l_ref.shape, F32)
    o_ref[...] = jnp.zeros(o_ref.shape, F32)
    query_places, doc_starts = [], []
    for turn in range(QUAD):
        query_place = query_at + (cols // 2) * member_of(member, turn) + lane // 2
        doc_start = jnp.zeros_like(query_place)
        for start in starts:
            doc_start = jnp.where(start <= query_place, jnp.maximum(doc_start, start), doc_start)
        query_places.append(query_place)
        doc_starts.append(doc_start)

    def scores(t, carry):
        k = kv[t, :, :HEAD]
        key_place = pattern + QUAD * SHARD * t
        for turn in range(QUAD):
            span = pl.ds(turn * cols, cols)
            s = dot(k, qs[turn][:cols, :HEAD], NT)
            allowed = (key_place >= doc_starts[turn]) & (key_place <= query_places[turn])
            s = jnp.where(allowed, s, NEGATIVE)
            s_ref[t, :, span] = s
            m_ref[turn] = jnp.maximum(m_ref[turn], fold8(s, jnp.max))
        return carry

    lax.fori_loop(first, last, scores, 0)
    tops = [jnp.max(m_ref[turn], axis=0, keepdims=True) for turn in range(QUAD)]

    def weigh(t, carry):
        v = flip(kv[t, :, HEAD:]).astype(BF16)
        for turn in range(QUAD):
            span = pl.ds(turn * cols, cols)
            e = jnp.exp2((s_ref[t, :, span] - tops[turn]) * EXP2_SCALE)
            l_ref[turn] += fold8(e, jnp.sum)
            e = e.astype(BF16)
            e_ref[t, :, span] = e
            o_ref[turn] += dot(v, e, NN)
        return carry

    lax.fori_loop(first, last, weigh, 0)
    for turn in range(QUAD):
        tile = member_of(member, turn)
        gradient = flip(qs[turn][:cols, HEAD:])
        norm = jnp.sum(l_ref[turn], axis=0, keepdims=True)
        delta = jnp.sum(gradient * o_ref[turn], axis=0, keepdims=True)
        for copy in range(QUAD):
            stats_ref[copy, pl.ds(tile, 1), :] = tops[turn]
            stats_ref[copy, pl.ds(QUAD + tile, 1), :] = norm
            stats_ref[copy, pl.ds(2 * QUAD + tile, 1), :] = delta
            stats_ref[copy, pl.ds(3 * QUAD + tile, 1), :] = jnp.zeros_like(norm)


def backward_kernel(
    active, qg, kv, e_ref, o_ref, stats, oq0, oq1, oq2, oq3, dkv_ref, dq_ref, f_ref, slab_ref
):
    member = lax.axis_index("dp") % QUAD
    first, last = active[0], active[1]
    qs = [qg.at[member_of(member, turn)] for turn in range(QUAD)]
    oqs = (oq0, oq1, oq2, oq3)
    cols = o_ref.shape[2]
    keys = kv.shape[1]
    dq_ref[...] = jnp.zeros(dq_ref.shape, F32)
    shares, deltas = [], []
    for turn in range(QUAD):
        tile = member_of(member, turn)
        row = lambda who, kind: stats[who, pl.ds(kind * QUAD + tile, 1), :]
        top = functools.reduce(jnp.maximum, [row(who, 0) for who in range(QUAD)])
        weights = [jnp.exp2((row(who, 0) - top) * EXP2_SCALE) for who in range(QUAD)]
        norm = sum(weights[who] * row(who, 1) for who in range(QUAD))
        deltas.append(sum(weights[who] * row(who, 2) for who in range(QUAD)) / norm)
        shares.append(jnp.exp2((row(member, 0) - top) * EXP2_SCALE) / norm)

    def clear(t, carry):
        f_ref[t] = jnp.zeros((keys, 2 * HEAD), F32)
        return carry

    lax.fori_loop(0, first, clear, 0)
    lax.fori_loop(last, BLOCKS, clear, 0)

    def grads(t, carry):
        k = kv[t, :, :HEAD]
        v = kv[t, :, HEAD:]
        kt = flip(k).astype(BF16)
        dk = jnp.zeros((keys, HEAD), F32)
        dv = jnp.zeros((keys, HEAD), F32)
        for turn in range(QUAD):
            q, gradient = qs[turn][:cols, :HEAD], qs[turn][:cols, HEAD:]
            p = e_ref[t, :, pl.ds(turn * cols, cols)].astype(F32) * shares[turn]
            ds = (p * (dot(v, gradient, NT) - deltas[turn])).astype(BF16)
            dv += dot(p.astype(BF16), gradient, NN)
            dk += dot(ds, q, NN)
            dq_ref[turn] += dot(kt, ds, NN)
        f_ref[t, :, :HEAD] = dk * SCALE
        f_ref[t, :, HEAD:] = dv
        return carry

    lax.fori_loop(first, last, grads, 0)
    for turn in range(QUAD):
        oqs[turn][:, :HEAD] = flip((o_ref[turn] * shares[turn]).astype(BF16)).astype(BF16)
        oqs[turn][:, HEAD:] = flip((dq_ref[turn] * SCALE).astype(BF16)).astype(BF16)
    for group in range(GROUPS):
        for srv in range(SRVS):
            at = PIECE * (SRVS * group + srv)
            for block in range(BLOCKS):
                slab_ref[group, srv, PIECE * block : PIECE * (block + 1), :] = f_ref[
                    block, at : at + PIECE, :
                ]
            dkv_ref[group, srv] = slab_ref[group, srv].astype(BF16)


def exchange(block, axis, groups=None):
    return lax.all_to_all(block, axis, 0, 0, tiled=True, axis_index_groups=groups)


def rotate(block, turn):
    pairs = [(q[i], q[(i + turn) % QUAD]) for q in NEAR for i in range(QUAD)]
    return lax.ppermute(block, "dp", pairs)


def local(queries, keys, values, output_gradient, doc_ids):
    rows = queries.shape[0] * queries.shape[1]
    part = GROUPS * PIECE
    wide = 2 * HEAD
    vmem = pl.BlockSpec(memory_space=pltpu.VMEM)
    smem = pl.BlockSpec(memory_space=pltpu.SMEM)
    params = pltpu.CompilerParams(vmem_limit_bytes=30 * 1024 * 1024)
    roomy = pltpu.CompilerParams(vmem_limit_bytes=60 * 1024 * 1024)
    call = functools.partial(pl.pallas_call, compiler_params=params)
    slabs_shape = (GROUPS, SRVS, BLOCKS * PIECE, wide)

    hbm = pl.BlockSpec(memory_space=pltpu.HBM)
    sources = (doc_ids.reshape(-1, 128), keys, values)
    packed = pl.pallas_call(
        pack_kernel,
        out_shape=jax.ShapeDtypeStruct((part + 8, wide), BF16),
        in_specs=[hbm] * 3,
        out_specs=vmem,
        scratch_shapes=[pltpu.VMEM(x.shape, x.dtype) for x in sources]
        + [
            pltpu.VMEM(keys.shape, F32),
            pltpu.VMEM(values.shape, F32),
            pltpu.VMEM((part + 8, wide), F32),
            pltpu.SemaphoreType.DMA((3,)),
        ],
        compiler_params=roomy,
        name="pack",
    )(*sources)
    gathered = lax.all_gather(packed, "dp", axis=0, axis_index_groups=FAR)
    slabs, qg = pl.pallas_call(
        fan_kernel,
        out_shape=(
            jax.ShapeDtypeStruct(slabs_shape, BF16),
            jax.ShapeDtypeStruct((rows + 8, wide), BF16),
        ),
        in_specs=[vmem, hbm, hbm],
        out_specs=(vmem, vmem),
        scratch_shapes=[
            pltpu.VMEM((QUAD, part + 8, wide), F32),
            pltpu.VMEM((GROUPS, BLOCKS * PIECE, wide), F32),
            pltpu.SemaphoreType.DMA((2,)),
        ],
        compiler_params=roomy,
        name="fan",
    )(gathered, queries.reshape(rows, HEAD), output_gradient.reshape(rows, HEAD))
    flat = (GROUPS * SRVS, BLOCKS * PIECE, wide)
    slabs = exchange(slabs.reshape(flat), ("head", "srv")).reshape(slabs_shape)
    qg = lax.all_gather(qg, "dp", axis=0, axis_index_groups=NEAR)

    e, o, stats, active, kv = call(
        forward_kernel,
        out_shape=(
            jax.ShapeDtypeStruct((BLOCKS, SHARD, QUAD * rows), BF16),
            jax.ShapeDtypeStruct((QUAD, HEAD, rows), F32),
            jax.ShapeDtypeStruct((QUAD, 4 * QUAD, rows), F32),
            jax.ShapeDtypeStruct((2,), jnp.int32),
            jax.ShapeDtypeStruct((BLOCKS, SHARD, wide), BF16),
        ),
        in_specs=[vmem] * 2,
        out_specs=(vmem, vmem, vmem, smem, vmem),
        scratch_shapes=[
            pltpu.VMEM((BLOCKS, SHARD, QUAD * rows), F32),
            pltpu.VMEM((QUAD, 8, rows), F32),
            pltpu.VMEM((QUAD, 8, rows), F32),
            pltpu.VMEM(slabs_shape, F32),
            pltpu.VMEM((BLOCKS, SHARD, wide), F32),
        ],
        name="forward",
    )(qg, slabs)
    stats = exchange(stats.reshape(QUAD * 4 * QUAD, rows), "dp", NEAR)
    stats = stats.reshape(QUAD, 4 * QUAD, rows)
    *oqs, dkv = call(
        backward_kernel,
        out_shape=(
            *[jax.ShapeDtypeStruct((rows, wide), BF16)] * QUAD,
            jax.ShapeDtypeStruct(slabs_shape, BF16),
        ),
        in_specs=[smem] + [vmem] * 5,
        out_specs=(vmem,) * 5,
        scratch_shapes=[
            pltpu.VMEM((QUAD, HEAD, rows), F32),
            pltpu.VMEM((BLOCKS, SHARD, wide), F32),
            pltpu.VMEM(slabs_shape, F32),
        ],
        name="backward",
    )(active, qg, kv, e, o, stats)

    oqs = [oqs[0]] + [rotate(oqs[turn], -turn) for turn in range(1, QUAD)]
    dkv = exchange(dkv.reshape(flat), ("head", "srv"))
    dkv, oqs = lax.optimization_barrier((dkv, oqs))
    dkv = call(
        fold_kernel,
        out_shape=jax.ShapeDtypeStruct((QUAD, part, wide), BF16),
        in_specs=[vmem],
        out_specs=vmem,
        scratch_shapes=[
            pltpu.VMEM((GROUPS, BLOCKS * PIECE, wide), F32),
            pltpu.VMEM((BLOCKS, part, wide), F32),
        ],
        name="fold",
    )(dkv.reshape(slabs_shape))
    dkv = exchange(dkv, "dp", FAR)
    k_grad, v_grad = call(
        finish_kernel,
        out_shape=(jax.ShapeDtypeStruct((PIECE, GROUPS * HEAD), BF16),) * 2,
        in_specs=[vmem],
        out_specs=(vmem, vmem),
        scratch_shapes=[pltpu.VMEM((part, wide), F32)],
        name="finish",
    )(dkv)

    oq = sum(x.astype(F32) for x in oqs).astype(BF16)
    attention = oq[:, :HEAD].reshape(queries.shape)
    q_grad = oq[:, HEAD:].reshape(queries.shape)
    return attention, q_grad, k_grad, v_grad


def solution(mesh):
    placed = (
        P("dp", "srv", "head"),
        P(("dp", "head"), None),
        P(("dp", "head"), None),
        P("dp", "srv", "head"),
        P("dp"),
    )
    return jax.shard_map(
        local,
        mesh=mesh,
        in_specs=placed,
        out_specs=(
            P("dp", "srv", "head"),
            P("dp", "srv", "head"),
            P(("dp", "head", "srv"), None),
            P(("dp", "head", "srv"), None),
        ),
        check_vma=False,
    )
```

time: 132 us -> 132 us (level)
  the two profiles are of different devices: /device:TPU:1 before, /device:TPU:38 now
where the time goes in v3:
time: 132 us; the launch traced here: 131 us
  blocking collectives  53.8 us (41%)
  waiting for transfers between devices  30 us (23%)
  starting transfers between devices  26.9 us (20%)
  Pallas kernels  18.6 us (14%)
    all_gather x1, blocking collectives, local(): gathered = lax.all_gather(packed, 'dp', axis=0, axis_index_groups=FAR)  28.7 us
    all_to_all x3, waiting for transfers between devices, exchange(): lax.all_to_all(block, axis, 0, 0, tiled=True, axis_index_groups=groups)  24.1 us
    all_to_all x3, starting transfers between devices, exchange(): lax.all_to_all(block, axis, 0, 0, tiled=True, axis_index_groups=groups)  18.6 us
    all_gather x1, blocking collectives, local(): qg = lax.all_gather(qg, 'dp', axis=0, axis_index_groups=NEAR)  16 us
    all_to_all x1, blocking collectives, exchange(): lax.all_to_all(block, axis, 0, 0, tiled=True, axis_index_groups=groups)  9.16 us
    ppermute x3, starting transfers between devices, rotate(): return lax.ppermute(block, 'dp', pairs)  8.31 us
    pallas_call x1, Pallas kernels, local(): call(backward_kernel, out_shape=(*[jax.ShapeDtypeStruct((rows, wide), BF1...  7.16 us
    ppermute x3, waiting for transfers between devices, rotate(): return lax.ppermute(block, 'dp', pairs)  5.9 us
  transfers between devices with their start and end apart: 6, of which 4 were waited for; matrix products, arithmetic and copies ran while one was open for 1% of the time, Pallas kernels for 0%

profile of v3, /device:TPU:38, one launch (start us, length us, event | category | flops | bytes accessed | tf_op | source)
XLA Modules:
  0.0 130.9 jit_solution(1136524316993308878)
XLA Ops:
  0.6 1.8 %pack.1 = bf16[168,256]{1,0:T(8,128)(2,1)} custom-call(s32[5,128]{1,0:T(8,128)} %bitcast.21, bf16[80,1024]{1,0:T(8,128)(2,1)} %keys_in.1, bf16[80,1024]{1,0:T(8,128)(2,1)} %values_in.1), custom_call_target="tpu_custom_call" | custom-call | tf_op jit(solution)/shard_map/pack/pallas_call | solution.py:309
  2.4 28.7 %all-gather = bf16[672,256]{1,0:T(8,128)(2,1)} all-gather(bf16[168,256]{1,0:T(8,128)(2,1)} %pack.1), channel_id=2, replica_groups={{0,128,256,384},{32,160,288,416},{64,192,320,448},{96,224,352,480},{1,1..., dimensions={0}, use_global_device_ids=true | all-gather | bytes 430080 | tf_op jit(solution)/shard_map/all_gather | solution.py:324
  31.1 2.9 %fan.1 = (bf16[8,4,60,256]{3,2,1,0:T(8,128)(2,1)}, bf16[264,256]{1,0:T(8,128)(2,1)}) custom-call(bf16[4,168,256]{2,1,0:T(8,128)(2,1)} %bitcast.15, bf16[256,128]{1,0:T(8,128)(2,1)} %bitcast.19, bf16[256,128]{1,0:T(8,128)(2,1)} %bitcast.20), custom_call_target="tpu_custom_call" | custom-call | tf_op jit(solution)/shard_map/fan/pallas_call | solution.py:325
  34.0 7.6 %all-to-all-start = ((bf16[32,60,256]{2,1,0:T(8,128)(2,1)}), bf16[32,60,256]{2,1,0:T(8,128)(2,1)S(1)}, u32[]{:S(2)}, u32[]{:S(2)}) async-start(bf16[32,60,256]{2,1,0:T(8,128)(2,1)} %bitcast.16), calls=%async_computation | async-start | bytes 2097152 | tf_op jit(solution)/shard_map/all_to_all | solution.py:288
  41.6 16.0 %all-gather.1 = bf16[1056,256]{1,0:T(8,128)(2,1)S(1)} all-gather(bf16[264,256]{1,0:T(8,128)(2,1)} %get-tuple-element.23), channel_id=3, replica_groups={{0,32,64,96},{128,160,192,224},{256,288,320,352},{384,416,448,480},{1,3..., dimensions={0}, use_global_device_ids=true | all-gather | bytes 675840 | tf_op jit(solution)/shard_map/all_gather | solution.py:343
  57.6 0.0 all-to-all-done
  57.6 5.2 %forward.1 = (bf16[3,640,1024]{2,1,0:T(8,128)(2,1)S(1)}, f32[4,128,256]{2,1,0:T(8,128)S(1)}, f32[4,16,256]{2,1,0:T(8,128)S(1)}, s32[2]{0:T(128)S(1)}, bf16[3,640,256]{2,1,0:T(8,128)(2,1)S(1)}) custom-call(bf16[4,264,256]{2,1,0:T(8,128)(2,1)S(1)} %bitcast.11, bf16[8,4,60,256]{3,2,1,0:T(8,128)(2,1)S(1)} %bitcast.14), custom_call_target="tpu_custom_call" | custom-call | tf_op jit(solution)/shard_map/forward/pallas_call | solution.py:345
  62.8 9.2 %all_to_all.21.stats = f32[4,16,256]{2,1,0:T(8,128)S(1)} all-to-all(f32[4,16,256]{2,1,0:T(8,128)S(1)} %get-tuple-element.29), channel_id=1, replica_groups={{0,32,64,96},{128,160,192,224},{256,288,320,352},{384,416,448,480},{1,3..., dimensions={0} | all-to-all | bytes 131072 | tf_op jit(solution)/shard_map/all_to_all | solution.py:288
  72.0 7.2 %backward.1 = (bf16[256,256]{1,0:T(8,128)(2,1)S(1)}, bf16[256,256]{1,0:T(8,128)(2,1)S(1)}, bf16[256,256]{1,0:T(8,128)(2,1)S(1)}, bf16[256,256]{1,0:T(8,128)(2,1)S(1)}, bf16[8,4,60,256]{3,2,1,0:T(8,128)(2,1)}) custom-call(s32[2]{0:T(128)S(1)} %get-tuple-element.25.active, bf16[4,264,256]{2,1,0:T(8,128)(2,1)S(1)} %bitcast.12, ...), custom_call_target="tpu_custom_call" | custom-call | tf_op jit(solution)/shard_map/backward/pallas_call | solution.py:367
  79.1 7.5 %all-to-all-start.2 = ((bf16[32,60,256]{2,1,0:T(8,128)(2,1)}), bf16[32,60,256]{2,1,0:T(8,128)(2,1)S(1)}, u32[]{:S(2)}, u32[]{:S(2)}) async-start(bf16[32,60,256]{2,1,0:T(8,128)(2,1)} %bitcast.7), calls=%async_computation.2 | async-start | bytes 2097152 | tf_op jit(solution)/shard_map/all_to_all | solution.py:288
  86.7 3.0 %collective-permute-start = (bf16[256,256]{1,0:T(8,128)(2,1)S(1)}, bf16[256,256]{1,0:T(8,128)(2,1)S(1)}, u32[]{:S(2)}, u32[]{:S(2)}) collective-permute-start(bf16[256,256]{1,0:T(8,128)(2,1)S(1)} %get-tuple-element.32), channel_id=1, source_target_pairs={{0,96},{32,0},{64,32},{96,64},{128,224},{160,128},{192,160},{224,1... | collective-permute-start | bytes 393224 | tf_op jit(solution)/shard_map/ppermute | solution.py:293
  89.7 1.9 %collective-permute-start.1 = (bf16[256,256]{1,0:T(8,128)(2,1)S(1)}, bf16[256,256]{1,0:T(8,128)(2,1)S(1)}, u32[]{:S(2)}, u32[]{:S(2)}) collective-permute-start(bf16[256,256]{1,0:T(8,128)(2,1)S(1)} %get-tuple-element.33), channel_id=1, source_target_pairs={{0,64},{32,96},{64,0},{96,32},{128,192},{160,224},{192,128},{224,1... | collective-permute-start | bytes 393224 | tf_op jit(solution)/shard_map/ppermute | solution.py:293
  91.7 3.4 %collective-permute-start.2 = (bf16[256,256]{1,0:T(8,128)(2,1)S(1)}, bf16[256,256]{1,0:T(8,128)(2,1)S(1)}, u32[]{:S(2)}, u32[]{:S(2)}) collective-permute-start(bf16[256,256]{1,0:T(8,128)(2,1)S(1)} %get-tuple-element.34), channel_id=1, source_target_pairs={{0,32},{32,64},{64,96},{96,0},{128,160},{160,192},{192,224},{224,1... | collective-permute-start | bytes 393224 | tf_op jit(solution)/shard_map/ppermute | solution.py:293
  95.0 0.0 collective-permute-done
  95.0 3.3 %collective-permute-done.1 = bf16[256,256]{1,0:T(8,128)(2,1)S(1)} collective-permute-done((bf16[256,256]{1,0:T(8,128)(2,1)S(1)}, bf16[256,256]{1,0:T(8,128)(2,1)S(1)}, u32[]{:S(2)}, u32[]{:S(2)}) %collective-permute-start.1) | collective-permute-done | bytes 131104 | tf_op jit(solution)/shard_map/ppermute | solution.py:293
  98.3 2.6 %collective-permute-done.2 = bf16[256,256]{1,0:T(8,128)(2,1)S(1)} collective-permute-done((bf16[256,256]{1,0:T(8,128)(2,1)S(1)}, bf16[256,256]{1,0:T(8,128)(2,1)S(1)}, u32[]{:S(2)}, u32[]{:S(2)}) %collective-permute-start.2) | collective-permute-done | bytes 131104 | tf_op jit(solution)/shard_map/ppermute | solution.py:293
  100.9 0.8 all-to-all-done.2
  101.8 0.9 fold.1
  102.7 3.5 %all-to-all-start.3 = ((bf16[4,160,256]{2,1,0:T(8,128)(2,1)}), bf16[4,160,256]{2,1,0:T(8,128)(2,1)S(1)}, u32[]{:S(2)}, u32[]{:S(2)}) async-start(bf16[4,160,256]{2,1,0:T(8,128)(2,1)} %fold.1), calls=%async_computation.3 | async-start | bytes 655360 | tf_op jit(solution)/shard_map/all_to_all | solution.py:288
  106.1 0.1 add_convert_fusion
  106.2 0.7 fusion
  106.9 23.3 %all-to-all-done.3.parts = bf16[4,160,256]{2,1,0:T(8,128)(2,1)S(1)} async-done(((bf16[4,160,256]{2,1,0:T(8,128)(2,1)}), bf16[4,160,256]{2,1,0:T(8,128)(2,1)S(1)}, u32[]{:S(2)}, u32[]{:S(2)}) %all-to-all-start.3) | async-done | bytes 327712 | tf_op jit(solution)/shard_map/all_to_all | solution.py:288
  130.2 0.7 finish.1
Async XLA Ops:
  34.0 23.6 %all-to-all-start = ((bf16[32,60,256]{2,1,0:T(8,128)(2,1)}), bf16[32,60,256]{2,1,0:T(8,128)(2,1)S(1)}, u32[]{:S(2)}, u32[]{:S(2)}) async-start(bf16[32,60,256]{2,1,0:T(8,128)(2,1)} %bitcast.16), calls=%async_computation | async-start | bytes 2097152 | tf_op jit(solution)/shard_map/all_to_all | solution.py:288
  79.1 22.6 %all-to-all-start.2 = ((bf16[32,60,256]{2,1,0:T(8,128)(2,1)}), bf16[32,60,256]{2,1,0:T(8,128)(2,1)S(1)}, u32[]{:S(2)}, u32[]{:S(2)}) async-start(bf16[32,60,256]{2,1,0:T(8,128)(2,1)} %bitcast.7), calls=%async_computation.2 | async-start | bytes 2097152 | tf_op jit(solution)/shard_map/all_to_all | solution.py:288
  86.7 8.3 %collective-permute-start = (bf16[256,256]{1,0:T(8,128)(2,1)S(1)}, bf16[256,256]{1,0:T(8,128)(2,1)S(1)}, u32[]{:S(2)}, u32[]{:S(2)}) collective-permute-start(bf16[256,256]{1,0:T(8,128)(2,1)S(1)} %get-tuple-element.32), channel_id=1, source_target_pairs={{0,96},{32,0},{64,32},{96,64},{128,224},{160,128},{192,160},{224,1... | collective-permute-start | bytes 393224 | tf_op jit(solution)/shard_map/ppermute | solution.py:293
  89.7 8.6 %collective-permute-start.1 = (bf16[256,256]{1,0:T(8,128)(2,1)S(1)}, bf16[256,256]{1,0:T(8,128)(2,1)S(1)}, u32[]{:S(2)}, u32[]{:S(2)}) collective-permute-start(bf16[256,256]{1,0:T(8,128)(2,1)S(1)} %get-tuple-element.33), channel_id=1, source_target_pairs={{0,64},{32,96},{64,0},{96,32},{128,192},{160,224},{192,128},{224,1... | collective-permute-start | bytes 393224 | tf_op jit(solution)/shard_map/ppermute | solution.py:293
  91.7 9.3 %collective-permute-start.2 = (bf16[256,256]{1,0:T(8,128)(2,1)S(1)}, bf16[256,256]{1,0:T(8,128)(2,1)S(1)}, u32[]{:S(2)}, u32[]{:S(2)}) collective-permute-start(bf16[256,256]{1,0:T(8,128)(2,1)S(1)} %get-tuple-element.34), channel_id=1, source_target_pairs={{0,32},{32,64},{64,96},{96,0},{128,160},{160,192},{192,224},{224,1... | collective-permute-start | bytes 393224 | tf_op jit(solution)/shard_map/ppermute | solution.py:293
  102.7 27.5 %all-to-all-start.3 = ((bf16[4,160,256]{2,1,0:T(8,128)(2,1)}), bf16[4,160,256]{2,1,0:T(8,128)(2,1)S(1)}, u32[]{:S(2)}, u32[]{:S(2)}) async-start(bf16[4,160,256]{2,1,0:T(8,128)(2,1)} %fold.1), calls=%async_computation.3 | async-start | bytes 655360 | tf_op jit(solution)/shard_map/all_to_all | solution.py:288

commit v4 on v3

--- a/solution.py
+++ b/solution.py
@@ -113,20 +113,25 @@
         copy.wait()
 
 
-def fold_kernel(parts, out_ref, slab_ref, f_ref):
+def fold_kernel(parts, own_ref, next_ref, far_ref, last_ref, slab_ref, f_ref):
+    quad = lax.axis_index("dp") // QUAD
     for group in range(GROUPS):
         slab_ref[group] = sum(parts[group, srv].astype(F32) for srv in range(SRVS))
         for block in range(BLOCKS):
             f_ref[block, PIECE * group : PIECE * (group + 1), :] = slab_ref[
                 group, PIECE * block : PIECE * (block + 1), :
             ]
-    out_ref[0] = jnp.zeros(out_ref.shape[1:], BF16)
-    for block in range(BLOCKS):
-        out_ref[block + 1] = f_ref[block].astype(BF16)
-
-
-def finish_kernel(parts, k_ref, v_ref, f_ref):
-    f_ref[...] = sum(parts[quad].astype(F32) for quad in range(QUAD))
+    for turn, ref in enumerate((own_ref, next_ref, far_ref, last_ref)):
+        owner = lax.rem(quad + turn, QUAD)
+        ref[...] = f_ref[jnp.maximum(owner - 1, 0)].astype(BF16)
+
+    @pl.when(quad == 0)
+    def _():
+        own_ref[...] = jnp.zeros(own_ref.shape, BF16)
+
+
+def finish_kernel(p0, p1, p2, p3, k_ref, v_ref, f_ref):
+    f_ref[...] = sum(part[...].astype(F32) for part in (p0, p1, p2, p3))
     for group in range(GROUPS):
         span = slice(PIECE * group, PIECE * (group + 1))
         columns = slice(HEAD * group, HEAD * (group + 1))
@@ -290,6 +295,16 @@
 
 def rotate(block, turn):
     pairs = [(q[i], q[(i + turn) % QUAD]) for q in NEAR for i in range(QUAD)]
+    return lax.ppermute(block, "dp", pairs)
+
+
+def carry_on(block, turn):
+    pairs = [
+        (QUAD * quad + m, QUAD * ((quad + turn) % QUAD) + m)
+        for quad in range(QUAD)
+        for m in range(QUAD)
+        if (quad + turn) % QUAD
+    ]
     return lax.ppermute(block, "dp", pairs)
 
 
@@ -385,24 +400,24 @@
     dkv, oqs = lax.optimization_barrier((dkv, oqs))
     dkv = call(
         fold_kernel,
-        out_shape=jax.ShapeDtypeStruct((QUAD, part, wide), BF16),
+        out_shape=(jax.ShapeDtypeStruct((part, wide), BF16),) * QUAD,
         in_specs=[vmem],
-        out_specs=vmem,
+        out_specs=(vmem,) * QUAD,
         scratch_shapes=[
             pltpu.VMEM((GROUPS, BLOCKS * PIECE, wide), F32),
             pltpu.VMEM((BLOCKS, part, wide), F32),
         ],
         name="fold",
     )(dkv.reshape(slabs_shape))
-    dkv = exchange(dkv, "dp", FAR)
+    dkv = [dkv[0]] + [carry_on(dkv[turn], turn) for turn in range(1, QUAD)]
     k_grad, v_grad = call(
         finish_kernel,
         out_shape=(jax.ShapeDtypeStruct((PIECE, GROUPS * HEAD), BF16),) * 2,
-        in_specs=[vmem],
+        in_specs=[vmem] * QUAD,
         out_specs=(vmem, vmem),
         scratch_shapes=[pltpu.VMEM((part, wide), F32)],
         name="finish",
-    )(dkv)
+    )(*dkv)
 
     oq = sum(x.astype(F32) for x in oqs).astype(BF16)
     attention = oq[:, :HEAD].reshape(queries.shape)

time: 132 us -> 127 us (0.962)
  the two profiles are of different devices: /device:TPU:38 before, /device:TPU:1 now
where the time goes in v4:
time: 127 us
  blocking collectives  48.1 us (38%)
  starting transfers between devices  46.2 us (36%)
  waiting for transfers between devices  18.9 us (15%)
  Pallas kernels  12 us (9%)
    all_gather x1, blocking collectives, local(): gathered = lax.all_gather(packed, 'dp', axis=0, axis_index_groups=FAR)  27.5 us
    all_to_all x2, starting transfers between devices, exchange(): lax.all_to_all(block, axis, 0, 0, tiled=True, axis_index_groups=groups)  20.5 us
    ppermute x3, starting transfers between devices, carry_on(): return lax.ppermute(block, 'dp', pairs)  18.1 us
    all_gather x1, blocking collectives, local(): qg = lax.all_gather(qg, 'dp', axis=0, axis_index_groups=NEAR)  13.3 us
    ppermute x3, waiting for transfers between devices, rotate(): return lax.ppermute(block, 'dp', pairs)  7.91 us
    ppermute x3, starting transfers between devices, rotate(): return lax.ppermute(block, 'dp', pairs)  7.55 us
    all_to_all x1, blocking collectives, exchange(): lax.all_to_all(block, axis, 0, 0, tiled=True, axis_index_groups=groups)  7.31 us
    ppermute x3, waiting for transfers between devices, carry_on(): return lax.ppermute(block, 'dp', pairs)  7.16 us
  transfers between devices with their start and end apart: 8, of which 4 were waited for; matrix products, arithmetic and copies ran while one was open for 1% of the time, Pallas kernels for 0%

profile of v4, /device:TPU:1, one launch (start us, length us, event | category | flops | bytes accessed | tf_op | source)
XLA Modules:
  0.0 126.7 jit_solution(9538918726880069604)
XLA Ops:
  0.6 1.8 %pack.1 = bf16[168,256]{1,0:T(8,128)(2,1)} custom-call(s32[5,128]{1,0:T(8,128)} %bitcast.21, bf16[80,1024]{1,0:T(8,128)(2,1)} %keys_in.1, bf16[80,1024]{1,0:T(8,128)(2,1)} %values_in.1), custom_call_target="tpu_custom_call" | custom-call | tf_op jit(solution)/shard_map/pack/pallas_call | solution.py:324
  2.4 27.5 %all-gather = bf16[672,256]{1,0:T(8,128)(2,1)} all-gather(bf16[168,256]{1,0:T(8,128)(2,1)} %pack.1), channel_id=2, replica_groups={{0,128,256,384},{32,160,288,416},{64,192,320,448},{96,224,352,480},{1,1..., dimensions={0}, use_global_device_ids=true | all-gather | bytes 430080 | tf_op jit(solution)/shard_map/all_gather | solution.py:339
  29.9 2.9 %fan.1 = (bf16[8,4,60,256]{3,2,1,0:T(8,128)(2,1)}, bf16[264,256]{1,0:T(8,128)(2,1)}) custom-call(bf16[4,168,256]{2,1,0:T(8,128)(2,1)} %bitcast.15, bf16[256,128]{1,0:T(8,128)(2,1)} %bitcast.19, bf16[256,128]{1,0:T(8,128)(2,1)} %bitcast.20), custom_call_target="tpu_custom_call" | custom-call | tf_op jit(solution)/shard_map/fan/pallas_call | solution.py:340
  32.8 11.8 %all-to-all-start = ((bf16[32,60,256]{2,1,0:T(8,128)(2,1)}), bf16[32,60,256]{2,1,0:T(8,128)(2,1)S(1)}, u32[]{:S(2)}, u32[]{:S(2)}) async-start(bf16[32,60,256]{2,1,0:T(8,128)(2,1)} %bitcast.16), calls=%async_computation | async-start | bytes 2097152 | tf_op jit(solution)/shard_map/all_to_all | solution.py:293
  44.7 13.3 %all-gather.1 = bf16[1056,256]{1,0:T(8,128)(2,1)S(1)} all-gather(bf16[264,256]{1,0:T(8,128)(2,1)} %get-tuple-element.27), channel_id=3, replica_groups={{0,32,64,96},{128,160,192,224},{256,288,320,352},{384,416,448,480},{1,3..., dimensions={0}, use_global_device_ids=true | all-gather | bytes 675840 | tf_op jit(solution)/shard_map/all_gather | solution.py:358
  58.0 3.0 %all-to-all-done = bf16[32,60,256]{2,1,0:T(8,128)(2,1)S(1)} async-done(((bf16[32,60,256]{2,1,0:T(8,128)(2,1)}), bf16[32,60,256]{2,1,0:T(8,128)(2,1)S(1)}, u32[]{:S(2)}, u32[]{:S(2)}) %all-to-all-start) | async-done | bytes 983072 | tf_op jit(solution)/shard_map/all_to_all | solution.py:293
  61.0 2.5 %forward.1 = (bf16[3,640,1024]{2,1,0:T(8,128)(2,1)S(1)}, f32[4,128,256]{2,1,0:T(8,128)S(1)}, f32[4,16,256]{2,1,0:T(8,128)S(1)}, s32[2]{0:T(128)S(1)}, bf16[3,640,256]{2,1,0:T(8,128)(2,1)S(1)}) custom-call(bf16[4,264,256]{2,1,0:T(8,128)(2,1)S(1)} %bitcast.11, bf16[8,4,60,256]{3,2,1,0:T(8,128)(2,1)S(1)} %bitcast.14), custom_call_target="tpu_custom_call" | custom-call | tf_op jit(solution)/shard_map/forward/pallas_call | solution.py:360
  63.5 7.3 %all_to_all.16.stats = f32[4,16,256]{2,1,0:T(8,128)S(1)} all-to-all(f32[4,16,256]{2,1,0:T(8,128)S(1)} %get-tuple-element.33), channel_id=1, replica_groups={{0,32,64,96},{128,160,192,224},{256,288,320,352},{384,416,448,480},{1,3..., dimensions={0} | all-to-all | bytes 131072 | tf_op jit(solution)/shard_map/all_to_all | solution.py:293
  70.8 3.9 %backward.1 = (bf16[256,256]{1,0:T(8,128)(2,1)S(1)}, bf16[256,256]{1,0:T(8,128)(2,1)S(1)}, bf16[256,256]{1,0:T(8,128)(2,1)S(1)}, bf16[256,256]{1,0:T(8,128)(2,1)S(1)}, bf16[8,4,60,256]{3,2,1,0:T(8,128)(2,1)}) custom-call(s32[2]{0:T(128)S(1)} %get-tuple-element.29.active, bf16[4,264,256]{2,1,0:T(8,128)(2,1)S(1)} %bitcast.12, ...), custom_call_target="tpu_custom_call" | custom-call | tf_op jit(solution)/shard_map/backward/pallas_call | solution.py:382
  74.7 8.7 %all-to-all-start.2 = ((bf16[32,60,256]{2,1,0:T(8,128)(2,1)}), bf16[32,60,256]{2,1,0:T(8,128)(2,1)S(1)}, u32[]{:S(2)}, u32[]{:S(2)}) async-start(bf16[32,60,256]{2,1,0:T(8,128)(2,1)} %bitcast.7), calls=%async_computation.2 | async-start | bytes 2097152 | tf_op jit(solution)/shard_map/all_to_all | solution.py:293
  83.4 2.4 %collective-permute-start = (bf16[256,256]{1,0:T(8,128)(2,1)S(1)}, bf16[256,256]{1,0:T(8,128)(2,1)S(1)}, u32[]{:S(2)}, u32[]{:S(2)}) collective-permute-start(bf16[256,256]{1,0:T(8,128)(2,1)S(1)} %get-tuple-element.36), channel_id=1, source_target_pairs={{0,96},{32,0},{64,32},{96,64},{128,224},{160,128},{192,160},{224,1... | collective-permute-start | bytes 393224 | tf_op jit(solution)/shard_map/ppermute | solution.py:298
  85.8 3.3 %collective-permute-start.1 = (bf16[256,256]{1,0:T(8,128)(2,1)S(1)}, bf16[256,256]{1,0:T(8,128)(2,1)S(1)}, u32[]{:S(2)}, u32[]{:S(2)}) collective-permute-start(bf16[256,256]{1,0:T(8,128)(2,1)S(1)} %get-tuple-element.37), channel_id=1, source_target_pairs={{0,64},{32,96},{64,0},{96,32},{128,192},{160,224},{192,128},{224,1... | collective-permute-start | bytes 393224 | tf_op jit(solution)/shard_map/ppermute | solution.py:298
  89.1 1.9 %collective-permute-start.2 = (bf16[256,256]{1,0:T(8,128)(2,1)S(1)}, bf16[256,256]{1,0:T(8,128)(2,1)S(1)}, u32[]{:S(2)}, u32[]{:S(2)}) collective-permute-start(bf16[256,256]{1,0:T(8,128)(2,1)S(1)} %get-tuple-element.38), channel_id=1, source_target_pairs={{0,32},{32,64},{64,96},{96,0},{128,160},{160,192},{192,224},{224,1... | collective-permute-start | bytes 393224 | tf_op jit(solution)/shard_map/ppermute | solution.py:298
  91.0 0.0 collective-permute-done
  91.0 7.9 %collective-permute-done.1 = bf16[256,256]{1,0:T(8,128)(2,1)S(1)} collective-permute-done((bf16[256,256]{1,0:T(8,128)(2,1)S(1)}, bf16[256,256]{1,0:T(8,128)(2,1)S(1)}, u32[]{:S(2)}, u32[]{:S(2)}) %collective-permute-start.1) | collective-permute-done | bytes 131104 | tf_op jit(solution)/shard_map/ppermute | solution.py:298
  98.9 0.8 all-to-all-done.2
  99.8 0.2 fold.1
  100.0 3.2 %collective-permute-start.3 = (bf16[160,256]{1,0:T(8,128)(2,1)S(1)}, bf16[160,256]{1,0:T(8,128)(2,1)S(1)}, u32[]{:S(2)}, u32[]{:S(2)}) collective-permute-start(bf16[160,256]{1,0:T(8,128)(2,1)S(1)} %get-tuple-element.45), channel_id=1, source_target_pairs={{0,128},{32,160},{64,192},{96,224},{128,256},{160,288},{192,320},{... | collective-permute-start | bytes 245768 | tf_op jit(solution)/shard_map/ppermute | solution.py:308
  103.1 9.5 %collective-permute-start.4 = (bf16[160,256]{1,0:T(8,128)(2,1)S(1)}, bf16[160,256]{1,0:T(8,128)(2,1)S(1)}, u32[]{:S(2)}, u32[]{:S(2)}) collective-permute-start(bf16[160,256]{1,0:T(8,128)(2,1)S(1)} %get-tuple-element.46), channel_id=1, source_target_pairs={{0,256},{32,288},{64,320},{96,352},{128,384},{160,416},{192,448},{... | collective-permute-start | bytes 245768 | tf_op jit(solution)/shard_map/ppermute | solution.py:308
  112.7 5.4 %collective-permute-start.5 = (bf16[160,256]{1,0:T(8,128)(2,1)S(1)}, bf16[160,256]{1,0:T(8,128)(2,1)S(1)}, u32[]{:S(2)}, u32[]{:S(2)}) collective-permute-start(bf16[160,256]{1,0:T(8,128)(2,1)S(1)} %get-tuple-element.47), channel_id=1, source_target_pairs={{0,384},{32,416},{64,448},{96,480},{256,128},{288,160},{320,192},{... | collective-permute-start | bytes 245768 | tf_op jit(solution)/shard_map/ppermute | solution.py:308
  118.1 0.1 add_convert_fusion
  118.2 0.7 fusion
  118.9 7.2 %collective-permute-done.5.p3 = bf16[160,256]{1,0:T(8,128)(2,1)S(1)} collective-permute-done((bf16[160,256]{1,0:T(8,128)(2,1)S(1)}, bf16[160,256]{1,0:T(8,128)(2,1)S(1)}, u32[]{:S(2)}, u32[]{:S(2)}) %collective-permute-start.5) | collective-permute-done | bytes 81952 | tf_op jit(solution)/shard_map/ppermute | solution.py:308
  126.0 0.7 finish.1
  (3 shorter events, 0.0 us)
Async XLA Ops:
  32.8 28.2 %all-to-all-start = ((bf16[32,60,256]{2,1,0:T(8,128)(2,1)}), bf16[32,60,256]{2,1,0:T(8,128)(2,1)S(1)}, u32[]{:S(2)}, u32[]{:S(2)}) async-start(bf16[32,60,256]{2,1,0:T(8,128)(2,1)} %bitcast.16), calls=%async_computation | async-start | bytes 2097152 | tf_op jit(solution)/shard_map/all_to_all | solution.py:293
  74.7 25.0 %all-to-all-start.2 = ((bf16[32,60,256]{2,1,0:T(8,128)(2,1)}), bf16[32,60,256]{2,1,0:T(8,128)(2,1)S(1)}, u32[]{:S(2)}, u32[]{:S(2)}) async-start(bf16[32,60,256]{2,1,0:T(8,128)(2,1)} %bitcast.7), calls=%async_computation.2 | async-start | bytes 2097152 | tf_op jit(solution)/shard_map/all_to_all | solution.py:293
  83.4 7.6 %collective-permute-start = (bf16[256,256]{1,0:T(8,128)(2,1)S(1)}, bf16[256,256]{1,0:T(8,128)(2,1)S(1)}, u32[]{:S(2)}, u32[]{:S(2)}) collective-permute-start(bf16[256,256]{1,0:T(8,128)(2,1)S(1)} %get-tuple-element.36), channel_id=1, source_target_pairs={{0,96},{32,0},{64,32},{96,64},{128,224},{160,128},{192,160},{224,1... | collective-permute-start | bytes 393224 | tf_op jit(solution)/shard_map/ppermute | solution.py:298
  85.8 13.1 %collective-permute-start.1 = (bf16[256,256]{1,0:T(8,128)(2,1)S(1)}, bf16[256,256]{1,0:T(8,128)(2,1)S(1)}, u32[]{:S(2)}, u32[]{:S(2)}) collective-permute-start(bf16[256,256]{1,0:T(8,128)(2,1)S(1)} %get-tuple-element.37), channel_id=1, source_target_pairs={{0,64},{32,96},{64,0},{96,32},{128,192},{160,224},{192,128},{224,1... | collective-permute-start | bytes 393224 | tf_op jit(solution)/shard_map/ppermute | solution.py:298
  89.1 9.8 %collective-permute-start.2 = (bf16[256,256]{1,0:T(8,128)(2,1)S(1)}, bf16[256,256]{1,0:T(8,128)(2,1)S(1)}, u32[]{:S(2)}, u32[]{:S(2)}) collective-permute-start(bf16[256,256]{1,0:T(8,128)(2,1)S(1)} %get-tuple-element.38), channel_id=1, source_target_pairs={{0,32},{32,64},{64,96},{96,0},{128,160},{160,192},{192,224},{224,1... | collective-permute-start | bytes 393224 | tf_op jit(solution)/shard_map/ppermute | solution.py:298
  100.0 18.9 %collective-permute-start.3 = (bf16[160,256]{1,0:T(8,128)(2,1)S(1)}, bf16[160,256]{1,0:T(8,128)(2,1)S(1)}, u32[]{:S(2)}, u32[]{:S(2)}) collective-permute-start(bf16[160,256]{1,0:T(8,128)(2,1)S(1)} %get-tuple-element.45), channel_id=1, source_target_pairs={{0,128},{32,160},{64,192},{96,224},{128,256},{160,288},{192,320},{... | collective-permute-start | bytes 245768 | tf_op jit(solution)/shard_map/ppermute | solution.py:308
  103.1 15.7 %collective-permute-start.4 = (bf16[160,256]{1,0:T(8,128)(2,1)S(1)}, bf16[160,256]{1,0:T(8,128)(2,1)S(1)}, u32[]{:S(2)}, u32[]{:S(2)}) collective-permute-start(bf16[160,256]{1,0:T(8,128)(2,1)S(1)} %get-tuple-element.46), channel_id=1, source_target_pairs={{0,256},{32,288},{64,320},{96,352},{128,384},{160,416},{192,448},{... | collective-permute-start | bytes 245768 | tf_op jit(solution)/shard_map/ppermute | solution.py:308
  112.7 13.4 %collective-permute-start.5 = (bf16[160,256]{1,0:T(8,128)(2,1)S(1)}, bf16[160,256]{1,0:T(8,128)(2,1)S(1)}, u32[]{:S(2)}, u32[]{:S(2)}) collective-permute-start(bf16[160,256]{1,0:T(8,128)(2,1)S(1)} %get-tuple-element.47), channel_id=1, source_target_pairs={{0,384},{32,416},{64,448},{96,480},{256,128},{288,160},{320,192},{... | collective-permute-start | bytes 245768 | tf_op jit(solution)/shard_map/ppermute | solution.py:308

commit v5 on v4

--- a/solution.py
+++ b/solution.py
@@ -13,6 +13,8 @@
 BLOCKS = 3
 SHARD = 640
 CONTEXT = 8192
+ROWS = 512
+DOC_MAX = 5120
 DOCS = 8
 GROUPS = 8
 SRVS = 4
@@ -298,13 +300,18 @@
     return lax.ppermute(block, "dp", pairs)
 
 
+def reached(quad, shard):
+    first = CONTEXT + ROWS * quad
+    return first - (DOC_MAX - 1) < SHARD * (shard + 1) and SHARD * shard < first + ROWS
+
+
 def carry_on(block, turn):
-    pairs = [
-        (QUAD * quad + m, QUAD * ((quad + turn) % QUAD) + m)
-        for quad in range(QUAD)
-        for m in range(QUAD)
-        if (quad + turn) % QUAD
-    ]
+    pairs = []
+    for quad in range(QUAD):
+        owner = (quad + turn) % QUAD
+        for m in range(QUAD):
+            if reached(quad, QUAD * owner + m):
+                pairs.append((QUAD * quad + m, QUAD * owner + m))
     return lax.ppermute(block, "dp", pairs)
 
 
@@ -409,7 +416,7 @@
         ],
         name="fold",
     )(dkv.reshape(slabs_shape))
-    dkv = [dkv[0]] + [carry_on(dkv[turn], turn) for turn in range(1, QUAD)]
+    dkv = [carry_on(dkv[turn], turn) for turn in (2, 1, 3)] + [dkv[0]]
     k_grad, v_grad = call(
         finish_kernel,
         out_shape=(jax.ShapeDtypeStruct((PIECE, GROUPS * HEAD), BF16),) * 2,

time: 127 us -> 118 us (0.929)
  starting transfers between devices: 46.2 us -> 39.9 us
  waiting for transfers between devices: 18.9 us -> 15.6 us
    ppermute x3, starting transfers between devices: 18.1 us -> 10.2 us  [carry_on(): return lax.ppermute(block, 'dp', pairs)]
    ppermute x3, waiting for transfers between devices: 7.16 us -> 4.64 us  [carry_on(): return lax.ppermute(block, 'dp', pairs)]
    ppermute x3, starting transfers between devices: 7.55 us -> 9.18 us  [rotate(): return lax.ppermute(block, 'dp', pairs)]
  transfers between devices with their start and end apart: 8 -> 8, of which waited for: 4 -> 3; matrix products, arithmetic and copies ran while one was open for 1% -> 1% of each run, Pallas kernels for 0% -> 0%
where the time goes in v5:
time: 118 us; the launch traced here: 117 us
  blocking collectives  48.1 us (41%)
  starting transfers between devices  39.9 us (34%)
  waiting for transfers between devices  15.6 us (13%)
  Pallas kernels  12 us (10%)
    all_gather x1, blocking collectives, local(): gathered = lax.all_gather(packed, 'dp', axis=0, axis_index_groups=FAR)  27.5 us
    all_to_all x2, starting transfers between devices, exchange(): lax.all_to_all(block, axis, 0, 0, tiled=True, axis_index_groups=groups)  20.5 us
    all_gather x1, blocking collectives, local(): qg = lax.all_gather(qg, 'dp', axis=0, axis_index_groups=NEAR)  13.3 us
    ppermute x3, starting transfers between devices, carry_on(): return lax.ppermute(block, 'dp', pairs)  10.2 us
    ppermute x3, starting transfers between devices, rotate(): return lax.ppermute(block, 'dp', pairs)  9.18 us
    ppermute x3, waiting for transfers between devices, rotate(): return lax.ppermute(block, 'dp', pairs)  7.95 us
    all_to_all x1, blocking collectives, exchange(): lax.all_to_all(block, axis, 0, 0, tiled=True, axis_index_groups=groups)  7.31 us
    ppermute x3, waiting for transfers between devices, carry_on(): return lax.ppermute(block, 'dp', pairs)  4.64 us
  transfers between devices with their start and end apart: 8, of which 3 were waited for; matrix products, arithmetic and copies ran while one was open for 1% of the time, Pallas kernels for 0%

profile of v5, /device:TPU:1, one launch (start us, length us, event | category | flops | bytes accessed | tf_op | source)
XLA Modules:
  0.0 117.1 jit_solution(12486070198263194363)
XLA Ops:
  0.6 1.8 %pack.1 = bf16[168,256]{1,0:T(8,128)(2,1)} custom-call(s32[5,128]{1,0:T(8,128)} %bitcast.21, bf16[80,1024]{1,0:T(8,128)(2,1)} %keys_in.1, bf16[80,1024]{1,0:T(8,128)(2,1)} %values_in.1), custom_call_target="tpu_custom_call" | custom-call | tf_op jit(solution)/shard_map/pack/pallas_call | solution.py:331
  2.4 27.5 %all-gather = bf16[672,256]{1,0:T(8,128)(2,1)} all-gather(bf16[168,256]{1,0:T(8,128)(2,1)} %pack.1), channel_id=2, replica_groups={{0,128,256,384},{32,160,288,416},{64,192,320,448},{96,224,352,480},{1,1..., dimensions={0}, use_global_device_ids=true | all-gather | bytes 430080 | tf_op jit(solution)/shard_map/all_gather | solution.py:346
  29.9 2.9 %fan.1 = (bf16[8,4,60,256]{3,2,1,0:T(8,128)(2,1)}, bf16[264,256]{1,0:T(8,128)(2,1)}) custom-call(bf16[4,168,256]{2,1,0:T(8,128)(2,1)} %bitcast.15, bf16[256,128]{1,0:T(8,128)(2,1)} %bitcast.19, bf16[256,128]{1,0:T(8,128)(2,1)} %bitcast.20), custom_call_target="tpu_custom_call" | custom-call | tf_op jit(solution)/shard_map/fan/pallas_call | solution.py:347
  32.8 11.8 %all-to-all-start = ((bf16[32,60,256]{2,1,0:T(8,128)(2,1)}), bf16[32,60,256]{2,1,0:T(8,128)(2,1)S(1)}, u32[]{:S(2)}, u32[]{:S(2)}) async-start(bf16[32,60,256]{2,1,0:T(8,128)(2,1)} %bitcast.16), calls=%async_computation | async-start | bytes 2097152 | tf_op jit(solution)/shard_map/all_to_all | solution.py:295
  44.7 13.3 %all-gather.1 = bf16[1056,256]{1,0:T(8,128)(2,1)S(1)} all-gather(bf16[264,256]{1,0:T(8,128)(2,1)} %get-tuple-element.27), channel_id=3, replica_groups={{0,32,64,96},{128,160,192,224},{256,288,320,352},{384,416,448,480},{1,3..., dimensions={0}, use_global_device_ids=true | all-gather | bytes 675840 | tf_op jit(solution)/shard_map/all_gather | solution.py:365
  58.0 3.0 %all-to-all-done = bf16[32,60,256]{2,1,0:T(8,128)(2,1)S(1)} async-done(((bf16[32,60,256]{2,1,0:T(8,128)(2,1)}), bf16[32,60,256]{2,1,0:T(8,128)(2,1)S(1)}, u32[]{:S(2)}, u32[]{:S(2)}) %all-to-all-start) | async-done | bytes 983072 | tf_op jit(solution)/shard_map/all_to_all | solution.py:295
  61.0 2.5 %forward.1 = (bf16[3,640,1024]{2,1,0:T(8,128)(2,1)S(1)}, f32[4,128,256]{2,1,0:T(8,128)S(1)}, f32[4,16,256]{2,1,0:T(8,128)S(1)}, s32[2]{0:T(128)S(1)}, bf16[3,640,256]{2,1,0:T(8,128)(2,1)S(1)}) custom-call(bf16[4,264,256]{2,1,0:T(8,128)(2,1)S(1)} %bitcast.11, bf16[8,4,60,256]{3,2,1,0:T(8,128)(2,1)S(1)} %bitcast.14), custom_call_target="tpu_custom_call" | custom-call | tf_op jit(solution)/shard_map/forward/pallas_call | solution.py:367
  63.5 7.3 %all_to_all.16.stats = f32[4,16,256]{2,1,0:T(8,128)S(1)} all-to-all(f32[4,16,256]{2,1,0:T(8,128)S(1)} %get-tuple-element.33), channel_id=1, replica_groups={{0,32,64,96},{128,160,192,224},{256,288,320,352},{384,416,448,480},{1,3..., dimensions={0} | all-to-all | bytes 131072 | tf_op jit(solution)/shard_map/all_to_all | solution.py:295
  70.8 3.9 %backward.1 = (bf16[256,256]{1,0:T(8,128)(2,1)S(1)}, bf16[256,256]{1,0:T(8,128)(2,1)S(1)}, bf16[256,256]{1,0:T(8,128)(2,1)S(1)}, bf16[256,256]{1,0:T(8,128)(2,1)S(1)}, bf16[8,4,60,256]{3,2,1,0:T(8,128)(2,1)}) custom-call(s32[2]{0:T(128)S(1)} %get-tuple-element.29.active, bf16[4,264,256]{2,1,0:T(8,128)(2,1)S(1)} %bitcast.12, ...), custom_call_target="tpu_custom_call" | custom-call | tf_op jit(solution)/shard_map/backward/pallas_call | solution.py:389
  74.7 8.7 %all-to-all-start.2 = ((bf16[32,60,256]{2,1,0:T(8,128)(2,1)}), bf16[32,60,256]{2,1,0:T(8,128)(2,1)S(1)}, u32[]{:S(2)}, u32[]{:S(2)}) async-start(bf16[32,60,256]{2,1,0:T(8,128)(2,1)} %bitcast.7), calls=%async_computation.2 | async-start | bytes 2097152 | tf_op jit(solution)/shard_map/all_to_all | solution.py:295
  83.4 2.4 %collective-permute-start = (bf16[256,256]{1,0:T(8,128)(2,1)S(1)}, bf16[256,256]{1,0:T(8,128)(2,1)S(1)}, u32[]{:S(2)}, u32[]{:S(2)}) collective-permute-start(bf16[256,256]{1,0:T(8,128)(2,1)S(1)} %get-tuple-element.36), channel_id=1, source_target_pairs={{0,96},{32,0},{64,32},{96,64},{128,224},{160,128},{192,160},{224,1... | collective-permute-start | bytes 393224 | tf_op jit(solution)/shard_map/ppermute | solution.py:300
  85.8 4.9 %collective-permute-start.1 = (bf16[256,256]{1,0:T(8,128)(2,1)S(1)}, bf16[256,256]{1,0:T(8,128)(2,1)S(1)}, u32[]{:S(2)}, u32[]{:S(2)}) collective-permute-start(bf16[256,256]{1,0:T(8,128)(2,1)S(1)} %get-tuple-element.37), channel_id=1, source_target_pairs={{0,64},{32,96},{64,0},{96,32},{128,192},{160,224},{192,128},{224,1... | collective-permute-start | bytes 393224 | tf_op jit(solution)/shard_map/ppermute | solution.py:300
  90.7 1.9 %collective-permute-start.2 = (bf16[256,256]{1,0:T(8,128)(2,1)S(1)}, bf16[256,256]{1,0:T(8,128)(2,1)S(1)}, u32[]{:S(2)}, u32[]{:S(2)}) collective-permute-start(bf16[256,256]{1,0:T(8,128)(2,1)S(1)} %get-tuple-element.38), channel_id=1, source_target_pairs={{0,32},{32,64},{64,96},{96,0},{128,160},{160,192},{192,224},{224,1... | collective-permute-start | bytes 393224 | tf_op jit(solution)/shard_map/ppermute | solution.py:300
  92.7 7.9 %collective-permute-done.1 = bf16[256,256]{1,0:T(8,128)(2,1)S(1)} collective-permute-done((bf16[256,256]{1,0:T(8,128)(2,1)S(1)}, bf16[256,256]{1,0:T(8,128)(2,1)S(1)}, u32[]{:S(2)}, u32[]{:S(2)}) %collective-permute-start.1) | collective-permute-done | bytes 131104 | tf_op jit(solution)/shard_map/ppermute | solution.py:300
  100.6 0.2 fold.1
  100.8 5.9 %collective-permute-start.3 = (bf16[160,256]{1,0:T(8,128)(2,1)S(1)}, bf16[160,256]{1,0:T(8,128)(2,1)S(1)}, u32[]{:S(2)}, u32[]{:S(2)}) collective-permute-start(bf16[160,256]{1,0:T(8,128)(2,1)S(1)} %get-tuple-element.44), channel_id=1, source_target_pairs={{0,256},{32,288},{64,320},{96,352},{128,384},{160,416},{192,448},{... | collective-permute-start | bytes 245768 | tf_op jit(solution)/shard_map/ppermute | solution.py:315
  106.8 2.9 %collective-permute-start.4 = (bf16[160,256]{1,0:T(8,128)(2,1)S(1)}, bf16[160,256]{1,0:T(8,128)(2,1)S(1)}, u32[]{:S(2)}, u32[]{:S(2)}) collective-permute-start(bf16[160,256]{1,0:T(8,128)(2,1)S(1)} %get-tuple-element.45), channel_id=1, source_target_pairs={{0,128},{32,160},{64,192},{96,224},{128,256},{160,288},{192,320},{... | collective-permute-start | bytes 245768 | tf_op jit(solution)/shard_map/ppermute | solution.py:315
  109.7 1.3 %collective-permute-start.5 = (bf16[160,256]{1,0:T(8,128)(2,1)S(1)}, bf16[160,256]{1,0:T(8,128)(2,1)S(1)}, u32[]{:S(2)}, u32[]{:S(2)}) collective-permute-start(bf16[160,256]{1,0:T(8,128)(2,1)S(1)} %get-tuple-element.46), channel_id=1, source_target_pairs={{0,384},{32,416},{320,192},{352,224},{384,256},{416,288},{448,320}... | collective-permute-start | bytes 245768 | tf_op jit(solution)/shard_map/ppermute | solution.py:315
  111.0 0.1 add_convert_fusion
  111.1 0.7 fusion
  111.7 0.0 collective-permute-done.3.p0
  111.7 0.0 collective-permute-done.4.p1
  111.7 4.6 %collective-permute-done.5.p2 = bf16[160,256]{1,0:T(8,128)(2,1)S(1)} collective-permute-done((bf16[160,256]{1,0:T(8,128)(2,1)S(1)}, bf16[160,256]{1,0:T(8,128)(2,1)S(1)}, u32[]{:S(2)}, u32[]{:S(2)}) %collective-permute-start.5) | collective-permute-done | bytes 81952 | tf_op jit(solution)/shard_map/ppermute | solution.py:315
  116.4 0.7 finish.1
  (3 shorter events, 0.0 us)
Async XLA Ops:
  32.8 28.2 %all-to-all-start = ((bf16[32,60,256]{2,1,0:T(8,128)(2,1)}), bf16[32,60,256]{2,1,0:T(8,128)(2,1)S(1)}, u32[]{:S(2)}, u32[]{:S(2)}) async-start(bf16[32,60,256]{2,1,0:T(8,128)(2,1)} %bitcast.16), calls=%async_computation | async-start | bytes 2097152 | tf_op jit(solution)/shard_map/all_to_all | solution.py:295
  74.7 25.9 %all-to-all-start.2 = ((bf16[32,60,256]{2,1,0:T(8,128)(2,1)}), bf16[32,60,256]{2,1,0:T(8,128)(2,1)S(1)}, u32[]{:S(2)}, u32[]{:S(2)}) async-start(bf16[32,60,256]{2,1,0:T(8,128)(2,1)} %bitcast.7), calls=%async_computation.2 | async-start | bytes 2097152 | tf_op jit(solution)/shard_map/all_to_all | solution.py:295
  83.4 9.2 %collective-permute-start = (bf16[256,256]{1,0:T(8,128)(2,1)S(1)}, bf16[256,256]{1,0:T(8,128)(2,1)S(1)}, u32[]{:S(2)}, u32[]{:S(2)}) collective-permute-start(bf16[256,256]{1,0:T(8,128)(2,1)S(1)} %get-tuple-element.36), channel_id=1, source_target_pairs={{0,96},{32,0},{64,32},{96,64},{128,224},{160,128},{192,160},{224,1... | collective-permute-start | bytes 393224 | tf_op jit(solution)/shard_map/ppermute | solution.py:300
  85.8 14.8 %collective-permute-start.1 = (bf16[256,256]{1,0:T(8,128)(2,1)S(1)}, bf16[256,256]{1,0:T(8,128)(2,1)S(1)}, u32[]{:S(2)}, u32[]{:S(2)}) collective-permute-start(bf16[256,256]{1,0:T(8,128)(2,1)S(1)} %get-tuple-element.37), channel_id=1, source_target_pairs={{0,64},{32,96},{64,0},{96,32},{128,192},{160,224},{192,128},{224,1... | collective-permute-start | bytes 393224 | tf_op jit(solution)/shard_map/ppermute | solution.py:300
  90.7 9.9 %collective-permute-start.2 = (bf16[256,256]{1,0:T(8,128)(2,1)S(1)}, bf16[256,256]{1,0:T(8,128)(2,1)S(1)}, u32[]{:S(2)}, u32[]{:S(2)}) collective-permute-start(bf16[256,256]{1,0:T(8,128)(2,1)S(1)} %get-tuple-element.38), channel_id=1, source_target_pairs={{0,32},{32,64},{64,96},{96,0},{128,160},{160,192},{192,224},{224,1... | collective-permute-start | bytes 393224 | tf_op jit(solution)/shard_map/ppermute | solution.py:300
  100.8 10.9 %collective-permute-start.3 = (bf16[160,256]{1,0:T(8,128)(2,1)S(1)}, bf16[160,256]{1,0:T(8,128)(2,1)S(1)}, u32[]{:S(2)}, u32[]{:S(2)}) collective-permute-start(bf16[160,256]{1,0:T(8,128)(2,1)S(1)} %get-tuple-element.44), channel_id=1, source_target_pairs={{0,256},{32,288},{64,320},{96,352},{128,384},{160,416},{192,448},{... | collective-permute-start | bytes 245768 | tf_op jit(solution)/shard_map/ppermute | solution.py:315
  106.8 5.0 %collective-permute-start.4 = (bf16[160,256]{1,0:T(8,128)(2,1)S(1)}, bf16[160,256]{1,0:T(8,128)(2,1)S(1)}, u32[]{:S(2)}, u32[]{:S(2)}) collective-permute-start(bf16[160,256]{1,0:T(8,128)(2,1)S(1)} %get-tuple-element.45), channel_id=1, source_target_pairs={{0,128},{32,160},{64,192},{96,224},{128,256},{160,288},{192,320},{... | collective-permute-start | bytes 245768 | tf_op jit(solution)/shard_map/ppermute | solution.py:315
  109.7 6.7 %collective-permute-start.5 = (bf16[160,256]{1,0:T(8,128)(2,1)S(1)}, bf16[160,256]{1,0:T(8,128)(2,1)S(1)}, u32[]{:S(2)}, u32[]{:S(2)}) collective-permute-start(bf16[160,256]{1,0:T(8,128)(2,1)S(1)} %get-tuple-element.46), channel_id=1, source_target_pairs={{0,384},{32,416},{320,192},{352,224},{384,256},{416,288},{448,320}... | collective-permute-start | bytes 245768 | tf_op jit(solution)/shard_map/ppermute | solution.py:315

commit v6 on v5

--- a/solution.py
+++ b/solution.py
@@ -48,7 +48,7 @@
 
 
 def member_of(member, turn):
-    return lax.rem(member - turn + QUAD, QUAD)
+    return member ^ turn
 
 
 def fetch(sources, targets, sems):
@@ -95,12 +95,18 @@
     out_ref[...] = f_ref[...].astype(BF16)
 
 
-def fan_kernel(gathered, queries, gradient, out_ref, qg_ref, f_ref, slab_ref, sems):
-    rows = queries.shape[0]
-    targets = (qg_ref.at[pl.ds(0, rows), pl.ds(0, HEAD)], qg_ref.at[pl.ds(0, rows), pl.ds(HEAD, HEAD)])
-    copies = fetch((queries, gradient), targets, sems)
-    for quad in range(QUAD):
-        f_ref[quad] = gathered[quad].astype(F32)
+def join_kernel(packed, queries, gradient, own_ref, qg_ref):
+    own_ref[...] = packed[...].astype(F32)
+    qg_ref[:, :HEAD] = queries[...]
+    qg_ref[:, HEAD:] = gradient[...]
+
+
+def fan_kernel(p0, p1, p2, p3, joined, out_ref, qg_ref, f_ref, slab_ref):
+    rows = joined.shape[0]
+    dp = lax.axis_index("dp")
+    quad, member = dp // QUAD, dp % QUAD
+    for turn, part in enumerate((p0, p1, p2, p3)):
+        f_ref[quad ^ turn] = part[...].astype(F32)
     for group in range(GROUPS):
         for block in range(BLOCKS):
             slab_ref[group, PIECE * block : PIECE * (block + 1), :] = f_ref[
@@ -109,10 +115,12 @@
         slab = slab_ref[group].astype(BF16)
         for srv in range(SRVS):
             out_ref[group, srv] = slab
-    count = sum(f_ref[quad, PIECE * GROUPS :, :] for quad in range(QUAD))
+    count = jnp.zeros((8, 2 * HEAD), F32)
+    for owner in range(1, QUAD):
+        held = f_ref[owner, PIECE * GROUPS :, :]
+        count += jnp.where(reached(quad, QUAD * owner + member), held, 0.0)
+    qg_ref[:rows, :] = joined[...]
     qg_ref[rows:, :] = count.astype(BF16)
-    for copy in copies:
-        copy.wait()
 
 
 def fold_kernel(parts, own_ref, next_ref, far_ref, last_ref, slab_ref, f_ref):
@@ -124,7 +132,7 @@
                 group, PIECE * block : PIECE * (block + 1), :
             ]
     for turn, ref in enumerate((own_ref, next_ref, far_ref, last_ref)):
-        owner = lax.rem(quad + turn, QUAD)
+        owner = quad ^ turn
         ref[...] = f_ref[jnp.maximum(owner - 1, 0)].astype(BF16)
 
     @pl.when(quad == 0)
@@ -151,13 +159,16 @@
     keys = kv.shape[1]
     query_at = CONTEXT + 2 * cols * quad
 
+    window_end = ((query_at + ROWS - 1) // SHARD + 1) * SHARD
     count = sum(jnp.sum(qg[who, cols:, :].astype(F32), axis=0, keepdims=True) for who in range(QUAD))
     lanes = lax.broadcasted_iota(jnp.int32, count.shape, 1)
     starts = []
     for doc in range(DOCS):
-        high = jnp.sum(jnp.where(lanes < doc, count, 0.0)) * 64.0
-        low = jnp.sum(jnp.where((lanes >= DOCS) & (lanes < DOCS + doc), count, 0.0))
-        starts.append((high + low).astype(jnp.int32))
+        high = jnp.sum(jnp.where((lanes >= doc) & (lanes < DOCS), count, 0.0)) * 64.0
+        low = jnp.sum(
+            jnp.where((lanes >= DOCS + doc) & (lanes < 2 * DOCS), count, 0.0)
+        )
+        starts.append(window_end - (high + low).astype(jnp.int32))
     reach = jnp.int32(0)
     for start in starts:
         reach = jnp.where(start <= query_at, jnp.maximum(reach, start), reach)
@@ -295,21 +306,30 @@
     return lax.all_to_all(block, axis, 0, 0, tiled=True, axis_index_groups=groups)
 
 
-def rotate(block, turn):
-    pairs = [(q[i], q[(i + turn) % QUAD]) for q in NEAR for i in range(QUAD)]
-    return lax.ppermute(block, "dp", pairs)
+def swap(block, turn):
+    return lax.ppermute(block, "dp", [(place, place ^ turn) for place in range(DP)])
 
 
 def reached(quad, shard):
     first = CONTEXT + ROWS * quad
-    return first - (DOC_MAX - 1) < SHARD * (shard + 1) and SHARD * shard < first + ROWS
+    return (first - (DOC_MAX - 1) < SHARD * (shard + 1)) & (SHARD * shard < first + ROWS)
+
+
+def hand_out(block, turn):
+    pairs = []
+    for owner in range(1, QUAD):
+        quad = owner ^ turn
+        for m in range(QUAD):
+            if reached(quad, QUAD * owner + m):
+                pairs.append((QUAD * owner + m, QUAD * quad + m))
+    return lax.ppermute(block, "dp", pairs)
 
 
 def carry_on(block, turn):
     pairs = []
     for quad in range(QUAD):
-        owner = (quad + turn) % QUAD
-        for m in range(QUAD):
+        owner = quad ^ turn
+        for m in range(QUAD) if owner else ():
             if reached(quad, QUAD * owner + m):
                 pairs.append((QUAD * quad + m, QUAD * owner + m))
     return lax.ppermute(block, "dp", pairs)
@@ -343,23 +363,32 @@
         compiler_params=roomy,
         name="pack",
     )(*sources)
-    gathered = lax.all_gather(packed, "dp", axis=0, axis_index_groups=FAR)
+    parts = [hand_out(packed, turn) for turn in (2, 3, 1)]
+    own, joined = call(
+        join_kernel,
+        out_shape=(
+            jax.ShapeDtypeStruct((part + 8, wide), F32),
+            jax.ShapeDtypeStruct((rows, wide), BF16),
+        ),
+        in_specs=[vmem] * 3,
+        out_specs=(vmem, vmem),
+        name="join",
+    )(packed, queries.reshape(rows, HEAD), output_gradient.reshape(rows, HEAD))
     slabs, qg = pl.pallas_call(
         fan_kernel,
         out_shape=(
             jax.ShapeDtypeStruct(slabs_shape, BF16),
             jax.ShapeDtypeStruct((rows + 8, wide), BF16),
         ),
-        in_specs=[vmem, hbm, hbm],
+        in_specs=[vmem] * (QUAD + 1),
         out_specs=(vmem, vmem),
         scratch_shapes=[
             pltpu.VMEM((QUAD, part + 8, wide), F32),
             pltpu.VMEM((GROUPS, BLOCKS * PIECE, wide), F32),
-            pltpu.SemaphoreType.DMA((2,)),
         ],
-        compiler_params=roomy,
+        compiler_params=params,
         name="fan",
-    )(gathered, queries.reshape(rows, HEAD), output_gradient.reshape(rows, HEAD))
+    )(own, parts[2], parts[0], parts[1], joined)
     flat = (GROUPS * SRVS, BLOCKS * PIECE, wide)
     slabs = exchange(slabs.reshape(flat), ("head", "srv")).reshape(slabs_shape)
     qg = lax.all_gather(qg, "dp", axis=0, axis_index_groups=NEAR)
@@ -402,7 +431,7 @@
         name="backward",
     )(active, qg, kv, e, o, stats)
 
-    oqs = [oqs[0]] + [rotate(oqs[turn], -turn) for turn in range(1, QUAD)]
+    oqs = [swap(oqs[turn], turn) for turn in (3, 2, 1)] + [oqs[0]]
     dkv = exchange(dkv.reshape(flat), ("head", "srv"))
     dkv, oqs = lax.optimization_barrier((dkv, oqs))
     dkv = call(
@@ -416,7 +445,7 @@
         ],
         name="fold",
     )(dkv.reshape(slabs_shape))
-    dkv = [carry_on(dkv[turn], turn) for turn in (2, 1, 3)] + [dkv[0]]
+    dkv = [carry_on(dkv[turn], turn) for turn in (2, 3, 1)] + [dkv[0]]
     k_grad, v_grad = call(
         finish_kernel,
         out_shape=(jax.ShapeDtypeStruct((PIECE, GROUPS * HEAD), BF16),) * 2,

time: 118 us -> 117 us (level); the launches traced: 117 us -> 115 us
  blocking collectives: 48.1 us -> 31.7 us
  starting transfers between devices: 39.9 us -> 48 us
  waiting for transfers between devices: 15.6 us -> 20.5 us
  local copies, waits for them, and re-layouts: 0.66 us -> 3.22 us
  Pallas kernels: 12 us -> 10.3 us
    all_gather x1 -> x0, blocking collectives: 27.5 us -> none  [local(): gathered = lax.all_gather(packed, 'dp', axis=0, axis_index_groups=FAR)]
    ppermute x3 -> x6, waiting for transfers between devices: 7.95 us -> 19 us  [the longest x3 12.7 us: hand_out(): return lax.ppermute(block, 'dp', pairs)]
    all_gather x1, blocking collectives: 13.3 us -> 22.1 us  [local(): qg = lax.all_gather(qg, 'dp', axis=0, axis_index_groups=NEAR)]
    ppermute x3, starting transfers between devices: 10.2 us -> 14.3 us  [carry_on(): return lax.ppermute(block, 'dp', pairs)]
    ppermute x3 -> x6, starting transfers between devices: 9.18 us -> 13.1 us  [the longest x3 9.27 us: swap(): lax.ppermute(block, 'dp', [(place, place ^ turn) for place in range(DP)])]
    ppermute x3, waiting for transfers between devices: 4.64 us -> 0.72 us  [carry_on(): return lax.ppermute(block, 'dp', pairs)]
    unnamed x0 -> x6, local copies, waits for them, and re-layouts: none -> 2.56 us
    all_to_all x1, blocking collectives: 7.31 us -> 9.68 us  [exchange(): lax.all_to_all(block, axis, 0, 0, tiled=True, axis_index_groups=groups)]
  transfers between devices with their start and end apart: 8 -> 11, of which waited for: 3 -> 5; matrix products, arithmetic and copies ran while one was open for 1% -> 1% of each run, Pallas kernels for 0% -> 0%
where the time goes in v6:
time: 117 us; the launch traced here: 115 us
  starting transfers between devices  48 us (41%)
  blocking collectives  31.7 us (27%)
  waiting for transfers between devices  20.5 us (18%)
  Pallas kernels  10.3 us (9%)
  local copies, waits for them, and re-layouts  3.22 us (3%)
    all_gather x1, blocking collectives, local(): qg = lax.all_gather(qg, 'dp', axis=0, axis_index_groups=NEAR)  22.1 us
    all_to_all x2, starting transfers between devices, exchange(): lax.all_to_all(block, axis, 0, 0, tiled=True, axis_index_groups=groups)  20.5 us
    ppermute x3, starting transfers between devices, carry_on(): return lax.ppermute(block, 'dp', pairs)  14.3 us
    ppermute x3, waiting for transfers between devices, hand_out(): return lax.ppermute(block, 'dp', pairs)  12.7 us
    all_to_all x1, blocking collectives, exchange(): lax.all_to_all(block, axis, 0, 0, tiled=True, axis_index_groups=groups)  9.68 us
    ppermute x3, starting transfers between devices, swap(): lax.ppermute(block, 'dp', [(place, place ^ turn) for place in range(DP)])  9.27 us
    ppermute x3, waiting for transfers between devices, swap(): lax.ppermute(block, 'dp', [(place, place ^ turn) for place in range(DP)])  6.23 us
    pallas_call x1, Pallas kernels, local(): call(backward_kernel, out_shape=(*[jax.ShapeDtypeStruct((rows, wide), BF1...  3.94 us
  transfers between devices with their start and end apart: 11, of which 5 were waited for; matrix products, arithmetic and copies ran while one was open for 1% of the time, Pallas kernels for 0%

profile of v6, /device:TPU:1, one launch (start us, length us, event | category | flops | bytes accessed | tf_op | source)
XLA Modules:
  0.0 114.6 jit_solution(16296622163730998499)
XLA Ops:
  0.6 1.8 %pack.1.packed = bf16[168,256]{1,0:T(8,128)(2,1)} custom-call(s32[5,128]{1,0:T(8,128)} %bitcast.18, bf16[80,1024]{1,0:T(8,128)(2,1)} %keys_in.1, bf16[80,1024]{1,0:T(8,128)(2,1)} %values_in.1), custom_call_target="tpu_custom_call" | custom-call | tf_op jit(solution)/shard_map/pack/pallas_call | solution.py:351
  2.4 1.3 %collective-permute-start.2 = (bf16[168,256]{1,0:T(8,128)(2,1)}, bf16[168,256]{1,0:T(8,128)(2,1)S(1)}, u32[]{:S(2)}, u32[]{:S(2)}) collective-permute-start(bf16[168,256]{1,0:T(8,128)(2,1)} %pack.1.packed), channel_id=1, source_target_pairs={{192,320},{224,352},{256,128},{288,160},{320,192},{352,224},{384,0... | collective-permute-start | bytes 258056 | tf_op jit(solution)/shard_map/ppermute | solution.py:325
  3.7 1.3 %collective-permute-start.1 = (bf16[168,256]{1,0:T(8,128)(2,1)}, bf16[168,256]{1,0:T(8,128)(2,1)S(1)}, u32[]{:S(2)}, u32[]{:S(2)}) collective-permute-start(bf16[168,256]{1,0:T(8,128)(2,1)} %pack.1.packed), channel_id=1, source_target_pairs={{224,480},{256,0},{288,32},{320,64},{352,96},{384,128},{416,160},{... | collective-permute-start | bytes 258056 | tf_op jit(solution)/shard_map/ppermute | solution.py:325
  5.0 1.3 %collective-permute-start = (bf16[168,256]{1,0:T(8,128)(2,1)}, bf16[168,256]{1,0:T(8,128)(2,1)S(1)}, u32[]{:S(2)}, u32[]{:S(2)}) collective-permute-start(bf16[168,256]{1,0:T(8,128)(2,1)} %pack.1.packed), channel_id=1, source_target_pairs={{128,0},{160,32},{192,64},{224,96},{256,384},{288,416},{320,448},{... | collective-permute-start | bytes 258056 | tf_op jit(solution)/shard_map/ppermute | solution.py:325
  6.3 0.9 copy-done
  7.2 0.8 copy-done.1
  8.1 0.8 copy-done.2
  8.9 8.3 %collective-permute-done.2.p3 = bf16[168,256]{1,0:T(8,128)(2,1)S(1)} collective-permute-done((bf16[168,256]{1,0:T(8,128)(2,1)}, bf16[168,256]{1,0:T(8,128)(2,1)S(1)}, u32[]{:S(2)}, u32[]{:S(2)}) %collective-permute-start.2) | collective-permute-done | bytes 86048 | tf_op jit(solution)/shard_map/ppermute | solution.py:325
  17.3 4.4 %collective-permute-done.1.p2 = bf16[168,256]{1,0:T(8,128)(2,1)S(1)} collective-permute-done((bf16[168,256]{1,0:T(8,128)(2,1)}, bf16[168,256]{1,0:T(8,128)(2,1)S(1)}, u32[]{:S(2)}, u32[]{:S(2)}) %collective-permute-start.1) | collective-permute-done | bytes 86048 | tf_op jit(solution)/shard_map/ppermute | solution.py:325
  21.6 1.2 %fan.1 = (bf16[8,4,60,256]{3,2,1,0:T(8,128)(2,1)}, bf16[264,256]{1,0:T(8,128)(2,1)S(1)}) custom-call(f32[168,256]{1,0:T(8,128)S(1)} %get-tuple-element.29.p0, bf16[168,256]{1,0:T(8,128)(2,1)S(1)} %collective-permute-done.p1, bf16[168,256]{1,0:T(8,128)(2,1)S(1)} %collective-permute-done.1.p2, bf16[168,256]{1,0:T(8,128)(2,1)S(1)} %collective-permute-done.2.p3, ...), custom_call_target="tpu_custom_call" | custom-call | tf_op jit(solution)/shard_map/fan/pallas_call | solution.py:377
  22.8 11.8 %all-to-all-start = ((bf16[32,60,256]{2,1,0:T(8,128)(2,1)}), bf16[32,60,256]{2,1,0:T(8,128)(2,1)S(1)}, u32[]{:S(2)}, u32[]{:S(2)}) async-start(bf16[32,60,256]{2,1,0:T(8,128)(2,1)} %bitcast.4), calls=%async_computation | async-start | bytes 2097152 | tf_op jit(solution)/shard_map/all_to_all | solution.py:306
  34.6 22.1 %all-gather = bf16[1056,256]{1,0:T(8,128)(2,1)S(1)} all-gather(bf16[264,256]{1,0:T(8,128)(2,1)S(1)} %get-tuple-element.31), channel_id=2, replica_groups={{0,32,64,96},{128,160,192,224},{256,288,320,352},{384,416,448,480},{1,3..., dimensions={0}, use_global_device_ids=true | all-gather | bytes 675840 | tf_op jit(solution)/shard_map/all_gather | solution.py:394
  56.7 2.5 %forward.1 = (bf16[3,640,1024]{2,1,0:T(8,128)(2,1)S(1)}, f32[4,128,256]{2,1,0:T(8,128)S(1)}, f32[4,16,256]{2,1,0:T(8,128)S(1)}, s32[2]{0:T(128)S(1)}, bf16[3,640,256]{2,1,0:T(8,128)(2,1)S(1)}) custom-call(bf16[4,264,256]{2,1,0:T(8,128)(2,1)S(1)} %bitcast.10, bf16[8,4,60,256]{3,2,1,0:T(8,128)(2,1)S(1)} %bitcast.13), custom_call_target="tpu_custom_call" | custom-call | tf_op jit(solution)/shard_map/forward/pallas_call | solution.py:396
  59.2 9.7 %all_to_all.16.stats = f32[4,16,256]{2,1,0:T(8,128)S(1)} all-to-all(f32[4,16,256]{2,1,0:T(8,128)S(1)} %get-tuple-element.37), channel_id=1, replica_groups={{0,32,64,96},{128,160,192,224},{256,288,320,352},{384,416,448,480},{1,3..., dimensions={0} | all-to-all | bytes 131072 | tf_op jit(solution)/shard_map/all_to_all | solution.py:306
  68.9 3.9 %backward.1 = (bf16[256,256]{1,0:T(8,128)(2,1)S(1)}, bf16[256,256]{1,0:T(8,128)(2,1)S(1)}, bf16[256,256]{1,0:T(8,128)(2,1)S(1)}, bf16[256,256]{1,0:T(8,128)(2,1)S(1)}, bf16[8,4,60,256]{3,2,1,0:T(8,128)(2,1)}) custom-call(s32[2]{0:T(128)S(1)} %get-tuple-element.33.active, bf16[4,264,256]{2,1,0:T(8,128)(2,1)S(1)} %bitcast.11, ...), custom_call_target="tpu_custom_call" | custom-call | tf_op jit(solution)/shard_map/backward/pallas_call | solution.py:418
  72.8 8.8 %all-to-all-start.2 = ((bf16[32,60,256]{2,1,0:T(8,128)(2,1)}), bf16[32,60,256]{2,1,0:T(8,128)(2,1)S(1)}, u32[]{:S(2)}, u32[]{:S(2)}) async-start(bf16[32,60,256]{2,1,0:T(8,128)(2,1)} %bitcast.6), calls=%async_computation.2 | async-start | bytes 2097152 | tf_op jit(solution)/shard_map/all_to_all | solution.py:306
  81.6 1.9 %collective-permute-start.3 = (bf16[256,256]{1,0:T(8,128)(2,1)S(1)}, bf16[256,256]{1,0:T(8,128)(2,1)S(1)}, u32[]{:S(2)}, u32[]{:S(2)}) collective-permute-start(bf16[256,256]{1,0:T(8,128)(2,1)S(1)} %get-tuple-element.39), channel_id=1, source_target_pairs={{0,96},{32,64},{64,32},{96,0},{128,224},{160,192},{192,160},{224,1... | collective-permute-start | bytes 393224 | tf_op jit(solution)/shard_map/ppermute | solution.py:310
  83.5 3.7 %collective-permute-start.4 = (bf16[256,256]{1,0:T(8,128)(2,1)S(1)}, bf16[256,256]{1,0:T(8,128)(2,1)S(1)}, u32[]{:S(2)}, u32[]{:S(2)}) collective-permute-start(bf16[256,256]{1,0:T(8,128)(2,1)S(1)} %get-tuple-element.40), channel_id=1, source_target_pairs={{0,64},{32,96},{64,0},{96,32},{128,192},{160,224},{192,128},{224,1... | collective-permute-start | bytes 393224 | tf_op jit(solution)/shard_map/ppermute | solution.py:310
  87.2 3.6 %collective-permute-start.5 = (bf16[256,256]{1,0:T(8,128)(2,1)S(1)}, bf16[256,256]{1,0:T(8,128)(2,1)S(1)}, u32[]{:S(2)}, u32[]{:S(2)}) collective-permute-start(bf16[256,256]{1,0:T(8,128)(2,1)S(1)} %get-tuple-element.41), channel_id=1, source_target_pairs={{0,32},{32,0},{64,96},{96,64},{128,160},{160,128},{192,224},{224,1... | collective-permute-start | bytes 393224 | tf_op jit(solution)/shard_map/ppermute | solution.py:310
  90.9 6.2 %collective-permute-done.4 = bf16[256,256]{1,0:T(8,128)(2,1)S(1)} collective-permute-done((bf16[256,256]{1,0:T(8,128)(2,1)S(1)}, bf16[256,256]{1,0:T(8,128)(2,1)S(1)}, u32[]{:S(2)}, u32[]{:S(2)}) %collective-permute-start.4) | collective-permute-done | bytes 131104 | tf_op jit(solution)/shard_map/ppermute | solution.py:310
  97.1 0.8 all-to-all-done.2
  98.1 3.2 %collective-permute-start.6 = (bf16[160,256]{1,0:T(8,128)(2,1)S(1)}, bf16[160,256]{1,0:T(8,128)(2,1)S(1)}, u32[]{:S(2)}, u32[]{:S(2)}) collective-permute-start(bf16[160,256]{1,0:T(8,128)(2,1)S(1)} %get-tuple-element.48), channel_id=1, source_target_pairs={{0,256},{32,288},{64,320},{96,352},{128,384},{160,416},{192,448},{... | collective-permute-start | bytes 245768 | tf_op jit(solution)/shard_map/ppermute | solution.py:335
  101.3 4.1 %collective-permute-start.7 = (bf16[160,256]{1,0:T(8,128)(2,1)S(1)}, bf16[160,256]{1,0:T(8,128)(2,1)S(1)}, u32[]{:S(2)}, u32[]{:S(2)}) collective-permute-start(bf16[160,256]{1,0:T(8,128)(2,1)S(1)} %get-tuple-element.49), channel_id=1, source_target_pairs={{0,384},{32,416},{128,256},{160,288},{192,320},{224,352},{320,192}... | collective-permute-start | bytes 245768 | tf_op jit(solution)/shard_map/ppermute | solution.py:335
  105.4 7.0 %collective-permute-start.8 = (bf16[160,256]{1,0:T(8,128)(2,1)S(1)}, bf16[160,256]{1,0:T(8,128)(2,1)S(1)}, u32[]{:S(2)}, u32[]{:S(2)}) collective-permute-start(bf16[160,256]{1,0:T(8,128)(2,1)S(1)} %get-tuple-element.50), channel_id=1, source_target_pairs={{0,128},{32,160},{64,192},{96,224},{256,384},{288,416},{320,448},{... | collective-permute-start | bytes 245768 | tf_op jit(solution)/shard_map/ppermute | solution.py:335
  (15 shorter events, 2.4 us)
Async XLA Ops:
  2.4 14.8 %collective-permute-start.2 = (bf16[168,256]{1,0:T(8,128)(2,1)}, bf16[168,256]{1,0:T(8,128)(2,1)S(1)}, u32[]{:S(2)}, u32[]{:S(2)}) collective-permute-start(bf16[168,256]{1,0:T(8,128)(2,1)} %pack.1.packed), channel_id=1, source_target_pairs={{192,320},{224,352},{256,128},{288,160},{320,192},{352,224},{384,0... | collective-permute-start | bytes 258056 | tf_op jit(solution)/shard_map/ppermute | solution.py:325
  3.7 17.9 %collective-permute-start.1 = (bf16[168,256]{1,0:T(8,128)(2,1)}, bf16[168,256]{1,0:T(8,128)(2,1)S(1)}, u32[]{:S(2)}, u32[]{:S(2)}) collective-permute-start(bf16[168,256]{1,0:T(8,128)(2,1)} %pack.1.packed), channel_id=1, source_target_pairs={{224,480},{256,0},{288,32},{320,64},{352,96},{384,128},{416,160},{... | collective-permute-start | bytes 258056 | tf_op jit(solution)/shard_map/ppermute | solution.py:325
  5.0 16.6 %collective-permute-start = (bf16[168,256]{1,0:T(8,128)(2,1)}, bf16[168,256]{1,0:T(8,128)(2,1)S(1)}, u32[]{:S(2)}, u32[]{:S(2)}) collective-permute-start(bf16[168,256]{1,0:T(8,128)(2,1)} %pack.1.packed), channel_id=1, source_target_pairs={{128,0},{160,32},{192,64},{224,96},{256,384},{288,416},{320,448},{... | collective-permute-start | bytes 258056 | tf_op jit(solution)/shard_map/ppermute | solution.py:325
  6.3 0.9 copy-start
  7.2 0.8 copy-start.1
  8.1 0.8 copy-start.2
  22.8 33.8 %all-to-all-start = ((bf16[32,60,256]{2,1,0:T(8,128)(2,1)}), bf16[32,60,256]{2,1,0:T(8,128)(2,1)S(1)}, u32[]{:S(2)}, u32[]{:S(2)}) async-start(bf16[32,60,256]{2,1,0:T(8,128)(2,1)} %bitcast.4), calls=%async_computation | async-start | bytes 2097152 | tf_op jit(solution)/shard_map/all_to_all | solution.py:306
  72.8 25.1 %all-to-all-start.2 = ((bf16[32,60,256]{2,1,0:T(8,128)(2,1)}), bf16[32,60,256]{2,1,0:T(8,128)(2,1)S(1)}, u32[]{:S(2)}, u32[]{:S(2)}) async-start(bf16[32,60,256]{2,1,0:T(8,128)(2,1)} %bitcast.6), calls=%async_computation.2 | async-start | bytes 2097152 | tf_op jit(solution)/shard_map/all_to_all | solution.py:306
  81.6 9.3 %collective-permute-start.3 = (bf16[256,256]{1,0:T(8,128)(2,1)S(1)}, bf16[256,256]{1,0:T(8,128)(2,1)S(1)}, u32[]{:S(2)}, u32[]{:S(2)}) collective-permute-start(bf16[256,256]{1,0:T(8,128)(2,1)S(1)} %get-tuple-element.39), channel_id=1, source_target_pairs={{0,96},{32,64},{64,32},{96,0},{128,224},{160,192},{192,160},{224,1... | collective-permute-start | bytes 393224 | tf_op jit(solution)/shard_map/ppermute | solution.py:310
  83.5 13.6 %collective-permute-start.4 = (bf16[256,256]{1,0:T(8,128)(2,1)S(1)}, bf16[256,256]{1,0:T(8,128)(2,1)S(1)}, u32[]{:S(2)}, u32[]{:S(2)}) collective-permute-start(bf16[256,256]{1,0:T(8,128)(2,1)S(1)} %get-tuple-element.40), channel_id=1, source_target_pairs={{0,64},{32,96},{64,0},{96,32},{128,192},{160,224},{192,128},{224,1... | collective-permute-start | bytes 393224 | tf_op jit(solution)/shard_map/ppermute | solution.py:310
  87.2 9.9 %collective-permute-start.5 = (bf16[256,256]{1,0:T(8,128)(2,1)S(1)}, bf16[256,256]{1,0:T(8,128)(2,1)S(1)}, u32[]{:S(2)}, u32[]{:S(2)}) collective-permute-start(bf16[256,256]{1,0:T(8,128)(2,1)S(1)} %get-tuple-element.41), channel_id=1, source_target_pairs={{0,32},{32,0},{64,96},{96,64},{128,160},{160,128},{192,224},{224,1... | collective-permute-start | bytes 393224 | tf_op jit(solution)/shard_map/ppermute | solution.py:310
  98.1 15.1 %collective-permute-start.6 = (bf16[160,256]{1,0:T(8,128)(2,1)S(1)}, bf16[160,256]{1,0:T(8,128)(2,1)S(1)}, u32[]{:S(2)}, u32[]{:S(2)}) collective-permute-start(bf16[160,256]{1,0:T(8,128)(2,1)S(1)} %get-tuple-element.48), channel_id=1, source_target_pairs={{0,256},{32,288},{64,320},{96,352},{128,384},{160,416},{192,448},{... | collective-permute-start | bytes 245768 | tf_op jit(solution)/shard_map/ppermute | solution.py:335
  101.3 11.9 %collective-permute-start.7 = (bf16[160,256]{1,0:T(8,128)(2,1)S(1)}, bf16[160,256]{1,0:T(8,128)(2,1)S(1)}, u32[]{:S(2)}, u32[]{:S(2)}) collective-permute-start(bf16[160,256]{1,0:T(8,128)(2,1)S(1)} %get-tuple-element.49), channel_id=1, source_target_pairs={{0,384},{32,416},{128,256},{160,288},{192,320},{224,352},{320,192}... | collective-permute-start | bytes 245768 | tf_op jit(solution)/shard_map/ppermute | solution.py:335
  105.4 8.5 %collective-permute-start.8 = (bf16[160,256]{1,0:T(8,128)(2,1)S(1)}, bf16[160,256]{1,0:T(8,128)(2,1)S(1)}, u32[]{:S(2)}, u32[]{:S(2)}) collective-permute-start(bf16[160,256]{1,0:T(8,128)(2,1)S(1)} %get-tuple-element.50), channel_id=1, source_target_pairs={{0,128},{32,160},{64,192},{96,224},{256,384},{288,416},{320,448},{... | collective-permute-start | bytes 245768 | tf_op jit(solution)/shard_map/ppermute | solution.py:335

commit v7 on v6

--- a/solution.py
+++ b/solution.py
@@ -433,7 +433,6 @@
 
     oqs = [swap(oqs[turn], turn) for turn in (3, 2, 1)] + [oqs[0]]
     dkv = exchange(dkv.reshape(flat), ("head", "srv"))
-    dkv, oqs = lax.optimization_barrier((dkv, oqs))
     dkv = call(
         fold_kernel,
         out_shape=(jax.ShapeDtypeStruct((part, wide), BF16),) * QUAD,
@@ -445,7 +444,7 @@
         ],
         name="fold",
     )(dkv.reshape(slabs_shape))
-    dkv = [carry_on(dkv[turn], turn) for turn in (2, 3, 1)] + [dkv[0]]
+    dkv = [carry_on(dkv[turn], turn) for turn in (3, 2, 1)] + [dkv[0]]
     k_grad, v_grad = call(
         finish_kernel,
         out_shape=(jax.ShapeDtypeStruct((PIECE, GROUPS * HEAD), BF16),) * 2,

time: 117 us -> 116 us (level)
  no operation moved by 1% of the time
where the time goes in v7:
time: 116 us; the launch traced here: 115 us
  starting transfers between devices  48 us (41%)
  blocking collectives  31.7 us (27%)
  waiting for transfers between devices  20.5 us (18%)
  Pallas kernels  10.3 us (9%)
  local copies, waits for them, and re-layouts  3.22 us (3%)
    all_gather x1, blocking collectives, local(): qg = lax.all_gather(qg, 'dp', axis=0, axis_index_groups=NEAR)  22.1 us
    all_to_all x2, starting transfers between devices, exchange(): lax.all_to_all(block, axis, 0, 0, tiled=True, axis_index_groups=groups)  20.5 us
    ppermute x3, starting transfers between devices, carry_on(): return lax.ppermute(block, 'dp', pairs)  14.3 us
    ppermute x3, waiting for transfers between devices, hand_out(): return lax.ppermute(block, 'dp', pairs)  12.7 us
    all_to_all x1, blocking collectives, exchange(): lax.all_to_all(block, axis, 0, 0, tiled=True, axis_index_groups=groups)  9.68 us
    ppermute x3, starting transfers between devices, swap(): lax.ppermute(block, 'dp', [(place, place ^ turn) for place in range(DP)])  9.27 us
    ppermute x3, waiting for transfers between devices, swap(): lax.ppermute(block, 'dp', [(place, place ^ turn) for place in range(DP)])  6.23 us
    pallas_call x1, Pallas kernels, local(): call(backward_kernel, out_shape=(*[jax.ShapeDtypeStruct((rows, wide), BF1...  3.94 us
  transfers between devices with their start and end apart: 11, of which 5 were waited for; matrix products, arithmetic and copies ran while one was open for 1% of the time, Pallas kernels for 0%

profile of v7, /device:TPU:1, one launch (start us, length us, event | category | flops | bytes accessed | tf_op | source)
XLA Modules:
  0.0 114.6 jit_solution(4277757806114776107)
XLA Ops:
  0.6 1.8 %pack.1.packed = bf16[168,256]{1,0:T(8,128)(2,1)} custom-call(s32[5,128]{1,0:T(8,128)} %bitcast.18, bf16[80,1024]{1,0:T(8,128)(2,1)} %keys_in.1, bf16[80,1024]{1,0:T(8,128)(2,1)} %values_in.1), custom_call_target="tpu_custom_call" | custom-call | tf_op jit(solution)/shard_map/pack/pallas_call | solution.py:351
  2.4 1.3 %collective-permute-start.2 = (bf16[168,256]{1,0:T(8,128)(2,1)}, bf16[168,256]{1,0:T(8,128)(2,1)S(1)}, u32[]{:S(2)}, u32[]{:S(2)}) collective-permute-start(bf16[168,256]{1,0:T(8,128)(2,1)} %pack.1.packed), channel_id=1, source_target_pairs={{192,320},{224,352},{256,128},{288,160},{320,192},{352,224},{384,0... | collective-permute-start | bytes 258056 | tf_op jit(solution)/shard_map/ppermute | solution.py:325
  3.7 1.3 %collective-permute-start.1 = (bf16[168,256]{1,0:T(8,128)(2,1)}, bf16[168,256]{1,0:T(8,128)(2,1)S(1)}, u32[]{:S(2)}, u32[]{:S(2)}) collective-permute-start(bf16[168,256]{1,0:T(8,128)(2,1)} %pack.1.packed), channel_id=1, source_target_pairs={{224,480},{256,0},{288,32},{320,64},{352,96},{384,128},{416,160},{... | collective-permute-start | bytes 258056 | tf_op jit(solution)/shard_map/ppermute | solution.py:325
  5.0 1.3 %collective-permute-start = (bf16[168,256]{1,0:T(8,128)(2,1)}, bf16[168,256]{1,0:T(8,128)(2,1)S(1)}, u32[]{:S(2)}, u32[]{:S(2)}) collective-permute-start(bf16[168,256]{1,0:T(8,128)(2,1)} %pack.1.packed), channel_id=1, source_target_pairs={{128,0},{160,32},{192,64},{224,96},{256,384},{288,416},{320,448},{... | collective-permute-start | bytes 258056 | tf_op jit(solution)/shard_map/ppermute | solution.py:325
  6.3 0.9 copy-done
  7.2 0.8 copy-done.1
  8.1 0.8 copy-done.2
  8.9 8.3 %collective-permute-done.2.p3 = bf16[168,256]{1,0:T(8,128)(2,1)S(1)} collective-permute-done((bf16[168,256]{1,0:T(8,128)(2,1)}, bf16[168,256]{1,0:T(8,128)(2,1)S(1)}, u32[]{:S(2)}, u32[]{:S(2)}) %collective-permute-start.2) | collective-permute-done | bytes 86048 | tf_op jit(solution)/shard_map/ppermute | solution.py:325
  17.3 4.4 %collective-permute-done.1.p2 = bf16[168,256]{1,0:T(8,128)(2,1)S(1)} collective-permute-done((bf16[168,256]{1,0:T(8,128)(2,1)}, bf16[168,256]{1,0:T(8,128)(2,1)S(1)}, u32[]{:S(2)}, u32[]{:S(2)}) %collective-permute-start.1) | collective-permute-done | bytes 86048 | tf_op jit(solution)/shard_map/ppermute | solution.py:325
  21.6 1.2 %fan.1 = (bf16[8,4,60,256]{3,2,1,0:T(8,128)(2,1)}, bf16[264,256]{1,0:T(8,128)(2,1)S(1)}) custom-call(f32[168,256]{1,0:T(8,128)S(1)} %get-tuple-element.24.p0, bf16[168,256]{1,0:T(8,128)(2,1)S(1)} %collective-permute-done.p1, bf16[168,256]{1,0:T(8,128)(2,1)S(1)} %collective-permute-done.1.p2, bf16[168,256]{1,0:T(8,128)(2,1)S(1)} %collective-permute-done.2.p3, ...), custom_call_target="tpu_custom_call" | custom-call | tf_op jit(solution)/shard_map/fan/pallas_call | solution.py:377
  22.8 11.8 %all-to-all-start = ((bf16[32,60,256]{2,1,0:T(8,128)(2,1)}), bf16[32,60,256]{2,1,0:T(8,128)(2,1)S(1)}, u32[]{:S(2)}, u32[]{:S(2)}) async-start(bf16[32,60,256]{2,1,0:T(8,128)(2,1)} %bitcast.4), calls=%async_computation | async-start | bytes 2097152 | tf_op jit(solution)/shard_map/all_to_all | solution.py:306
  34.6 22.1 %all-gather = bf16[1056,256]{1,0:T(8,128)(2,1)S(1)} all-gather(bf16[264,256]{1,0:T(8,128)(2,1)S(1)} %get-tuple-element.26), channel_id=2, replica_groups={{0,32,64,96},{128,160,192,224},{256,288,320,352},{384,416,448,480},{1,3..., dimensions={0}, use_global_device_ids=true | all-gather | bytes 675840 | tf_op jit(solution)/shard_map/all_gather | solution.py:394
  56.7 2.5 %forward.1 = (bf16[3,640,1024]{2,1,0:T(8,128)(2,1)S(1)}, f32[4,128,256]{2,1,0:T(8,128)S(1)}, f32[4,16,256]{2,1,0:T(8,128)S(1)}, s32[2]{0:T(128)S(1)}, bf16[3,640,256]{2,1,0:T(8,128)(2,1)S(1)}) custom-call(bf16[4,264,256]{2,1,0:T(8,128)(2,1)S(1)} %bitcast.10, bf16[8,4,60,256]{3,2,1,0:T(8,128)(2,1)S(1)} %bitcast.13), custom_call_target="tpu_custom_call" | custom-call | tf_op jit(solution)/shard_map/forward/pallas_call | solution.py:396
  59.2 9.7 %all_to_all.16.stats = f32[4,16,256]{2,1,0:T(8,128)S(1)} all-to-all(f32[4,16,256]{2,1,0:T(8,128)S(1)} %get-tuple-element.32), channel_id=1, replica_groups={{0,32,64,96},{128,160,192,224},{256,288,320,352},{384,416,448,480},{1,3..., dimensions={0} | all-to-all | bytes 131072 | tf_op jit(solution)/shard_map/all_to_all | solution.py:306
  68.9 3.9 %backward.1 = (bf16[256,256]{1,0:T(8,128)(2,1)S(1)}, bf16[256,256]{1,0:T(8,128)(2,1)S(1)}, bf16[256,256]{1,0:T(8,128)(2,1)S(1)}, bf16[256,256]{1,0:T(8,128)(2,1)S(1)}, bf16[8,4,60,256]{3,2,1,0:T(8,128)(2,1)}) custom-call(s32[2]{0:T(128)S(1)} %get-tuple-element.28.active, bf16[4,264,256]{2,1,0:T(8,128)(2,1)S(1)} %bitcast.11, ...), custom_call_target="tpu_custom_call" | custom-call | tf_op jit(solution)/shard_map/backward/pallas_call | solution.py:418
  72.8 8.8 %all-to-all-start.2 = ((bf16[32,60,256]{2,1,0:T(8,128)(2,1)}), bf16[32,60,256]{2,1,0:T(8,128)(2,1)S(1)}, u32[]{:S(2)}, u32[]{:S(2)}) async-start(bf16[32,60,256]{2,1,0:T(8,128)(2,1)} %bitcast.8), calls=%async_computation.2 | async-start | bytes 2097152 | tf_op jit(solution)/shard_map/all_to_all | solution.py:306
  81.6 1.9 %collective-permute-start.3 = (bf16[256,256]{1,0:T(8,128)(2,1)S(1)}, bf16[256,256]{1,0:T(8,128)(2,1)S(1)}, u32[]{:S(2)}, u32[]{:S(2)}) collective-permute-start(bf16[256,256]{1,0:T(8,128)(2,1)S(1)} %get-tuple-element.33), channel_id=1, source_target_pairs={{0,96},{32,64},{64,32},{96,0},{128,224},{160,192},{192,160},{224,1... | collective-permute-start | bytes 393224 | tf_op jit(solution)/shard_map/ppermute | solution.py:310
  83.5 3.7 %collective-permute-start.4 = (bf16[256,256]{1,0:T(8,128)(2,1)S(1)}, bf16[256,256]{1,0:T(8,128)(2,1)S(1)}, u32[]{:S(2)}, u32[]{:S(2)}) collective-permute-start(bf16[256,256]{1,0:T(8,128)(2,1)S(1)} %get-tuple-element.34), channel_id=1, source_target_pairs={{0,64},{32,96},{64,0},{96,32},{128,192},{160,224},{192,128},{224,1... | collective-permute-start | bytes 393224 | tf_op jit(solution)/shard_map/ppermute | solution.py:310
  87.2 3.6 %collective-permute-start.5 = (bf16[256,256]{1,0:T(8,128)(2,1)S(1)}, bf16[256,256]{1,0:T(8,128)(2,1)S(1)}, u32[]{:S(2)}, u32[]{:S(2)}) collective-permute-start(bf16[256,256]{1,0:T(8,128)(2,1)S(1)} %get-tuple-element.35), channel_id=1, source_target_pairs={{0,32},{32,0},{64,96},{96,64},{128,160},{160,128},{192,224},{224,1... | collective-permute-start | bytes 393224 | tf_op jit(solution)/shard_map/ppermute | solution.py:310
  90.9 6.2 %collective-permute-done.4 = bf16[256,256]{1,0:T(8,128)(2,1)S(1)} collective-permute-done((bf16[256,256]{1,0:T(8,128)(2,1)S(1)}, bf16[256,256]{1,0:T(8,128)(2,1)S(1)}, u32[]{:S(2)}, u32[]{:S(2)}) %collective-permute-start.4) | collective-permute-done | bytes 131104 | tf_op jit(solution)/shard_map/ppermute | solution.py:310
  98.1 6.0 %collective-permute-start.6 = (bf16[160,256]{1,0:T(8,128)(2,1)S(1)}, bf16[160,256]{1,0:T(8,128)(2,1)S(1)}, u32[]{:S(2)}, u32[]{:S(2)}) collective-permute-start(bf16[160,256]{1,0:T(8,128)(2,1)S(1)} %get-tuple-element.38), channel_id=1, source_target_pairs={{0,384},{32,416},{128,256},{160,288},{192,320},{224,352},{320,192}... | collective-permute-start | bytes 245768 | tf_op jit(solution)/shard_map/ppermute | solution.py:335
  104.1 1.3 %collective-permute-start.7 = (bf16[160,256]{1,0:T(8,128)(2,1)S(1)}, bf16[160,256]{1,0:T(8,128)(2,1)S(1)}, u32[]{:S(2)}, u32[]{:S(2)}) collective-permute-start(bf16[160,256]{1,0:T(8,128)(2,1)S(1)} %get-tuple-element.39), channel_id=1, source_target_pairs={{0,256},{32,288},{64,320},{96,352},{128,384},{160,416},{192,448},{... | collective-permute-start | bytes 245768 | tf_op jit(solution)/shard_map/ppermute | solution.py:335
  105.4 7.0 %collective-permute-start.8 = (bf16[160,256]{1,0:T(8,128)(2,1)S(1)}, bf16[160,256]{1,0:T(8,128)(2,1)S(1)}, u32[]{:S(2)}, u32[]{:S(2)}) collective-permute-start(bf16[160,256]{1,0:T(8,128)(2,1)S(1)} %get-tuple-element.40), channel_id=1, source_target_pairs={{0,128},{32,160},{64,192},{96,224},{256,384},{288,416},{320,448},{... | collective-permute-start | bytes 245768 | tf_op jit(solution)/shard_map/ppermute | solution.py:335
  113.1 0.8 collective-permute-done.8.p2
  (15 shorter events, 2.4 us)
Async XLA Ops:
  2.4 14.8 %collective-permute-start.2 = (bf16[168,256]{1,0:T(8,128)(2,1)}, bf16[168,256]{1,0:T(8,128)(2,1)S(1)}, u32[]{:S(2)}, u32[]{:S(2)}) collective-permute-start(bf16[168,256]{1,0:T(8,128)(2,1)} %pack.1.packed), channel_id=1, source_target_pairs={{192,320},{224,352},{256,128},{288,160},{320,192},{352,224},{384,0... | collective-permute-start | bytes 258056 | tf_op jit(solution)/shard_map/ppermute | solution.py:325
  3.7 17.9 %collective-permute-start.1 = (bf16[168,256]{1,0:T(8,128)(2,1)}, bf16[168,256]{1,0:T(8,128)(2,1)S(1)}, u32[]{:S(2)}, u32[]{:S(2)}) collective-permute-start(bf16[168,256]{1,0:T(8,128)(2,1)} %pack.1.packed), channel_id=1, source_target_pairs={{224,480},{256,0},{288,32},{320,64},{352,96},{384,128},{416,160},{... | collective-permute-start | bytes 258056 | tf_op jit(solution)/shard_map/ppermute | solution.py:325
  5.0 16.6 %collective-permute-start = (bf16[168,256]{1,0:T(8,128)(2,1)}, bf16[168,256]{1,0:T(8,128)(2,1)S(1)}, u32[]{:S(2)}, u32[]{:S(2)}) collective-permute-start(bf16[168,256]{1,0:T(8,128)(2,1)} %pack.1.packed), channel_id=1, source_target_pairs={{128,0},{160,32},{192,64},{224,96},{256,384},{288,416},{320,448},{... | collective-permute-start | bytes 258056 | tf_op jit(solution)/shard_map/ppermute | solution.py:325
  6.3 0.9 copy-start
  7.2 0.8 copy-start.1
  8.1 0.8 copy-start.2
  22.8 33.8 %all-to-all-start = ((bf16[32,60,256]{2,1,0:T(8,128)(2,1)}), bf16[32,60,256]{2,1,0:T(8,128)(2,1)S(1)}, u32[]{:S(2)}, u32[]{:S(2)}) async-start(bf16[32,60,256]{2,1,0:T(8,128)(2,1)} %bitcast.4), calls=%async_computation | async-start | bytes 2097152 | tf_op jit(solution)/shard_map/all_to_all | solution.py:306
  72.8 25.1 %all-to-all-start.2 = ((bf16[32,60,256]{2,1,0:T(8,128)(2,1)}), bf16[32,60,256]{2,1,0:T(8,128)(2,1)S(1)}, u32[]{:S(2)}, u32[]{:S(2)}) async-start(bf16[32,60,256]{2,1,0:T(8,128)(2,1)} %bitcast.8), calls=%async_computation.2 | async-start | bytes 2097152 | tf_op jit(solution)/shard_map/all_to_all | solution.py:306
  81.6 9.3 %collective-permute-start.3 = (bf16[256,256]{1,0:T(8,128)(2,1)S(1)}, bf16[256,256]{1,0:T(8,128)(2,1)S(1)}, u32[]{:S(2)}, u32[]{:S(2)}) collective-permute-start(bf16[256,256]{1,0:T(8,128)(2,1)S(1)} %get-tuple-element.33), channel_id=1, source_target_pairs={{0,96},{32,64},{64,32},{96,0},{128,224},{160,192},{192,160},{224,1... | collective-permute-start | bytes 393224 | tf_op jit(solution)/shard_map/ppermute | solution.py:310
  83.5 13.6 %collective-permute-start.4 = (bf16[256,256]{1,0:T(8,128)(2,1)S(1)}, bf16[256,256]{1,0:T(8,128)(2,1)S(1)}, u32[]{:S(2)}, u32[]{:S(2)}) collective-permute-start(bf16[256,256]{1,0:T(8,128)(2,1)S(1)} %get-tuple-element.34), channel_id=1, source_target_pairs={{0,64},{32,96},{64,0},{96,32},{128,192},{160,224},{192,128},{224,1... | collective-permute-start | bytes 393224 | tf_op jit(solution)/shard_map/ppermute | solution.py:310
  87.2 9.9 %collective-permute-start.5 = (bf16[256,256]{1,0:T(8,128)(2,1)S(1)}, bf16[256,256]{1,0:T(8,128)(2,1)S(1)}, u32[]{:S(2)}, u32[]{:S(2)}) collective-permute-start(bf16[256,256]{1,0:T(8,128)(2,1)S(1)} %get-tuple-element.35), channel_id=1, source_target_pairs={{0,32},{32,0},{64,96},{96,64},{128,160},{160,128},{192,224},{224,1... | collective-permute-start | bytes 393224 | tf_op jit(solution)/shard_map/ppermute | solution.py:310
  98.1 15.0 %collective-permute-start.6 = (bf16[160,256]{1,0:T(8,128)(2,1)S(1)}, bf16[160,256]{1,0:T(8,128)(2,1)S(1)}, u32[]{:S(2)}, u32[]{:S(2)}) collective-permute-start(bf16[160,256]{1,0:T(8,128)(2,1)S(1)} %get-tuple-element.38), channel_id=1, source_target_pairs={{0,384},{32,416},{128,256},{160,288},{192,320},{224,352},{320,192}... | collective-permute-start | bytes 245768 | tf_op jit(solution)/shard_map/ppermute | solution.py:335
  104.1 9.0 %collective-permute-start.7 = (bf16[160,256]{1,0:T(8,128)(2,1)S(1)}, bf16[160,256]{1,0:T(8,128)(2,1)S(1)}, u32[]{:S(2)}, u32[]{:S(2)}) collective-permute-start(bf16[160,256]{1,0:T(8,128)(2,1)S(1)} %get-tuple-element.39), channel_id=1, source_target_pairs={{0,256},{32,288},{64,320},{96,352},{128,384},{160,416},{192,448},{... | collective-permute-start | bytes 245768 | tf_op jit(solution)/shard_map/ppermute | solution.py:335
  105.4 8.5 %collective-permute-start.8 = (bf16[160,256]{1,0:T(8,128)(2,1)S(1)}, bf16[160,256]{1,0:T(8,128)(2,1)S(1)}, u32[]{:S(2)}, u32[]{:S(2)}) collective-permute-start(bf16[160,256]{1,0:T(8,128)(2,1)S(1)} %get-tuple-element.40), channel_id=1, source_target_pairs={{0,128},{32,160},{64,192},{96,224},{256,384},{288,416},{320,448},{... | collective-permute-start | bytes 245768 | tf_op jit(solution)/shard_map/ppermute | solution.py:335

commit v8 on v6

--- a/solution.py
+++ b/solution.py
@@ -211,7 +211,8 @@
         for turn in range(QUAD):
             span = pl.ds(turn * cols, cols)
             s = dot(k, qs[turn][:cols, :HEAD], NT)
-            allowed = (key_place >= doc_starts[turn]) & (key_place <= query_places[turn])
+            since = (key_place - doc_starts[turn]).astype(jnp.uint32)
+            allowed = since <= (query_places[turn] - doc_starts[turn]).astype(jnp.uint32)
             s = jnp.where(allowed, s, NEGATIVE)
             s_ref[t, :, span] = s
             m_ref[turn] = jnp.maximum(m_ref[turn], fold8(s, jnp.max))

time: 117 us -> 118 us (level); the launches traced: 115 us -> 119 us
  Pallas kernels: 10.3 us -> 13.1 us
    pallas_call x1, Pallas kernels: 3.94 us -> 5.56 us  [local(): call(backward_kernel, out_shape=(*[jax.ShapeDtypeStruct((rows, wide), BF1...]
    ppermute x3, starting transfers between devices: 14.3 us -> 15.6 us  [carry_on(): return lax.ppermute(block, 'dp', pairs)]
    pallas_call x1, Pallas kernels: 2.49 us -> 3.68 us  [local(): call(forward_kernel, out_shape=(jax.ShapeDtypeStruct((BLOCKS, SHARD, QUAD...]
where the time goes in v8:
time: 118 us; the launch traced here: 119 us
  starting transfers between devices  49 us (42%)
  blocking collectives  31.9 us (27%)
  waiting for transfers between devices  20.5 us (17%)
  Pallas kernels  13.1 us (11%)
  local copies, waits for them, and re-layouts  3.22 us (3%)
    all_gather x1, blocking collectives, local(): qg = lax.all_gather(qg, 'dp', axis=0, axis_index_groups=NEAR)  22.1 us
    all_to_all x2, starting transfers between devices, exchange(): lax.all_to_all(block, axis, 0, 0, tiled=True, axis_index_groups=groups)  20.3 us
    ppermute x3, starting transfers between devices, carry_on(): return lax.ppermute(block, 'dp', pairs)  15.6 us
    ppermute x3, waiting for transfers between devices, hand_out(): return lax.ppermute(block, 'dp', pairs)  12.7 us
    all_to_all x1, blocking collectives, exchange(): lax.all_to_all(block, axis, 0, 0, tiled=True, axis_index_groups=groups)  9.84 us
    ppermute x3, starting transfers between devices, swap(): lax.ppermute(block, 'dp', [(place, place ^ turn) for place in range(DP)])  9.27 us
    ppermute x3, waiting for transfers between devices, swap(): lax.ppermute(block, 'dp', [(place, place ^ turn) for place in range(DP)])  6.23 us
    pallas_call x1, Pallas kernels, local(): call(backward_kernel, out_shape=(*[jax.ShapeDtypeStruct((rows, wide), BF1...  5.56 us
  transfers between devices with their start and end apart: 11, of which 5 were waited for; matrix products, arithmetic and copies ran while one was open for 1% of the time, Pallas kernels for 0%

profile of v8, /device:TPU:1, one launch (start us, length us, event | category | flops | bytes accessed | tf_op | source)
XLA Modules:
  0.0 118.6 jit_solution(8544429876433410615)
XLA Ops:
  0.6 1.8 %pack.1.packed = bf16[168,256]{1,0:T(8,128)(2,1)} custom-call(s32[5,128]{1,0:T(8,128)} %bitcast.18, bf16[80,1024]{1,0:T(8,128)(2,1)} %keys_in.1, bf16[80,1024]{1,0:T(8,128)(2,1)} %values_in.1), custom_call_target="tpu_custom_call" | custom-call | tf_op jit(solution)/shard_map/pack/pallas_call | solution.py:352
  2.4 1.3 %collective-permute-start.2 = (bf16[168,256]{1,0:T(8,128)(2,1)}, bf16[168,256]{1,0:T(8,128)(2,1)S(1)}, u32[]{:S(2)}, u32[]{:S(2)}) collective-permute-start(bf16[168,256]{1,0:T(8,128)(2,1)} %pack.1.packed), channel_id=1, source_target_pairs={{192,320},{224,352},{256,128},{288,160},{320,192},{352,224},{384,0... | collective-permute-start | bytes 258056 | tf_op jit(solution)/shard_map/ppermute | solution.py:326
  3.7 1.3 %collective-permute-start.1 = (bf16[168,256]{1,0:T(8,128)(2,1)}, bf16[168,256]{1,0:T(8,128)(2,1)S(1)}, u32[]{:S(2)}, u32[]{:S(2)}) collective-permute-start(bf16[168,256]{1,0:T(8,128)(2,1)} %pack.1.packed), channel_id=1, source_target_pairs={{224,480},{256,0},{288,32},{320,64},{352,96},{384,128},{416,160},{... | collective-permute-start | bytes 258056 | tf_op jit(solution)/shard_map/ppermute | solution.py:326
  5.0 1.3 %collective-permute-start = (bf16[168,256]{1,0:T(8,128)(2,1)}, bf16[168,256]{1,0:T(8,128)(2,1)S(1)}, u32[]{:S(2)}, u32[]{:S(2)}) collective-permute-start(bf16[168,256]{1,0:T(8,128)(2,1)} %pack.1.packed), channel_id=1, source_target_pairs={{128,0},{160,32},{192,64},{224,96},{256,384},{288,416},{320,448},{... | collective-permute-start | bytes 258056 | tf_op jit(solution)/shard_map/ppermute | solution.py:326
  6.3 0.9 copy-done
  7.2 0.8 copy-done.1
  8.1 0.8 copy-done.2
  8.9 8.3 %collective-permute-done.2.p3 = bf16[168,256]{1,0:T(8,128)(2,1)S(1)} collective-permute-done((bf16[168,256]{1,0:T(8,128)(2,1)}, bf16[168,256]{1,0:T(8,128)(2,1)S(1)}, u32[]{:S(2)}, u32[]{:S(2)}) %collective-permute-start.2) | collective-permute-done | bytes 86048 | tf_op jit(solution)/shard_map/ppermute | solution.py:326
  17.3 4.4 %collective-permute-done.1.p2 = bf16[168,256]{1,0:T(8,128)(2,1)S(1)} collective-permute-done((bf16[168,256]{1,0:T(8,128)(2,1)}, bf16[168,256]{1,0:T(8,128)(2,1)S(1)}, u32[]{:S(2)}, u32[]{:S(2)}) %collective-permute-start.1) | collective-permute-done | bytes 86048 | tf_op jit(solution)/shard_map/ppermute | solution.py:326
  21.6 1.2 fan.1
  22.8 11.8 %all-to-all-start = ((bf16[32,60,256]{2,1,0:T(8,128)(2,1)}), bf16[32,60,256]{2,1,0:T(8,128)(2,1)S(1)}, u32[]{:S(2)}, u32[]{:S(2)}) async-start(bf16[32,60,256]{2,1,0:T(8,128)(2,1)} %bitcast.4), calls=%async_computation | async-start | bytes 2097152 | tf_op jit(solution)/shard_map/all_to_all | solution.py:307
  34.6 22.1 %all-gather = bf16[1056,256]{1,0:T(8,128)(2,1)S(1)} all-gather(bf16[264,256]{1,0:T(8,128)(2,1)S(1)} %get-tuple-element.31), channel_id=2, replica_groups={{0,32,64,96},{128,160,192,224},{256,288,320,352},{384,416,448,480},{1,3..., dimensions={0}, use_global_device_ids=true | all-gather | bytes 675840 | tf_op jit(solution)/shard_map/all_gather | solution.py:395
  56.7 3.7 %forward.1 = (bf16[3,640,1024]{2,1,0:T(8,128)(2,1)S(1)}, f32[4,128,256]{2,1,0:T(8,128)S(1)}, f32[4,16,256]{2,1,0:T(8,128)S(1)}, s32[2]{0:T(128)S(1)}, bf16[3,640,256]{2,1,0:T(8,128)(2,1)S(1)}) custom-call(bf16[4,264,256]{2,1,0:T(8,128)(2,1)S(1)} %bitcast.10, bf16[8,4,60,256]{3,2,1,0:T(8,128)(2,1)S(1)} %bitcast.13), custom_call_target="tpu_custom_call" | custom-call | tf_op jit(solution)/shard_map/forward/pallas_call | solution.py:397
  60.4 9.8 %all_to_all.16.stats = f32[4,16,256]{2,1,0:T(8,128)S(1)} all-to-all(f32[4,16,256]{2,1,0:T(8,128)S(1)} %get-tuple-element.37), channel_id=1, replica_groups={{0,32,64,96},{128,160,192,224},{256,288,320,352},{384,416,448,480},{1,3..., dimensions={0} | all-to-all | bytes 131072 | tf_op jit(solution)/shard_map/all_to_all | solution.py:307
  70.2 5.6 %backward.1 = (bf16[256,256]{1,0:T(8,128)(2,1)S(1)}, bf16[256,256]{1,0:T(8,128)(2,1)S(1)}, bf16[256,256]{1,0:T(8,128)(2,1)S(1)}, bf16[256,256]{1,0:T(8,128)(2,1)S(1)}, bf16[8,4,60,256]{3,2,1,0:T(8,128)(2,1)}) custom-call(s32[2]{0:T(128)S(1)} %get-tuple-element.33.active, bf16[4,264,256]{2,1,0:T(8,128)(2,1)S(1)} %bitcast.11, ...), custom_call_target="tpu_custom_call" | custom-call | tf_op jit(solution)/shard_map/backward/pallas_call | solution.py:419
  75.8 8.6 %all-to-all-start.2 = ((bf16[32,60,256]{2,1,0:T(8,128)(2,1)}), bf16[32,60,256]{2,1,0:T(8,128)(2,1)S(1)}, u32[]{:S(2)}, u32[]{:S(2)}) async-start(bf16[32,60,256]{2,1,0:T(8,128)(2,1)} %bitcast.6), calls=%async_computation.2 | async-start | bytes 2097152 | tf_op jit(solution)/shard_map/all_to_all | solution.py:307
  84.3 2.4 %collective-permute-start.3 = (bf16[256,256]{1,0:T(8,128)(2,1)S(1)}, bf16[256,256]{1,0:T(8,128)(2,1)S(1)}, u32[]{:S(2)}, u32[]{:S(2)}) collective-permute-start(bf16[256,256]{1,0:T(8,128)(2,1)S(1)} %get-tuple-element.39), channel_id=1, source_target_pairs={{0,96},{32,64},{64,32},{96,0},{128,224},{160,192},{192,160},{224,1... | collective-permute-start | bytes 393224 | tf_op jit(solution)/shard_map/ppermute | solution.py:311
  86.7 3.3 %collective-permute-start.4 = (bf16[256,256]{1,0:T(8,128)(2,1)S(1)}, bf16[256,256]{1,0:T(8,128)(2,1)S(1)}, u32[]{:S(2)}, u32[]{:S(2)}) collective-permute-start(bf16[256,256]{1,0:T(8,128)(2,1)S(1)} %get-tuple-element.40), channel_id=1, source_target_pairs={{0,64},{32,96},{64,0},{96,32},{128,192},{160,224},{192,128},{224,1... | collective-permute-start | bytes 393224 | tf_op jit(solution)/shard_map/ppermute | solution.py:311
  90.0 3.6 %collective-permute-start.5 = (bf16[256,256]{1,0:T(8,128)(2,1)S(1)}, bf16[256,256]{1,0:T(8,128)(2,1)S(1)}, u32[]{:S(2)}, u32[]{:S(2)}) collective-permute-start(bf16[256,256]{1,0:T(8,128)(2,1)S(1)} %get-tuple-element.41), channel_id=1, source_target_pairs={{0,32},{32,0},{64,96},{96,64},{128,160},{160,128},{192,224},{224,1... | collective-permute-start | bytes 393224 | tf_op jit(solution)/shard_map/ppermute | solution.py:311
  93.6 6.2 %collective-permute-done.4 = bf16[256,256]{1,0:T(8,128)(2,1)S(1)} collective-permute-done((bf16[256,256]{1,0:T(8,128)(2,1)S(1)}, bf16[256,256]{1,0:T(8,128)(2,1)S(1)}, u32[]{:S(2)}, u32[]{:S(2)}) %collective-permute-start.4) | collective-permute-done | bytes 131104 | tf_op jit(solution)/shard_map/ppermute | solution.py:311
  99.9 0.8 all-to-all-done.2
  100.9 3.3 %collective-permute-start.6 = (bf16[160,256]{1,0:T(8,128)(2,1)S(1)}, bf16[160,256]{1,0:T(8,128)(2,1)S(1)}, u32[]{:S(2)}, u32[]{:S(2)}) collective-permute-start(bf16[160,256]{1,0:T(8,128)(2,1)S(1)} %get-tuple-element.48), channel_id=1, source_target_pairs={{0,256},{32,288},{64,320},{96,352},{128,384},{160,416},{192,448},{... | collective-permute-start | bytes 245768 | tf_op jit(solution)/shard_map/ppermute | solution.py:336
  104.2 5.2 %collective-permute-start.7 = (bf16[160,256]{1,0:T(8,128)(2,1)S(1)}, bf16[160,256]{1,0:T(8,128)(2,1)S(1)}, u32[]{:S(2)}, u32[]{:S(2)}) collective-permute-start(bf16[160,256]{1,0:T(8,128)(2,1)S(1)} %get-tuple-element.49), channel_id=1, source_target_pairs={{0,384},{32,416},{128,256},{160,288},{192,320},{224,352},{320,192}... | collective-permute-start | bytes 245768 | tf_op jit(solution)/shard_map/ppermute | solution.py:336
  109.4 7.0 %collective-permute-start.8 = (bf16[160,256]{1,0:T(8,128)(2,1)S(1)}, bf16[160,256]{1,0:T(8,128)(2,1)S(1)}, u32[]{:S(2)}, u32[]{:S(2)}) collective-permute-start(bf16[160,256]{1,0:T(8,128)(2,1)S(1)} %get-tuple-element.50), channel_id=1, source_target_pairs={{0,128},{32,160},{64,192},{96,224},{256,384},{288,416},{320,448},{... | collective-permute-start | bytes 245768 | tf_op jit(solution)/shard_map/ppermute | solution.py:336
  (15 shorter events, 2.4 us)
Async XLA Ops:
  2.4 14.8 %collective-permute-start.2 = (bf16[168,256]{1,0:T(8,128)(2,1)}, bf16[168,256]{1,0:T(8,128)(2,1)S(1)}, u32[]{:S(2)}, u32[]{:S(2)}) collective-permute-start(bf16[168,256]{1,0:T(8,128)(2,1)} %pack.1.packed), channel_id=1, source_target_pairs={{192,320},{224,352},{256,128},{288,160},{320,192},{352,224},{384,0... | collective-permute-start | bytes 258056 | tf_op jit(solution)/shard_map/ppermute | solution.py:326
  3.7 17.9 %collective-permute-start.1 = (bf16[168,256]{1,0:T(8,128)(2,1)}, bf16[168,256]{1,0:T(8,128)(2,1)S(1)}, u32[]{:S(2)}, u32[]{:S(2)}) collective-permute-start(bf16[168,256]{1,0:T(8,128)(2,1)} %pack.1.packed), channel_id=1, source_target_pairs={{224,480},{256,0},{288,32},{320,64},{352,96},{384,128},{416,160},{... | collective-permute-start | bytes 258056 | tf_op jit(solution)/shard_map/ppermute | solution.py:326
  5.0 16.6 %collective-permute-start = (bf16[168,256]{1,0:T(8,128)(2,1)}, bf16[168,256]{1,0:T(8,128)(2,1)S(1)}, u32[]{:S(2)}, u32[]{:S(2)}) collective-permute-start(bf16[168,256]{1,0:T(8,128)(2,1)} %pack.1.packed), channel_id=1, source_target_pairs={{128,0},{160,32},{192,64},{224,96},{256,384},{288,416},{320,448},{... | collective-permute-start | bytes 258056 | tf_op jit(solution)/shard_map/ppermute | solution.py:326
  6.3 0.9 copy-start
  7.2 0.8 copy-start.1
  8.1 0.8 copy-start.2
  22.8 33.8 %all-to-all-start = ((bf16[32,60,256]{2,1,0:T(8,128)(2,1)}), bf16[32,60,256]{2,1,0:T(8,128)(2,1)S(1)}, u32[]{:S(2)}, u32[]{:S(2)}) async-start(bf16[32,60,256]{2,1,0:T(8,128)(2,1)} %bitcast.4), calls=%async_computation | async-start | bytes 2097152 | tf_op jit(solution)/shard_map/all_to_all | solution.py:307
  75.8 24.9 %all-to-all-start.2 = ((bf16[32,60,256]{2,1,0:T(8,128)(2,1)}), bf16[32,60,256]{2,1,0:T(8,128)(2,1)S(1)}, u32[]{:S(2)}, u32[]{:S(2)}) async-start(bf16[32,60,256]{2,1,0:T(8,128)(2,1)} %bitcast.6), calls=%async_computation.2 | async-start | bytes 2097152 | tf_op jit(solution)/shard_map/all_to_all | solution.py:307
  84.3 9.3 %collective-permute-start.3 = (bf16[256,256]{1,0:T(8,128)(2,1)S(1)}, bf16[256,256]{1,0:T(8,128)(2,1)S(1)}, u32[]{:S(2)}, u32[]{:S(2)}) collective-permute-start(bf16[256,256]{1,0:T(8,128)(2,1)S(1)} %get-tuple-element.39), channel_id=1, source_target_pairs={{0,96},{32,64},{64,32},{96,0},{128,224},{160,192},{192,160},{224,1... | collective-permute-start | bytes 393224 | tf_op jit(solution)/shard_map/ppermute | solution.py:311
  86.7 13.2 %collective-permute-start.4 = (bf16[256,256]{1,0:T(8,128)(2,1)S(1)}, bf16[256,256]{1,0:T(8,128)(2,1)S(1)}, u32[]{:S(2)}, u32[]{:S(2)}) collective-permute-start(bf16[256,256]{1,0:T(8,128)(2,1)S(1)} %get-tuple-element.40), channel_id=1, source_target_pairs={{0,64},{32,96},{64,0},{96,32},{128,192},{160,224},{192,128},{224,1... | collective-permute-start | bytes 393224 | tf_op jit(solution)/shard_map/ppermute | solution.py:311
  90.0 9.9 %collective-permute-start.5 = (bf16[256,256]{1,0:T(8,128)(2,1)S(1)}, bf16[256,256]{1,0:T(8,128)(2,1)S(1)}, u32[]{:S(2)}, u32[]{:S(2)}) collective-permute-start(bf16[256,256]{1,0:T(8,128)(2,1)S(1)} %get-tuple-element.41), channel_id=1, source_target_pairs={{0,32},{32,0},{64,96},{96,64},{128,160},{160,128},{192,224},{224,1... | collective-permute-start | bytes 393224 | tf_op jit(solution)/shard_map/ppermute | solution.py:311
  100.9 16.3 %collective-permute-start.6 = (bf16[160,256]{1,0:T(8,128)(2,1)S(1)}, bf16[160,256]{1,0:T(8,128)(2,1)S(1)}, u32[]{:S(2)}, u32[]{:S(2)}) collective-permute-start(bf16[160,256]{1,0:T(8,128)(2,1)S(1)} %get-tuple-element.48), channel_id=1, source_target_pairs={{0,256},{32,288},{64,320},{96,352},{128,384},{160,416},{192,448},{... | collective-permute-start | bytes 245768 | tf_op jit(solution)/shard_map/ppermute | solution.py:336
  104.2 13.0 %collective-permute-start.7 = (bf16[160,256]{1,0:T(8,128)(2,1)S(1)}, bf16[160,256]{1,0:T(8,128)(2,1)S(1)}, u32[]{:S(2)}, u32[]{:S(2)}) collective-permute-start(bf16[160,256]{1,0:T(8,128)(2,1)S(1)} %get-tuple-element.49), channel_id=1, source_target_pairs={{0,384},{32,416},{128,256},{160,288},{192,320},{224,352},{320,192}... | collective-permute-start | bytes 245768 | tf_op jit(solution)/shard_map/ppermute | solution.py:336
  109.4 8.5 %collective-permute-start.8 = (bf16[160,256]{1,0:T(8,128)(2,1)S(1)}, bf16[160,256]{1,0:T(8,128)(2,1)S(1)}, u32[]{:S(2)}, u32[]{:S(2)}) collective-permute-start(bf16[160,256]{1,0:T(8,128)(2,1)S(1)} %get-tuple-element.50), channel_id=1, source_target_pairs={{0,128},{32,160},{64,192},{96,224},{256,384},{288,416},{320,448},{... | collective-permute-start | bytes 245768 | tf_op jit(solution)/shard_map/ppermute | solution.py:336
